TPU v7x, 32 devices: a whole 2x2x4 slice. The times are simulated.
32 devices in a mesh: seq: 8 (over z, x), chan: 4 (over y, core).
Axes of the slice: x: 2, y: 2, z: 4, core: 2. Of those that a mesh axis runs over, the one named last changes fastest.
Arguments:
- query_in: bfloat16 [131072, 1024], P('seq', 'chan'), may hold values from -6 to 6
- key_in: bfloat16 [131072, 1024], P('seq', 'chan'), may hold values from -6 to 6
- value_in: bfloat16 [131072, 1024], P('seq', 'chan'), may hold values from -6 to 6
- freq_kernel: bfloat16 [512, 256, 1024], P(('seq', 'chan')), may hold values from -6 to 6
- factor_b1: bfloat16 [256, 512, 512], P('seq', 'chan'), may hold values from -0.25 to 0.25
- factor_b2: bfloat16 [512, 256, 256], P(('seq', 'chan')), may hold values from -0.375 to 0.375
- factor_c2: bfloat16 [512, 256, 256], P(('seq', 'chan')), may hold values from -0.375 to 0.375
- factor_c1: bfloat16 [256, 512, 512], P('seq', 'chan'), may hold values from -0.25 to 0.25
- cotangent: bfloat16 [131072, 1024], P('seq', 'chan'), may hold values from -0.75 to 0.75
Outputs:
- grad_query: bfloat16 [131072, 1024], P('seq', 'chan')
- grad_key: bfloat16 [131072, 1024], P('seq', 'chan')
- grad_value: bfloat16 [131072, 1024], P('seq', 'chan')
- grad_freq: bfloat16 [512, 256, 1024], P(('seq', 'chan'))
- grad_b1: bfloat16 [256, 512, 512], P('seq', 'chan')
- grad_b2: bfloat16 [512, 256, 256], P(('seq', 'chan'))
- grad_c2: bfloat16 [512, 256, 256], P(('seq', 'chan'))
- grad_c1: bfloat16 [256, 512, 512], P('seq', 'chan')
All inputs are finite; a program needn't handle non-finite values.
Results may differ from a plain program's by a relative error of at most 0.022.
Values may be sent and summed in bfloat16 or wider, within the bound.
No kernel may reach another device: no remote copies, remote signals or barrier semaphores. Data moves between devices by JAX's collectives and lax.ppermute only.
A program may use at most 320 MiB of HBM per device.

v0:
```python
import jax
import jax.numpy as jnp
from jax import lax
from jax.sharding import PartitionSpec as P

BS = 512


def apply_in(weights, tensor, seq_count):
    freq_rows, out_width, in_width = weights.shape
    shaped = weights.reshape(freq_rows, out_width, seq_count, in_width // seq_count)
    result = jnp.einsum("ipsa,iscah->ipch", shaped, tensor, preferred_element_type=jnp.float32)
    return result.reshape(freq_rows, out_width, -1)


def apply_out(weights, tensor, seq_count, chan_count):
    freq_rows, out_width, in_width = weights.shape
    shaped = weights.reshape(freq_rows, seq_count, out_width // seq_count, in_width)
    spread = tensor.reshape(freq_rows, in_width, chan_count, -1)
    return jnp.einsum("isap,ipch->iscah", shaped, spread, preferred_element_type=jnp.float32)


def outer_in(left, right, chan_count):
    freq_rows, out_width, full_width = left.shape
    spread = left.reshape(freq_rows, out_width, chan_count, -1)
    result = jnp.einsum("ipch,iscah->ipsa", spread, right, preferred_element_type=jnp.float32)
    return result.reshape(freq_rows, out_width, -1)


def forward_freq(arrived, factor_b2, freq_kernel, factor_c2, seq_count, chan_count):
    spectrum = apply_in(factor_b2, arrived, seq_count).astype(jnp.bfloat16)
    filtered = (freq_kernel.astype(jnp.float32) * spectrum.astype(jnp.float32)).astype(jnp.bfloat16)
    section_three = apply_out(factor_c2, filtered, seq_count, chan_count).astype(jnp.bfloat16)
    return (spectrum, filtered, section_three)


def backward_freq(
    grad_three,
    section_one,
    spectrum,
    filtered,
    factor_b2,
    freq_kernel,
    factor_c2,
    seq_count,
    chan_count,
):
    grad_c2 = jnp.swapaxes(outer_in(filtered, grad_three, chan_count), 1, 2).astype(jnp.bfloat16)
    grad_filtered = apply_in(jnp.swapaxes(factor_c2, 1, 2), grad_three, seq_count)
    grad_freq = (grad_filtered * spectrum.astype(jnp.float32)).astype(jnp.bfloat16)
    grad_spectrum = (grad_filtered * freq_kernel.astype(jnp.float32)).astype(jnp.bfloat16)
    grad_b2 = outer_in(grad_spectrum, section_one, chan_count).astype(jnp.bfloat16)
    grad_one = apply_out(
        jnp.swapaxes(factor_b2, 1, 2), grad_spectrum, seq_count, chan_count
    ).astype(jnp.bfloat16)
    return (grad_freq, grad_b2, grad_c2, grad_one)


def chan_into(tensor, seq_count, chan_count):
    arrived = lax.all_to_all(tensor, ("seq", "chan"), split_axis=0, concat_axis=1, tiled=True)
    moved = arrived.reshape(arrived.shape[0], seq_count, chan_count, -1, arrived.shape[2])
    return moved


def chan_outof(tensor):
    flattened = tensor.reshape(tensor.shape[0], -1, tensor.shape[4])
    moved = lax.all_to_all(flattened, ("seq", "chan"), split_axis=1, concat_axis=0, tiled=True)
    return moved


def shards(
    query_in, key_in, value_in, freq_kernel, factor_b1, factor_b2, factor_c2, factor_c1, cotangent
):
    seq_count = lax.axis_size("seq")
    chan_count = lax.axis_size("chan")
    tok_rows, chan_width = query_in.shape
    local_blocks = tok_rows // BS
    key_value = (key_in.astype(jnp.float32) * value_in.astype(jnp.float32)).astype(jnp.bfloat16)
    grad_mixed = (cotangent.astype(jnp.float32) * query_in.astype(jnp.float32)).astype(jnp.bfloat16)
    kv_local = key_value.reshape(local_blocks, BS, chan_width)
    mixed_grad_blk = grad_mixed.reshape(local_blocks, BS, chan_width)
    section_one = jnp.einsum(
        "aij,ajc->iac",
        lax.all_gather(factor_b1, "chan", axis=1, tiled=True),
        kv_local,
        preferred_element_type=jnp.float32,
    ).astype(jnp.bfloat16)
    arrived = chan_into(section_one, seq_count, chan_count)
    spectrum, filtered, section_three = forward_freq(
        arrived, factor_b2, freq_kernel, factor_c2, seq_count, chan_count
    )
    three_local = chan_outof(section_three)
    mixed_blocks = jnp.einsum(
        "aki,iac->akc",
        lax.all_gather(factor_c1, "chan", axis=1, tiled=True),
        three_local,
        preferred_element_type=jnp.float32,
    )
    mixed_out = mixed_blocks.reshape(tok_rows, chan_width)
    grad_query = (cotangent.astype(jnp.float32) * mixed_out).astype(jnp.bfloat16)
    picked_grad = mixed_grad_blk
    c1_sums = lax.psum_scatter(
        jnp.einsum(
            "akc,iac->kai", picked_grad, three_local, preferred_element_type=jnp.float32
        ).astype(jnp.bfloat16),
        "chan",
        scatter_dimension=0,
        tiled=True,
    ).astype(jnp.float32)
    grad_c1 = jnp.transpose(c1_sums, (1, 0, 2)).astype(jnp.bfloat16)
    picked = mixed_grad_blk
    grad_three = jnp.einsum(
        "aki,akc->iac",
        lax.all_gather(factor_c1, "chan", axis=1, tiled=True),
        picked,
        preferred_element_type=jnp.float32,
    ).astype(jnp.bfloat16)
    grad_freq, grad_b2, grad_c2, grad_one = backward_freq(
        chan_into(grad_three, seq_count, chan_count),
        arrived,
        spectrum,
        filtered,
        factor_b2,
        freq_kernel,
        factor_c2,
        seq_count,
        chan_count,
    )
    one_local = chan_outof(grad_one)
    picked_grad = one_local
    b1_sums = lax.psum_scatter(
        jnp.einsum(
            "iac,ajc->iaj", picked_grad, kv_local, preferred_element_type=jnp.float32
        ).astype(jnp.bfloat16),
        "chan",
        scatter_dimension=0,
        tiled=True,
    ).astype(jnp.float32)
    grad_b1 = jnp.transpose(b1_sums, (1, 0, 2)).astype(jnp.bfloat16)
    picked = one_local
    grad_kv_blk = jnp.einsum(
        "aij,iac->ajc",
        lax.all_gather(factor_b1, "chan", axis=1, tiled=True),
        picked,
        preferred_element_type=jnp.float32,
    )
    grad_kv = grad_kv_blk.reshape(tok_rows, chan_width)
    grad_key = (grad_kv * value_in.astype(jnp.float32)).astype(jnp.bfloat16)
    grad_value = (grad_kv * key_in.astype(jnp.float32)).astype(jnp.bfloat16)
    return (grad_query, grad_key, grad_value, grad_freq, grad_b1, grad_b2, grad_c2, grad_c1)


def solution(mesh):
    return jax.shard_map(
        shards,
        mesh=mesh,
        in_specs=(
            P("seq", "chan"),
            P("seq", "chan"),
            P("seq", "chan"),
            P(("seq", "chan"), None, None),
            P("seq", "chan", None),
            P(("seq", "chan"), None, None),
            P(("seq", "chan"), None, None),
            P("seq", "chan", None),
            P("seq", "chan"),
        ),
        out_specs=(
            P("seq", "chan"),
            P("seq", "chan"),
            P("seq", "chan"),
            P(("seq", "chan"), None, None),
            P("seq", "chan", None),
            P(("seq", "chan"), None, None),
            P(("seq", "chan"), None, None),
            P("seq", "chan", None),
        ),
        check_vma=False,
    )
```

profile of v0, /device:TPU:0, one launch (start us, length us, event | category | flops | bytes accessed | tf_op | source)
XLA Modules:
  0.0 1361.8 jit_solution(4756301610428389728)
XLA Ops:
  8.7 9.6 fusion.5
  18.3 100.0 %all-gather.3.cloned.1.call-done = bf16[32,512,512]{2,1,0:T(8,128)(2,1)} async-done(((bf16[32,128,512]{2,1,0:T(8,128)(2,1)}), bf16[32,512,512]{2,1,0:T(8,128)(2,1)}) %all-gather.3.cloned.1.call-update) | async-done | bytes 16777232 | tf_op jit(solution)/shard_map/all_gather | solution.py:84
  118.2 14.9 %convert_bitcast_fusion.3 = bf16[512,32,256]{0,2,1:T(8,128)(2,1)} fusion(bf16[32,512,256]{2,1,0:T(8,128)(2,1)} %bitcast.129, bf16[32,512,512]{2,1,0:T(8,128)(2,1)} %all-gather.3.cloned.1.call-done), kind=kOutput, calls=%fused_computation.34 | convolution fusion | flops 4299161600 | bytes 33554432 | tf_op jit(solution)/shard_map/aij,ajc->iac/dot_general | solution.py:82
  133.1 14.9 %copy.68 = bf16[512,32,256]{2,1,0:T(8,128)(2,1)} copy(bf16[512,32,256]{0,2,1:T(8,128)(2,1)} %convert_bitcast_fusion.3) | data formatting | bytes 16777216 | tf_op jit(solution)/shard_map/convert_element_type | solution.py:87
  148.0 4.8 all-to-all-start
  152.8 9.7 fusion.1
  162.5 143.4 %all-gather.5.cloned.1.call-done = bf16[32,512,512]{2,1,0:T(8,128)(2,1)} async-done(((bf16[32,128,512]{2,1,0:T(8,128)(2,1)}), bf16[32,512,512]{2,1,0:T(8,128)(2,1)}) %all-gather.5.cloned.1.call-update) | async-done | bytes 16777232 | tf_op jit(solution)/shard_map/all_gather | solution.py:95
  305.9 14.3 %convert_bitcast_fusion.1 = bf16[512,32,256]{0,2,1:T(8,128)(2,1)} fusion(bf16[32,512,256]{2,1,0:T(8,128)(2,1)} %bitcast.123, bf16[32,512,512]{2,1,0:T(8,128)(2,1)} %all-gather.5.cloned.1.call-done), kind=kOutput, calls=%fused_computation.32 | convolution fusion | flops 4299161600 | bytes 33554432 | tf_op jit(solution)/shard_map/aki,akc->iac/dot_general | solution.py:112
  320.2 14.5 %copy.81 = bf16[512,32,256]{2,1,0:T(8,128)(2,1)} copy(bf16[512,32,256]{0,2,1:T(8,128)(2,1)} %convert_bitcast_fusion.1) | data formatting | bytes 16777216 | tf_op jit(solution)/shard_map/convert_element_type | solution.py:117
  334.7 3.5 all-to-all-done
  338.2 9.2 all-to-all-start.2
  347.7 3.9 copy.70
  351.6 12.3 fusion.26
  363.9 17.6 %copy.72 = f32[16,256,1024]{2,1,0:T(8,128)} copy(f32[16,256,1024]{1,2,0:T(8,128)} %bitcast.141) | data formatting | bytes 33554432 | tf_op jit(solution)/shard_map/convert_element_type | solution.py:32
  381.5 151.1 %all-to-all-done.2 = bf16[512,32,256]{2,1,0:T(8,128)(2,1)} async-done(((bf16[512,32,256]{2,1,0:T(8,128)(2,1)}), bf16[512,32,256]{2,1,0:T(8,128)(2,1)}, u32[]{:S(2)}, u32[]{:S(2)}) %all-to-all-start.2) | async-done | bytes 8388640 | tf_op jit(solution)/shard_map/all_to_all | solution.py:60
  532.6 11.7 fusion.13
  544.3 17.6 %copy.84 = f32[16,256,1024]{2,1,0:T(8,128)} copy(f32[16,256,1024]{1,2,0:T(8,128)} %bitcast.142) | data formatting | bytes 33554432 | tf_op jit(solution)/shard_map/reshape | solution.py:13
  561.9 23.1 %multiply_convert_fusion = (bf16[16,256,1024]{2,1,0:T(8,128)(2,1)}, bf16[16,256,1024]{2,1,0:T(8,128)(2,1)}, bf16[16,256,1024]{2,1,0:T(8,128)(2,1)}) fusion(f32[16,256,1024]{2,1,0:T(8,128)} %copy.84, f32[16,256,1024]{2,1,0:T(8,128)} %copy.72, bf16[16,256,1024]{2,1,0:T(8,128)(2,1)} %param.12), kind=kLoop, calls=%fused_computation.15 | loop fusion | flops 29360128 | bytes 67108864 | tf_op jit(solution)/shard_map/convert_element_type | solution.py:50
  585.0 14.6 %reshape.76 = bf16[16,256,4,256]{3,2,1,0:T(4,128)(2,1)} reshape(bf16[16,256,1024]{2,1,0:T(8,128)(2,1)} %get-tuple-element.33) | data formatting | bytes 16777216 | tf_op jit(solution)/shard_map/reshape | solution.py:19
  599.6 7.4 convert_bitcast_fusion.2
  607.0 8.1 copy.74
  615.2 11.5 copy.75
  626.7 191.1 %all_to_all.66 = bf16[16,1024,256]{2,0,1:T(8,128)(2,1)} all-to-all(bf16[16,1024,256]{2,0,1:T(8,128)(2,1)} %copy.75), channel_id=1, replica_groups=mesh['seq'=8,'chan'=4] {'seq','chan'}, dimensions={1} | all-to-all | bytes 16777216 | tf_op jit(solution)/shard_map/all_to_all | solution.py:67
  817.8 10.5 copy.77
  828.4 15.4 %convolution_convert_fusion = bf16[32,512,512]{2,1,0:T(8,128)(2,1)} fusion(bf16[32,512,256]{2,1,0:T(8,128)(2,1)} %bitcast.124, bf16[512,32,256]{2,1,0:T(8,128)(2,1)} %bitcast.125), kind=kOutput, calls=%fused_computation.16 | convolution fusion | flops 4303355904 | bytes 33554432 | tf_op jit(solution)/shard_map/akc,iac->kai/dot_general | solution.py:103
  843.7 21.2 %copy.134 = bf16[512,16384]{1,0:T(8,128)(2,1)} copy(bf16[512,16384]{0,1:T(8,128)(2,1)} %bitcast.131) | data formatting | bytes 33554432
  865.0 15.5 %reshape.84 = bf16[16,256,4,256]{3,2,1,0:T(4,128)(2,1)} reshape(bf16[16,256,1024]{2,1,0:T(8,128)(2,1)} %get-tuple-element.34) | data formatting | bytes 16777216 | tf_op jit(solution)/shard_map/reshape | solution.py:19
  880.5 8.7 convert_bitcast_fusion
  889.2 8.4 copy.87
  897.6 11.6 copy.88
  909.2 189.1 %all_to_all.67 = bf16[16,1024,256]{2,0,1:T(8,128)(2,1)} all-to-all(bf16[16,1024,256]{2,0,1:T(8,128)(2,1)} %copy.88), channel_id=1, replica_groups=mesh['seq'=8,'chan'=4] {'seq','chan'}, dimensions={1} | all-to-all | bytes 16777216 | tf_op jit(solution)/shard_map/all_to_all | solution.py:67
  1098.3 10.6 copy.90
  1108.9 16.1 %convolution_convert_fusion.1 = bf16[32,512,512]{2,1,0:T(8,128)(2,1)} fusion(bf16[32,512,256]{2,1,0:T(8,128)(2,1)} %bitcast.130, bf16[512,32,256]{2,1,0:T(8,128)(2,1)} %bitcast.127), kind=kOutput, calls=%fused_computation.17 | convolution fusion | flops 4303355904 | bytes 33554432 | tf_op jit(solution)/shard_map/iac,ajc->iaj/dot_general | solution.py:132
  1125.0 21.7 %copy.132 = bf16[512,16384]{1,0:T(8,128)(2,1)} copy(bf16[512,16384]{0,1:T(8,128)(2,1)} %bitcast.132) | data formatting | bytes 33554432
  1146.7 8.8 copy.82
  1155.6 11.7 copy.69
  1167.2 9.5 bitcast_convert_fusion.2
  1176.7 2.4 copy.100
  1179.1 9.6 bitcast_convert_fusion.1
  1188.7 54.5 %convolution_bitcast_fusion.1 = f32[32,512,256]{1,2,0:T(8,128)} fusion(bf16[32,512,512]{2,1,0:T(8,128)(2,1)} %all-gather.5.cloned.1.call-done, bf16[512,32,256]{2,1,0:T(8,128)(2,1)} %bitcast.126), kind=kOutput, calls=%fused_computation.19 | convolution fusion | flops 4294967296 | bytes 41943040 | tf_op jit(solution)/shard_map/aki,iac->akc/dot_general | solution.py:93
  1243.3 17.7 %copy.79 = f32[32,512,256]{2,1,0:T(8,128)} copy(f32[32,512,256]{1,2,0:T(8,128)} %convolution_bitcast_fusion.1) | data formatting | bytes 33554432 | tf_op jit(solution)/shard_map/aki,iac->akc/dot_general | solution.py:93
  1260.9 22.4 %convolution_bitcast_fusion = f32[32,512,256]{1,2,0:T(8,128)} fusion(bf16[32,512,512]{2,1,0:T(8,128)(2,1)} %all-gather.3.cloned.1.call-done, bf16[512,32,256]{2,1,0:T(8,128)(2,1)} %bitcast.128), kind=kOutput, calls=%fused_computation.18 | convolution fusion | flops 4294967296 | bytes 41943040 | tf_op jit(solution)/shard_map/aij,iac->ajc/dot_general | solution.py:141
  1283.4 17.4 %copy.92 = f32[32,512,256]{2,1,0:T(8,128)} copy(f32[32,512,256]{1,2,0:T(8,128)} %convolution_bitcast_fusion) | data formatting | bytes 33554432 | tf_op jit(solution)/shard_map/aij,iac->ajc/dot_general | solution.py:141
  1300.8 28.5 %fusion.4 = (bf16[16384,256]{1,0:T(8,128)(2,1)}, bf16[16384,256]{1,0:T(8,128)(2,1)}, bf16[16384,256]{1,0:T(8,128)(2,1)}) fusion(bf16[16384,256]{1,0:T(8,128)(2,1)} %param.10, f32[32,512,256]{2,1,0:T(8,128)} %copy.92, bf16[16384,256]{1,0:T(8,128)(2,1)} %param.11, f32[32,512,256]{2,1,0:T(8,128)} %copy.79, bf16[16384,256]{1,0:T(8,128)(2,1)} %param.17), kind=kLoop, calls=%fused_computation.11 | loop fusion | flops 37748736 | bytes 83886080 | tf_op jit(solution)/shard_map/convert_element_type | solution.py:149
  1329.3 6.4 copy.135
  1335.6 6.6 copy.101
  1342.2 6.4 copy.133
  1348.6 6.4 copy.99
  (16 shorter events, 1.9 us)
Async XLA Ops:
  7.2 525.5 %copy-start = (bf16[16,256,256]{2,1,0:T(8,128)(2,1)S(1)}, bf16[16,256,256]{2,1,0:T(8,128)(2,1)}, u32[]{:S(2)}) copy-start(bf16[16,256,256]{2,1,0:T(8,128)(2,1)} %param.15) | copy-start | bytes 6291460
  7.2 111.1 %all-gather.3.cloned.1.call-start = ((), (), s32[]{:S(2)}) async-start(), calls=%async_computation.6 | async-start | bytes 20971520 | tf_op jit(solution)/shard_map/all_gather | solution.py:84
  7.9 298.0 %all-gather.5.cloned.1.call-start = ((), (), s32[]{:S(2)}) async-start(), calls=%async_computation.7 | async-start | bytes 20971520 | tf_op jit(solution)/shard_map/all_gather | solution.py:95
  148.0 190.2 %all-to-all-start = ((bf16[512,32,256]{2,1,0:T(8,128)(2,1)}), bf16[512,32,256]{2,1,0:T(8,128)(2,1)}, u32[]{:S(2)}, u32[]{:S(2)}) async-start(bf16[512,32,256]{2,1,0:T(8,128)(2,1)} %copy.68), calls=%async_computation | async-start | bytes 16777216 | tf_op jit(solution)/shard_map/all_to_all | solution.py:60
  338.2 194.4 %all-to-all-start.2 = ((bf16[512,32,256]{2,1,0:T(8,128)(2,1)}), bf16[512,32,256]{2,1,0:T(8,128)(2,1)}, u32[]{:S(2)}, u32[]{:S(2)}) async-start(bf16[512,32,256]{2,1,0:T(8,128)(2,1)} %copy.81), calls=%async_computation.2 | async-start | bytes 16777216 | tf_op jit(solution)/shard_map/all_to_all | solution.py:60
  347.4 981.9 %reduce-scatter.9.cloned.1.call-start = ((), (), s32[]{:S(2)}) async-start(), calls=%async_computation.9 | async-start | bytes 20971520
  864.9 477.3 %reduce-scatter.7.cloned.1.call-start = ((), (), s32[]{:S(2)}) async-start(), calls=%async_computation.8 | async-start | bytes 20971520
  865.0 15.5 %copy-start.2 = (bf16[16,256,256]{1,2,0:T(8,128)(2,1)S(1)}, bf16[16,256,256]{1,2,0:T(8,128)(2,1)}, u32[]{:S(2)}) copy-start(bf16[16,256,256]{1,2,0:T(8,128)(2,1)} %copy.70) | copy-start | bytes 6291460
  1335.6 19.4 %copy-start.1 = (bf16[16,256,256]{2,1,0:T(8,128)(2,1)S(1)}, bf16[16,256,256]{2,1,0:T(8,128)(2,1)}, u32[]{:S(2)}) copy-start(bf16[16,256,256]{2,1,0:T(8,128)(2,1)} %param.15) | copy-start | bytes 6291460
Sparse Core Ops, SparseCore 0:
  9.6 108.6 all-gather.2
  119.8 186.0 all-gather.4
  865.0 208.1 reduce-scatter.8
  1146.8 125.3 reduce-scatter.6
where the time goes:
time: 1370 us; the launch traced here: 1360 us
  waiting for transfers between devices  399 us (29%)
  blocking collectives  380 us (28%)
  local copies, waits for them, and re-layouts  286 us (21%)
  matrix products  197 us (14%)
  other arithmetic  70.9 us (5%)
  starting transfers between devices  14.4 us (1%)
  between operations  14.1 us (1%)
    all_to_all x2, blocking collectives, chan_outof(): lax.all_to_all(flattened, ('seq', 'chan'), split_axis=1, concat_axis=0, t...  380 us
    all_to_all x2, waiting for transfers between devices, chan_into(): lax.all_to_all(tensor, ('seq', 'chan'), split_axis=0, concat_axis=1, tile...  155 us
    all_gather x1, waiting for transfers between devices, shards(): lax.all_gather(factor_c1, 'chan', axis=1, tiled=True)  143 us
    all_gather x1, waiting for transfers between devices, shards(): lax.all_gather(factor_b1, 'chan', axis=1, tiled=True)  100 us
    unnamed x14, local copies, waits for them, and re-layouts  74.9 us
    dot_general x1, matrix products, shards(): jnp.einsum('aki,iac->akc', lax.all_gather(factor_c1, 'chan', axis=1, tile...  54.5 us
    reshape x2, local copies, waits for them, and re-layouts, apply_out(): spread = tensor.reshape(freq_rows, in_width, chan_count, -1)  30.1 us
    convert_element_type x1, other arithmetic, shards(): grad_value = (grad_kv * key_in.astype(jnp.float32)).astype(jnp.bfloat16)  28.5 us
  transfers between devices with their start and end apart: 6, of which 4 were waited for; matrix products, arithmetic and copies ran while one was open for 29% of the time, Pallas kernels for 0%

commit v1 on v0

v1 whole, which is shorter than its diff:
```python
import jax
import jax.numpy as jnp
from jax import lax
from jax.experimental import pallas as pl
from jax.experimental.pallas import tpu as pltpu
from jax.sharding import PartitionSpec as P

BS = 512
BOTH = ("seq", "chan")
BF = jnp.bfloat16
F32 = jnp.float32
VMEM_BYTES = 56 * 1024 * 1024


def dot(left, right, left_dim, right_dim):
    return lax.dot_general(
        left, right, (((left_dim,), (right_dim,)), ((), ())), preferred_element_type=F32
    )


def times(left, right):
    return (left.astype(F32) * right.astype(F32)).astype(BF)


def rows_of(order, k, rows):
    return pl.ds(pl.multiple_of(order[k] * rows, rows), rows)


def token_call(block_body, order, shards, start, shift, count, local, tokens, outs, flops):
    own, *others = shards
    rows, width = own.shape[1], tokens[0].shape[2]
    offsets = [start, shift] + [o[1] for o in outs if o != "pairs"]
    if local is not None:
        offsets.append(local[1])
    step = count if count < 4 else 4 if count % 8 == 0 else 2
    while any(x % step for x in (count, *offsets)):
        step -= 1

    def blocks(first, *rest):
        zeros = (0,) * len(rest)
        return pl.BlockSpec((step, *rest), lambda a, o: (a + first // step, *zeros))

    def exchanged(first, devices, _, part, width):
        return pl.BlockSpec(
            (devices, step, part, width), lambda a, o: (0, a + first // step, 0, 0)
        )

    args = [own, *others]
    in_specs = [blocks(start, rows, BS)] + [blocks(shift, rows, BS)] * len(others)
    if local is not None:
        args.append(local[0])
        if len(local[0].shape) == 4:
            in_specs.append(exchanged(local[1], *local[0].shape))
        else:
            in_specs.append(blocks(local[1], BS, width))
    args += tokens
    in_specs += [blocks(start, BS, width)] * len(tokens)
    out_specs, out_shape, aliases = [], [], {}
    for k, out in enumerate(outs):
        if out == "pairs":
            out_specs.append(pl.BlockSpec((2, step, rows, BS), lambda a, o: (0, a, 0, 0)))
            out_shape.append(jax.ShapeDtypeStruct((2, count, rows, BS), BF))
            continue
        shape, first, earlier = out
        out_specs.append(
            exchanged(first, *shape) if len(shape) == 4 else blocks(first, *shape[1:])
        )
        out_shape.append(jax.ShapeDtypeStruct(shape, BF))
        if earlier is not None:
            aliases[1 + len(args)] = k
            args.append(earlier)
            in_specs.append(pl.BlockSpec(memory_space=pl.ANY))

    def body(order, *refs):
        for b in range(step):
            block_body(order, b, *refs)

    return pl.pallas_call(
        body,
        grid_spec=pltpu.PrefetchScalarGridSpec(
            num_scalar_prefetch=1, grid=(count // step,), in_specs=in_specs, out_specs=out_specs
        ),
        out_shape=out_shape,
        input_output_aliases=aliases,
        compiler_params=pltpu.CompilerParams(
            dimension_semantics=("arbitrary",), vmem_limit_bytes=VMEM_BYTES
        ),
        cost_estimate=pl.CostEstimate(flops=1000, bytes_accessed=1000, transcendentals=0),
    )(order, *args)


def rows_in(ref, order, b, k=None):
    if len(ref.shape) == 3:
        return ref[b] if k is None else ref[b, rows_of(order, k, ref.shape[1] // 4), :]
    devices, _, rows, width = ref.shape
    if k is None:
        return ref[:, b].reshape(devices * rows, width)
    return ref[rows_of(order, k, devices // 4), b].reshape(devices * rows // 4, width)


def stacked(pick):
    return jnp.concatenate([pick(k) for k in range(4)], axis=0)


def one_body(order, b, w0, w1, w2, w3, key, value, *rest):
    out, rows = rest[-1], w0.shape[1]
    weight = jnp.concatenate([w[b] for w in (w0, w1, w2, w3)], axis=0)
    section = dot(weight, times(key[b], value[b]), 1, 0).astype(BF)
    for k in range(4):
        part = section[k * rows : (k + 1) * rows]
        if len(out.shape) == 3:
            out[b, rows_of(order, k, rows), :] = part
        else:
            count = out.shape[0] // 4
            out[rows_of(order, k, count), b] = part.reshape(count, *out.shape[2:])


def three_body(order, b, w0, w1, w2, w3, cot, query, *rest):
    out = rest[-1]
    weight = jnp.concatenate([w[b] for w in (w0, w1, w2, w3)], axis=0)
    grad_mixed = stacked(lambda k: times(rows_in(cot, order, b, k), rows_in(query, order, b, k)))
    section = dot(weight, grad_mixed, 0, 0).astype(BF)
    if len(out.shape) == 3:
        out[b] = section
    else:
        out[:, b] = section.reshape(out.shape[0], *out.shape[2:])


def query_body(order, b, w0, w1, w2, w3, arrived, cot, query, *rest):
    grad_query, keep, send = rest[-3:]
    rows = w0.shape[1]
    weight = jnp.concatenate([w[b] for w in (w0, w1, w2, w3)], axis=0)
    three = rows_in(arrived, order, b)
    mixed = dot(weight, three, 1, 0)
    grad_mixed = stacked(lambda k: times(rows_in(cot, order, b, k), rows_in(query, order, b, k)))
    pairs = dot(grad_mixed, three, 1, 1).astype(BF)
    for k in range(4):
        here = slice(k * rows, (k + 1) * rows)
        gate = rows_in(cot, order, b, k).astype(F32)
        grad_query[b, rows_of(order, k, rows), :] = (gate * mixed[here]).astype(BF)
        (send if k >= 2 else keep)[k % 2, b] = pairs[here]


def key_body(order, b, w0, w1, w2, w3, arrived, key, value, *rest):
    grad_key, grad_value, keep, send = rest[-4:]
    rows = w0.shape[1]
    weight = jnp.concatenate([w[b] for w in (w0, w1, w2, w3)], axis=0)
    grad_one = stacked(lambda k: rows_in(arrived, order, b, k))
    pairs = dot(grad_one, times(key[b], value[b]), 1, 1).astype(BF)
    for k in range(4):
        (send if k >= 2 else keep)[k % 2, b] = pairs[k * rows : (k + 1) * rows]
    grad_kv = dot(weight, grad_one, 0, 0)
    grad_key[b] = (grad_kv * value[b].astype(F32)).astype(BF)
    grad_value[b] = (grad_kv * key[b].astype(F32)).astype(BF)


def freq_call(row_body, inputs, outputs, flops):
    count = inputs[0].shape[0]
    step = 2 - count % 2

    def spec(x):
        rest = x.shape[1:]
        return pl.BlockSpec((step, *rest), lambda i: (i,) + (0,) * len(rest))

    def body(*refs):
        for r in range(step):
            row_body(r, *refs)

    moved = sum(2 * x.size for x in (*inputs, *outputs))
    return pl.pallas_call(
        body,
        grid=(count // step,),
        in_specs=[spec(x) for x in inputs],
        out_specs=[spec(x) for x in outputs],
        out_shape=[jax.ShapeDtypeStruct(x.shape, BF) for x in outputs],
        compiler_params=pltpu.CompilerParams(
            dimension_semantics=("arbitrary",), vmem_limit_bytes=VMEM_BYTES
        ),
        cost_estimate=pl.CostEstimate(flops=flops, bytes_accessed=moved, transcendentals=0),
    )(*inputs)


def split_rows(outs, r, m, value):
    at = 0
    for out in outs:
        size = out.shape[2]
        out[r, m] = value[at : at + size]
        at += size


def forward_freq(b2_turned, c2, kernel, ones, threes):
    def body(r, *refs):
        b2, c2, kern = refs[:3]
        one = refs[3 : 3 + len(ones)]
        spectrum, *three = refs[3 + len(ones) :]
        _, chan_count, _, width = one[0].shape
        for m in range(chan_count):
            cols = pl.ds(m * width, width)
            section = jnp.concatenate([x[r, m] for x in one], axis=0)
            spec = dot(b2[r], section, 0, 0).astype(BF)
            spectrum[r, :, cols] = spec
            split_rows(three, r, m, dot(c2[r], times(kern[r, :, cols], spec), 1, 0).astype(BF))

    return freq_call(
        body, [b2_turned, c2, kernel, *ones], [kernel, *threes], 4 * kernel.size * kernel.shape[1]
    )


def backward_freq(b2_turned, c2, kernel, spectrum, ones, threes):
    def body(r, *refs):
        b2, c2, kern, spectrum = refs[:4]
        one = refs[4 : 4 + len(ones)]
        three = refs[4 + len(ones) : 4 + len(ones) + len(threes)]
        grad_freq, grad_b2, grad_c2, *grad_one = refs[4 + len(ones) + len(threes) :]
        _, chan_count, _, width = one[0].shape
        sum_b2 = sum_c2 = None
        for m in range(chan_count):
            cols = pl.ds(m * width, width)
            section = jnp.concatenate([x[r, m] for x in one], axis=0)
            grad_three = jnp.concatenate([x[r, m] for x in three], axis=0)
            spec, kernel_cols = spectrum[r, :, cols], kern[r, :, cols]
            grad_filtered = dot(c2[r], grad_three, 0, 0)
            grad_freq[r, :, cols] = (grad_filtered * spec.astype(F32)).astype(BF)
            grad_spectrum = (grad_filtered * kernel_cols.astype(F32)).astype(BF)
            split_rows(grad_one, r, m, dot(b2[r], grad_spectrum, 1, 0).astype(BF))
            part_c2 = dot(grad_three, times(kernel_cols, spec), 1, 1)
            part_b2 = dot(section, grad_spectrum, 1, 1)
            sum_b2 = part_b2 if sum_b2 is None else sum_b2 + part_b2
            sum_c2 = part_c2 if sum_c2 is None else sum_c2 + part_c2
        grad_b2[r] = sum_b2.astype(BF)
        grad_c2[r] = sum_c2.astype(BF)

    return freq_call(
        body,
        [b2_turned, c2, kernel, spectrum, *ones, *threes],
        [kernel, b2_turned, c2, *ones],
        10 * kernel.size * kernel.shape[1],
    )


def exchange(tensor):
    return lax.all_to_all(tensor, BOTH, split_axis=0, concat_axis=0, tiled=True)


def tie(*tensors):
    return lax.optimization_barrier(tensors)


def swap(tensor, distance, chan_count):
    return lax.ppermute(tensor, "chan", [(m, m ^ distance) for m in range(chan_count)])


def shards(
    query_in, key_in, value_in, freq_kernel, factor_b1, factor_b2, factor_c2, factor_c1, cotangent
):
    seq_count = lax.axis_size("seq")
    chan_count = lax.axis_size("chan")
    devices = seq_count * chan_count
    tok_rows, width = query_in.shape
    local = tok_rows // BS
    unit = local // 4
    half = unit // 2
    rows, blocks, _ = freq_kernel.shape
    query, key, value, cot = [
        x.reshape(local, BS, width) for x in (query_in, key_in, value_in, cotangent)
    ]
    me = lax.axis_index("chan").astype(jnp.int32)
    order = jnp.stack([me, me ^ 2, me ^ 1, me ^ 3])

    def far(part):
        return swap(part, 2, chan_count)

    def near(part):
        return swap(part, 1, chan_count)

    def gathered(factor, part, moved):
        return [factor, moved, near(part), near(moved)]

    def spread(tensor, spans):
        shaped = tensor.reshape(rows, seq_count, local, blocks)
        parts = [shaped[:, :, s : s + n].reshape(rows, -1, blocks) for s, n in spans]
        return jnp.concatenate(parts, axis=1)

    def unspread(tensor, spans):
        at, parts = 0, []
        for _, n in spans:
            size = seq_count * n
            parts.append(tensor[:, at : at + size].reshape(rows, seq_count, n, blocks))
            at += size
        return jnp.concatenate(parts, axis=2).reshape(rows, blocks, blocks)

    direct = rows % 16 == 0

    def part_shape(count):
        return (devices, count, rows, width) if direct else (count, BS, width)

    def send_in(out):
        if not direct:
            out = jnp.transpose(out.reshape(-1, devices, rows, width), (1, 0, 2, 3))
        return out.reshape(-1, width)

    def receive_in(tensor):
        shaped = tensor.reshape(seq_count, chan_count, -1, rows, width)
        return jnp.transpose(shaped, (3, 1, 0, 2, 4)).reshape(rows, chan_count, -1, width)

    def send_out(tensor):
        shaped = tensor.reshape(rows, chan_count, seq_count, -1, width)
        return jnp.transpose(shaped, (2, 1, 3, 0, 4)).reshape(-1, width)

    def receive_out(tensor):
        shaped = tensor.reshape(devices, -1, rows, width)
        if direct:
            return shaped
        return jnp.transpose(shaped, (1, 0, 2, 3)).reshape(-1, BS, width)

    def near_sum(keep, send):
        got = near(send)
        passed = (keep[1].astype(F32) + got[1].astype(F32)).astype(BF)
        return (keep, got), passed

    def far_sum(mine, got):
        keep, near_got = mine
        return (keep[0].astype(F32) + near_got[0].astype(F32) + got.astype(F32)).astype(BF)

    def far_sums(mine, got):
        return [far_sum((mine[2 * k], mine[2 * k + 1]), g) for k, g in enumerate(got)]

    def make_one(start, shift, count, shard, first, earlier):
        out = (part_shape(unit), first, earlier)
        return token_call(
            one_body, order, shard, start, shift, count, None, [key, value], [out], 2
        )[0]

    def make_three(start, shard, total, first, earlier):
        out = (part_shape(total), first, earlier)
        return token_call(
            three_body, order, shard, start, 0, unit, None, [cot, query], [out], 2
        )[0]

    def make_query(start, shift, count, shard, arrived, first, earlier):
        return token_call(
            query_body, order, shard, start, shift, count, (arrived, first), [cot, query],
            [((local, BS, width), start, e) for e in earlier] + ["pairs", "pairs"], 4,
        )

    def make_key(start, shift, count, shard, arrived, first, earlier):
        return token_call(
            key_body, order, shard, start, shift, count, (arrived, first), [key, value],
            [((local, BS, width), start, e) for e in earlier] + ["pairs", "pairs"], 4,
        )

    def steps(make, start, pieces, arrived, earlier):
        mine, got = [], []
        for at, count, shard, shift in pieces:
            *earlier, keep, give = make(start + at, shift, count, shard, arrived, at, earlier)
            near_mine, passed = near_sum(keep, give)
            mine += near_mine
            got.append(far(passed))
        return earlier, mine, got

    b_spans = [(k * unit, unit) for k in range(4)]
    c_spans = [(0, unit), (unit, 3 * unit)]
    b_pieces, c_shards, ones = [], [], []

    part0a = factor_b1[:half]
    moved0a = far(part0a)
    b2 = spread(jnp.swapaxes(factor_b2, 1, 2), b_spans)
    c2 = spread(factor_c2, c_spans)
    moved0a, factor_b1, factor_c1, b2, c2 = tie(moved0a, factor_b1, factor_c1, b2, c2)
    part0b = factor_b1[half:unit]
    moved0b = far(part0b)
    shard = gathered(factor_b1, part0a, moved0a)
    out = make_one(0, 0, half, shard, 0, None)
    out, moved0b, factor_b1 = tie(out, moved0b, factor_b1)
    b_pieces.append([(0, half, shard, 0)])
    most = unit - max(1, unit // 4)
    part1a = factor_b1[unit : unit + most]
    moved1a = far(part1a)
    shard = gathered(factor_b1, part0b, moved0b)
    send = send_in(make_one(half, 0, unit - half, shard, half, out))
    b_pieces[0].append((half, unit - half, shard, 0))
    send, moved1a, factor_b1 = tie(send, moved1a, factor_b1)
    recv = exchange(send)

    part1b = factor_b1[unit + most : 2 * unit]
    moved1b = far(part1b)
    shard = gathered(factor_b1, part1a, moved1a)
    out = make_one(unit, 0, most, shard, 0, None)
    b_pieces.append([(0, most, shard, 0)])
    out, moved1b, factor_b1 = tie(out, moved1b, factor_b1)
    part = factor_b1[2 * unit : 3 * unit]
    moved = far(part)
    shard = gathered(factor_b1, part1b, moved1b)
    send = send_in(make_one(unit + most, 0, unit - most, shard, most, out))
    b_pieces[1].append((most, unit - most, shard, 0))
    recv, send, moved, factor_b1 = tie(recv, send, moved, factor_b1)
    nexts = [
        (factor_b1, 3 * unit), (factor_c1, 0), (factor_c1, unit), (factor_c1, 2 * unit),
        (factor_c1, 3 * unit),
    ]
    later = exchange(send)

    for k in (2, 3):
        ones.append(receive_in(recv))
        recv = later
        factor, at = nexts[k - 2]
        next_part = factor[at : at + unit]
        next_moved = far(next_part)
        shard = gathered(factor_b1, part, moved)
        b_pieces.append([(0, unit, shard, 0)])
        send = send_in(make_one(k * unit, 0, unit, shard, 0, None))
        recv, send, next_moved, *ones = tie(recv, send, next_moved, *ones)
        later = exchange(send)
        part, moved = next_part, next_moved

    ones.append(receive_in(recv))
    recv = later
    factor, at = nexts[2]
    next_part = factor[at : at + unit]
    next_moved = far(next_part)
    c_shards.append(gathered(factor_c1, part, moved))
    send = send_in(make_three(0, c_shards[0], unit, 0, None))
    recv, send, next_moved, *ones = tie(recv, send, next_moved, *ones)
    three0 = exchange(send)
    part, moved = next_part, next_moved

    ones.append(receive_in(recv))
    factor, at = nexts[3]
    next_part = factor[at : at + unit]
    next_moved = far(next_part)
    c_shards.append(gathered(factor_c1, part, moved))
    shapes = [
        jax.ShapeDtypeStruct((rows, chan_count, seq_count * n, width), BF) for _, n in c_spans
    ]
    spectrum, out_b, out_a = forward_freq(b2, c2, freq_kernel, ones, shapes)
    send = send_out(out_a)
    three0, send, out_b, spectrum, next_moved, *ones = tie(
        three0, send, out_b, spectrum, next_moved, *ones
    )
    back_a = exchange(send)
    part, moved = next_part, next_moved

    three0 = receive_in(three0)
    send_b = send_out(out_b)
    factor, at = nexts[4]
    next_part = factor[at : at + unit]
    next_moved = far(next_part)
    c_shards.append(gathered(factor_c1, part, moved))
    c_shards.append(gathered(factor_c1, next_part, next_moved))
    out = None
    for k in (1, 2, 3):
        out = make_three(k * unit, c_shards[k], 3 * unit, (k - 1) * unit, out)
    send = send_in(out)
    back_a, send, three0, send_b = tie(back_a, send, three0, send_b)
    three1 = exchange(send)

    arrived = receive_out(back_a)
    grad_query, c_mine, c_pass = None, [], []
    for k in (1, 2, 3):
        grad_query, keep, give = make_query(
            k * unit, 0, unit, c_shards[k], arrived, (k - 1) * unit, [grad_query]
        )
        mine, passed = near_sum(keep, give)
        c_mine += mine
        c_pass.append(passed)
    c_got = [far(p) for p in c_pass[:2]]
    three1, send_b, grad_query, passed, *rest = tie(
        three1, send_b, grad_query, c_pass[2], *c_mine, *c_got
    )
    c_mine, c_got = rest[:6], rest[6:]
    back_b = exchange(send_b)

    c_got.append(far(passed))
    three1 = receive_in(three1)
    grad_freq, grad_b2, grad_c2, *outs = backward_freq(
        b2, c2, freq_kernel, spectrum, ones, [three0, three1]
    )
    send = send_out(outs[0])
    back_b, send, grad_freq, grad_b2, grad_c2, *rest = tie(
        back_b, send, grad_freq, grad_b2, grad_c2, *c_got, *outs[1:]
    )
    c_got, outs = rest[:3], rest[3:]
    recv = exchange(send)

    def joined(*groups):
        tied = list(tie(*[x for group in groups for x in group]))
        return [[tied.pop(0) for _ in group] for group in groups]

    pieces = [(0, unit, c_shards[0], 0)]
    grad_query, mine, got = steps(make_query, 0, pieces, receive_out(back_b), [grad_query])
    c_sums = far_sums(c_mine, c_got)
    (recv, send), (grad_query,), mine, got, c_sums = joined(
        [recv, send_out(outs[0])], grad_query, mine, got, c_sums
    )
    later = exchange(send)

    c_sums = far_sums(mine, got) + c_sums
    grads, sums = [None, None], []
    for k in range(3):
        grads, mine, got = steps(make_key, k * unit, b_pieces[k], receive_out(recv), grads)
        if k < 2:
            (recv, send), grads, mine, got, sums, c_sums = joined(
                [later, send_out(outs[k + 1])], grads, mine, got, sums, c_sums
            )
            later = exchange(send)
        else:
            grad_c1 = jnp.concatenate(c_sums, axis=0)
            grad_b2 = jnp.swapaxes(unspread(grad_b2, b_spans), 1, 2)
            grad_c2 = unspread(grad_c2, c_spans)
            sums = [jnp.concatenate(sums, axis=0)]
            (recv, grad_b2, grad_c2, grad_c1), grads, mine, got, sums = joined(
                [later, grad_b2, grad_c2, grad_c1], grads, mine, got, sums
            )
        sums += far_sums(mine, got)
    grads, mine, got = steps(make_key, 3 * unit, b_pieces[3], receive_out(recv), grads)
    sums += far_sums(mine, got)

    return (
        grad_query.reshape(query_in.shape),
        grads[0].reshape(query_in.shape),
        grads[1].reshape(query_in.shape),
        grad_freq,
        jnp.concatenate(sums, axis=0),
        grad_b2,
        grad_c2,
        grad_c1,
    )


def solution(mesh):
    token = P("seq", "chan")
    freq = P(BOTH, None, None)
    block = P("seq", "chan", None)
    return jax.shard_map(
        shards,
        mesh=mesh,
        in_specs=(token, token, token, freq, block, freq, freq, block, token),
        out_specs=(token, token, token, freq, block, freq, freq, block),
        check_vma=False,
    )
```

time: 1370 us -> 953 us (0.70)
  blocking collectives: 380 us -> 0 us
  matrix products: 197 us -> 0 us
  local copies, waits for them, and re-layouts: 286 us -> 94.8 us
  Pallas kernels: 0 us -> 163 us
  waiting for transfers between devices: 399 us -> 543 us
  starting transfers between devices: 14.4 us -> 106 us
  other arithmetic: 70.9 us -> 35.1 us
    ppermute x0 -> x50, waiting for transfers between devices: none -> 472 us  [swap(): lax.ppermute(tensor, 'chan', [(m, m ^ distance) for m in range(chan_count)])]
    all_to_all x2 -> x0, blocking collectives: 380 us -> none  [chan_outof(): lax.all_to_all(flattened, ('seq', 'chan'), split_axis=1, concat_axis=0, t...]
    all_gather x2 -> x0, waiting for transfers between devices: 243 us -> none  [the longest x1 143 us: shards(): lax.all_gather(factor_c1, 'chan', axis=1, tiled=True)]
    dot_general x12 -> x0, matrix products: 197 us -> none  [the longest x1 54.5 us: shards(): jnp.einsum('aki,iac->akc', lax.all_gather(factor_c1, 'chan', axis=1, tile...]
    pallas_call x0 -> x22, Pallas kernels: none -> 163 us  [the longest x20 123 us: token_call(): pl.pallas_call(body, grid_spec=pltpu.PrefetchScalarGridSpec(num_scalar_pr...]
    all_to_all x2 -> x12, waiting for transfers between devices: 155 us -> 71 us  [exchange(): return lax.all_to_all(tensor, BOTH, split_axis=0, concat_axis=0, tiled=True)]
    convert_element_type x5 -> x0, local copies, waits for them, and re-layouts: 63.5 us -> none  [the longest x1 17.6 us: forward_freq(): spectrum.astype(jnp.float32)]
    all_to_all x2 -> x12, starting transfers between devices: 14 us -> 60.9 us  [exchange(): return lax.all_to_all(tensor, BOTH, split_axis=0, concat_axis=0, tiled=True)]
  transfers between devices with their start and end apart: 6 -> 62, of which waited for: 4 -> 36; matrix products, arithmetic and copies ran while one was open for 29% -> 10% of each run, Pallas kernels for 0% -> 16%
where the time goes in v1:
time: 953 us; the launch traced here: 943 us
  waiting for transfers between devices  543 us (57%)
  Pallas kernels  163 us (17%)
  starting transfers between devices  106 us (11%)
  local copies, waits for them, and re-layouts  94.8 us (10%)
  other arithmetic  35.1 us (4%)
    ppermute x50, waiting for transfers between devices, swap(): lax.ppermute(tensor, 'chan', [(m, m ^ distance) for m in range(chan_count)])  472 us
    pallas_call x20, Pallas kernels, token_call(): pl.pallas_call(body, grid_spec=pltpu.PrefetchScalarGridSpec(num_scalar_pr...  123 us
    all_to_all x12, waiting for transfers between devices, exchange(): return lax.all_to_all(tensor, BOTH, split_axis=0, concat_axis=0, tiled=True)  71 us
    all_to_all x12, starting transfers between devices, exchange(): return lax.all_to_all(tensor, BOTH, split_axis=0, concat_axis=0, tiled=True)  60.9 us
    ppermute x50, starting transfers between devices, swap(): lax.ppermute(tensor, 'chan', [(m, m ^ distance) for m in range(chan_count)])  44.7 us
    pallas_call x2, Pallas kernels, freq_call(): pl.pallas_call(body, grid=(count // step,), in_specs=[spec(x) for x in in...  39.7 us
    unnamed x170, local copies, waits for them, and re-layouts  28.7 us
    reshape x6, local copies, waits for them, and re-layouts, send_out(): shaped = tensor.reshape(rows, chan_count, seq_count, -1, width)  27.4 us
  transfers between devices with their start and end apart: 62, of which 36 were waited for; matrix products, arithmetic and copies ran while one was open for 10% of the time, Pallas kernels for 16%

profile of v1, /device:TPU:0, one launch (start us, length us, event | category | flops | bytes accessed | tf_op | source)
XLA Modules:
  0.0 943.3 jit_solution(1873728639209267853)
XLA Ops:
  27.0 6.7 collective-permute-done.3.refs_1_
  44.7 9.6 %collective-permute-done.6.refs_1_ = bf16[6,128,512]{2,1,0:T(8,128)(2,1)S(1)} collective-permute-done((bf16[6,128,512]{2,1,0:T(8,128)(2,1)S(1)}, bf16[6,128,512]{2,1,0:T(8,128)(2,1)S(1)}, u32[]{:S(2)}, u32[]{:S(2)}) %collective-permute-start.6) | collective-permute-done | bytes 786464 | tf_op jit(solution)/shard_map/ppermute | solution.py:250
  54.2 6.1 all-to-all-start
  65.4 5.9 shard_map.154.refs_6_
  71.3 11.7 %collective-permute-done.9.refs_1_ = bf16[2,128,512]{2,1,0:T(8,128)(2,1)S(1)} collective-permute-done((bf16[2,128,512]{2,1,0:T(8,128)(2,1)S(1)}, bf16[2,128,512]{2,1,0:T(8,128)(2,1)S(1)}, u32[]{:S(2)}, u32[]{:S(2)}) %collective-permute-start.9) | collective-permute-done | bytes 262176 | tf_op jit(solution)/shard_map/ppermute | solution.py:250
  95.4 18.7 %collective-permute-done.12.refs_1_ = bf16[8,128,512]{2,1,0:T(8,128)(2,1)} collective-permute-done((bf16[8,128,512]{2,1,0:T(8,128)(2,1)}, bf16[8,128,512]{2,1,0:T(8,128)(2,1)}, u32[]{:S(2)}, u32[]{:S(2)}) %collective-permute-start.12) | collective-permute-done | bytes 1048608 | tf_op jit(solution)/shard_map/ppermute | solution.py:250
  114.2 8.7 all-to-all-start.1
  130.6 5.9 shard_map.156
  136.5 34.1 %collective-permute-done.15.refs_1_ = bf16[8,128,512]{2,1,0:T(8,128)(2,1)S(1)} collective-permute-done((bf16[8,128,512]{2,1,0:T(8,128)(2,1)S(1)}, bf16[8,128,512]{2,1,0:T(8,128)(2,1)S(1)}, u32[]{:S(2)}, u32[]{:S(2)}) %collective-permute-start.15) | collective-permute-done | bytes 1048608 | tf_op jit(solution)/shard_map/ppermute | solution.py:250
  187.7 5.9 shard_map.157
  193.5 30.8 %collective-permute-done.18.refs_1_ = bf16[8,128,512]{2,1,0:T(8,128)(2,1)} collective-permute-done((bf16[8,128,512]{2,1,0:T(8,128)(2,1)S(1)}, bf16[8,128,512]{2,1,0:T(8,128)(2,1)}, u32[]{:S(2)}, u32[]{:S(2)}) %collective-permute-start.18) | collective-permute-done | bytes 1048608 | tf_op jit(solution)/shard_map/ppermute | solution.py:250
  234.4 5.9 shard_map.158
  240.3 36.4 %collective-permute-done.21.refs_1_ = bf16[8,128,512]{2,1,0:T(8,128)(2,1)} collective-permute-done((bf16[8,128,512]{2,1,0:T(8,128)(2,1)}, bf16[8,128,512]{2,1,0:T(8,128)(2,1)}, u32[]{:S(2)}, u32[]{:S(2)}) %collective-permute-start.21) | collective-permute-done | bytes 1048608 | tf_op jit(solution)/shard_map/ppermute | solution.py:250
  287.5 16.3 %shard_map.159 = (bf16[16,256,1024]{2,1,0:T(8,128)(2,1)}, bf16[16,4,64,256]{3,2,1,0:T(8,128)(2,1)}, bf16[16,4,192,256]{3,2,1,0:T(8,128)(2,1)}) custom-call(bf16[16,256,256]{2,1,0:T(8,128)(2,1)} %get-tuple-element.198.refs_0_, bf16[16,256,256]{2,1,0:T(8,128)(2,1)} %get-tuple-element.199.refs_1_, bf16[16,256,1024]{2,1,0:T(8,128)(2,1)} %refs_2_.3, ...), custom_call_target="tpu_custom_call" | custom-call | flops 4294967296 | bytes 37748736 | tf_op jit(solution)/shard_map/pallas_call | solution.py:170
  303.9 10.6 %copy.44 = bf16[16,4,8,24,256]{4,0,3,1,2:T(8,128)(2,1)} copy(bf16[16,4,8,24,256]{4,3,2,1,0:T(8,128)(2,1)} %bitcast.268) | data formatting | bytes 12582912 | tf_op jit(solution)/shard_map/reshape | solution.py:307
  314.5 15.2 %collective-permute-done.22.refs_1_ = bf16[8,128,512]{2,1,0:T(8,128)(2,1)S(1)} collective-permute-done((bf16[8,128,512]{2,1,0:T(8,128)(2,1)}, bf16[8,128,512]{2,1,0:T(8,128)(2,1)S(1)}, u32[]{:S(2)}, u32[]{:S(2)}) %collective-permute-start.22) | collective-permute-done | bytes 1048608 | tf_op jit(solution)/shard_map/ppermute | solution.py:250
  330.7 4.7 all-to-all-start.5
  338.3 79.3 %collective-permute-done.23.refs_1_ = bf16[8,128,512]{2,1,0:T(8,128)(2,1)S(1)} collective-permute-done((bf16[8,128,512]{2,1,0:T(8,128)(2,1)}, bf16[8,128,512]{2,1,0:T(8,128)(2,1)S(1)}, u32[]{:S(2)}, u32[]{:S(2)}) %collective-permute-start.23) | collective-permute-done | bytes 1048608 | tf_op jit(solution)/shard_map/ppermute | solution.py:250
  418.6 5.8 shard_map.160.refs_6_
  430.6 5.8 shard_map.161.refs_6_
  437.4 5.8 shard_map.162
  443.3 32.1 %all-to-all-done.5 = bf16[32,384,256]{2,1,0:T(8,128)(2,1)} async-done(((bf16[32,384,256]{2,1,0:T(8,128)(2,1)}), bf16[32,384,256]{2,1,0:T(8,128)(2,1)}, u32[]{:S(2)}, u32[]{:S(2)}) %all-to-all-start.5) | async-done | bytes 6291488 | tf_op jit(solution)/shard_map/all_to_all | solution.py:242
  475.4 5.7 all-to-all-start.6
  481.1 7.6 shard_map.163
  488.7 7.7 shard_map.164
  496.9 7.8 shard_map.165
  509.7 53.8 %collective-permute-done.34 = bf16[8,128,512]{2,1,0:T(8,128)(2,1)S(1)} collective-permute-done((bf16[8,128,512]{2,1,0:T(8,128)(2,1)S(1)}, bf16[8,128,512]{2,1,0:T(8,128)(2,1)S(1)}, u32[]{:S(2)}, u32[]{:S(2)}) %collective-permute-start.34) | collective-permute-done | bytes 1048608 | tf_op jit(solution)/shard_map/ppermute | solution.py:250
  564.6 21.9 %collective-permute-done.33 = bf16[8,128,512]{2,1,0:T(8,128)(2,1)} collective-permute-done((bf16[8,128,512]{2,1,0:T(8,128)(2,1)S(1)}, bf16[8,128,512]{2,1,0:T(8,128)(2,1)}, u32[]{:S(2)}, u32[]{:S(2)}) %collective-permute-start.33) | collective-permute-done | bytes 1048608 | tf_op jit(solution)/shard_map/ppermute | solution.py:250
  586.5 34.7 %all-to-all-done.6 = bf16[32,384,256]{2,1,0:T(8,128)(2,1)} async-done(((bf16[32,384,256]{2,1,0:T(8,128)(2,1)}), bf16[32,384,256]{2,1,0:T(8,128)(2,1)}, u32[]{:S(2)}, u32[]{:S(2)}) %all-to-all-start.6) | async-done | bytes 6291488 | tf_op jit(solution)/shard_map/all_to_all | solution.py:242
  621.2 5.7 all-to-all-start.7
  628.8 7.7 copy.47
  636.6 23.4 %shard_map.166 = (bf16[16,256,1024]{2,1,0:T(8,128)(2,1)}, bf16[16,256,256]{2,1,0:T(8,128)(2,1)}, bf16[16,256,256]{2,1,0:T(8,128)(2,1)}, bf16[16,4,64,256]{3,2,1,...) custom-call(bf16[16,256,256]{2,1,0:T(8,128)(2,1)} %get-tuple-element, ...), custom_call_target="tpu_custom_call" | custom-call | flops 10737418240 | bytes 58720256 | tf_op jit(solution)/shard_map/pallas_call | solution.py:170
  660.0 4.6 copy.48
  664.6 10.2 %collective-permute-done.35 = bf16[8,128,512]{2,1,0:T(8,128)(2,1)} collective-permute-done((bf16[8,128,512]{2,1,0:T(8,128)(2,1)S(1)}, bf16[8,128,512]{2,1,0:T(8,128)(2,1)}, u32[]{:S(2)}, u32[]{:S(2)}) %collective-permute-start.35) | collective-permute-done | bytes 1048608 | tf_op jit(solution)/shard_map/ppermute | solution.py:250
  681.1 7.6 shard_map.167
  708.1 23.0 %collective-permute-done.37 = bf16[8,128,512]{2,1,0:T(8,128)(2,1)} collective-permute-done((bf16[8,128,512]{2,1,0:T(8,128)(2,1)S(1)}, bf16[8,128,512]{2,1,0:T(8,128)(2,1)}, u32[]{:S(2)}, u32[]{:S(2)}) %collective-permute-start.37) | collective-permute-done | bytes 1048608 | tf_op jit(solution)/shard_map/ppermute | solution.py:250
  736.8 5.2 shard_map.168
  742.0 5.4 shard_map.169
  759.9 13.0 %collective-permute-done.41 = bf16[4,128,512]{2,1,0:T(8,128)(2,1)S(1)} collective-permute-done((bf16[4,128,512]{2,1,0:T(8,128)(2,1)S(1)}, bf16[4,128,512]{2,1,0:T(8,128)(2,1)S(1)}, u32[]{:S(2)}, u32[]{:S(2)}) %collective-permute-start.41) | collective-permute-done | bytes 524320 | tf_op jit(solution)/shard_map/ppermute | solution.py:250
  773.7 13.6 %collective-permute-done.40 = bf16[4,128,512]{2,1,0:T(8,128)(2,1)} collective-permute-done((bf16[4,128,512]{2,1,0:T(8,128)(2,1)S(1)}, bf16[4,128,512]{2,1,0:T(8,128)(2,1)}, u32[]{:S(2)}, u32[]{:S(2)}) %collective-permute-start.40) | collective-permute-done | bytes 524320 | tf_op jit(solution)/shard_map/ppermute | solution.py:250
  791.7 8.5 shard_map.170
  803.5 4.5 shard_map.171
  815.0 28.4 %collective-permute-done.45 = bf16[2,128,512]{2,1,0:T(8,128)(2,1)S(1)} collective-permute-done((bf16[2,128,512]{2,1,0:T(8,128)(2,1)S(1)}, bf16[2,128,512]{2,1,0:T(8,128)(2,1)S(1)}, u32[]{:S(2)}, u32[]{:S(2)}) %collective-permute-start.45) | collective-permute-done | bytes 262176 | tf_op jit(solution)/shard_map/ppermute | solution.py:250
  844.8 4.6 all-to-all-start.11
  849.4 8.1 shard_map.172
  870.9 27.4 %collective-permute-done.47 = bf16[8,128,512]{2,1,0:T(8,128)(2,1)} collective-permute-done((bf16[8,128,512]{2,1,0:T(8,128)(2,1)S(1)}, bf16[8,128,512]{2,1,0:T(8,128)(2,1)}, u32[]{:S(2)}, u32[]{:S(2)}) %collective-permute-start.47) | collective-permute-done | bytes 1048608 | tf_op jit(solution)/shard_map/ppermute | solution.py:250
  898.3 7.9 shard_map.173
  919.7 19.2 %collective-permute-done.49 = bf16[8,128,512]{2,1,0:T(8,128)(2,1)} collective-permute-done((bf16[8,128,512]{2,1,0:T(8,128)(2,1)S(1)}, bf16[8,128,512]{2,1,0:T(8,128)(2,1)}, u32[]{:S(2)}, u32[]{:S(2)}) %collective-permute-start.49) | collective-permute-done | bytes 1048608 | tf_op jit(solution)/shard_map/ppermute | solution.py:250
  (320 shorter events, 212.2 us)
Async XLA Ops:
  2.5 19.4 %collective-permute-start.1 = (bf16[4,128,512]{2,1,0:T(8,128)(2,1)}, bf16[4,128,512]{2,1,0:T(8,128)(2,1)S(1)}, u32[]{:S(2)}, u32[]{:S(2)}) collective-permute-start(bf16[4,128,512]{2,1,0:T(8,128)(2,1)} %slice.186), channel_id=1, source_target_pairs={{0,1},{1,0},{2,3},{3,2},{4,5},{5,4},{6,7},{7,6},{8,9},{9,8},{10,11... | collective-permute-start | bytes 1572872 | tf_op jit(solution)/shard_map/ppermute | solution.py:250
  3.0 15.3 %collective-permute-start = (bf16[4,128,512]{2,1,0:T(8,128)(2,1)}, bf16[4,128,512]{2,1,0:T(8,128)(2,1)S(1)}, u32[]{:S(2)}, u32[]{:S(2)}) collective-permute-start(bf16[4,128,512]{2,1,0:T(8,128)(2,1)} %slice.186), channel_id=1, source_target_pairs={{0,2},{1,3},{2,0},{3,1},{4,6},{5,7},{6,4},{7,5},{8,10},{9,11},{10,... | collective-permute-start | bytes 1572872 | tf_op jit(solution)/shard_map/ppermute | solution.py:250
  19.6 14.2 %collective-permute-start.3 = (bf16[4,128,512]{2,1,0:T(8,128)(2,1)S(1)}, bf16[4,128,512]{2,1,0:T(8,128)(2,1)S(1)}, u32[]{:S(2)}, u32[]{:S(2)}) collective-permute-start(bf16[4,128,512]{2,1,0:T(8,128)(2,1)S(1)} %slice.193), channel_id=1, source_target_pairs={{0,2},{1,3},{2,0},{3,1},{4,6},{5,7},{6,4},{7,5},{8,10},{9,11},{10,... | collective-permute-start | bytes 1572872 | tf_op jit(solution)/shard_map/ppermute | solution.py:250
  35.2 19.0 %collective-permute-start.6 = (bf16[6,128,512]{2,1,0:T(8,128)(2,1)S(1)}, bf16[6,128,512]{2,1,0:T(8,128)(2,1)S(1)}, u32[]{:S(2)}, u32[]{:S(2)}) collective-permute-start(bf16[6,128,512]{2,1,0:T(8,128)(2,1)S(1)} %slice.194), channel_id=1, source_target_pairs={{0,2},{1,3},{2,0},{3,1},{4,6},{5,7},{6,4},{7,5},{8,10},{9,11},{10,... | collective-permute-start | bytes 2359304 | tf_op jit(solution)/shard_map/ppermute | solution.py:250
  54.2 60.0 %all-to-all-start = ((bf16[32,128,256]{2,1,0:T(8,128)(2,1)}), bf16[32,128,256]{2,1,0:T(8,128)(2,1)S(1)}, u32[]{:S(2)}, u32[]{:S(2)}) async-start(bf16[32,128,256]{2,1,0:T(8,128)(2,1)} %bitcast.242), calls=%async_computation | async-start | bytes 4194304 | tf_op jit(solution)/shard_map/all_to_all | solution.py:242
  61.8 21.2 %collective-permute-start.9 = (bf16[2,128,512]{2,1,0:T(8,128)(2,1)S(1)}, bf16[2,128,512]{2,1,0:T(8,128)(2,1)S(1)}, u32[]{:S(2)}, u32[]{:S(2)}) collective-permute-start(bf16[2,128,512]{2,1,0:T(8,128)(2,1)S(1)} %slice.195), channel_id=1, source_target_pairs={{0,2},{1,3},{2,0},{3,1},{4,6},{5,7},{6,4},{7,5},{8,10},{9,11},{10,... | collective-permute-start | bytes 786440 | tf_op jit(solution)/shard_map/ppermute | solution.py:250
  85.4 28.8 %collective-permute-start.12 = (bf16[8,128,512]{2,1,0:T(8,128)(2,1)}, bf16[8,128,512]{2,1,0:T(8,128)(2,1)}, u32[]{:S(2)}, u32[]{:S(2)}) collective-permute-start(bf16[8,128,512]{2,1,0:T(8,128)(2,1)} %slice.196), channel_id=1, source_target_pairs={{0,2},{1,3},{2,0},{3,1},{4,6},{5,7},{6,4},{7,5},{8,10},{9,11},{10,... | collective-permute-start | bytes 3145736 | tf_op jit(solution)/shard_map/ppermute | solution.py:250
  114.2 57.5 %all-to-all-start.1 = ((bf16[32,128,256]{2,1,0:T(8,128)(2,1)}), bf16[32,128,256]{2,1,0:T(8,128)(2,1)}, u32[]{:S(2)}, u32[]{:S(2)}) async-start(bf16[32,128,256]{2,1,0:T(8,128)(2,1)} %bitcast.243), calls=%async_computation.1 | async-start | bytes 4194304 | tf_op jit(solution)/shard_map/all_to_all | solution.py:242
  122.9 5.7 collective-permute-start.13
  123.2 5.4 collective-permute-start.14
  124.8 45.8 %collective-permute-start.15 = (bf16[8,128,512]{2,1,0:T(8,128)(2,1)S(1)}, bf16[8,128,512]{2,1,0:T(8,128)(2,1)S(1)}, u32[]{:S(2)}, u32[]{:S(2)}) collective-permute-start(bf16[8,128,512]{2,1,0:T(8,128)(2,1)S(1)} %slice.197), channel_id=1, source_target_pairs={{0,2},{1,3},{2,0},{3,1},{4,6},{5,7},{6,4},{7,5},{8,10},{9,11},{10,... | collective-permute-start | bytes 3145736 | tf_op jit(solution)/shard_map/ppermute | solution.py:250
  171.7 52.9 %all-to-all-start.2 = ((bf16[32,128,256]{2,1,0:T(8,128)(2,1)}), bf16[32,128,256]{2,1,0:T(8,128)(2,1)S(1)}, u32[]{:S(2)}, u32[]{:S(2)}) async-start(bf16[32,128,256]{2,1,0:T(8,128)(2,1)} %bitcast.254), calls=%async_computation.2 | async-start | bytes 4194304 | tf_op jit(solution)/shard_map/all_to_all | solution.py:242
  179.8 5.9 collective-permute-start.16
  180.0 5.7 collective-permute-start.17
  180.3 44.0 %collective-permute-start.18 = (bf16[8,128,512]{2,1,0:T(8,128)(2,1)S(1)}, bf16[8,128,512]{2,1,0:T(8,128)(2,1)}, u32[]{:S(2)}, u32[]{:S(2)}) collective-permute-start(bf16[8,128,512]{2,1,0:T(8,128)(2,1)S(1)} %get-tuple-element.347), channel_id=1, source_target_pairs={{0,2},{1,3},{2,0},{3,1},{4,6},{5,7},{6,4},{7,5},{8,10},{9,11},{10,... | collective-permute-start | bytes 3145736 | tf_op jit(solution)/shard_map/ppermute | solution.py:250
  224.6 53.0 %all-to-all-start.3 = ((bf16[32,128,256]{2,1,0:T(8,128)(2,1)}), bf16[32,128,256]{2,1,0:T(8,128)(2,1)}, u32[]{:S(2)}, u32[]{:S(2)}) async-start(bf16[32,128,256]{2,1,0:T(8,128)(2,1)} %bitcast.255), calls=%async_computation.3 | async-start | bytes 4194304 | tf_op jit(solution)/shard_map/all_to_all | solution.py:242
  229.4 47.2 %collective-permute-start.21 = (bf16[8,128,512]{2,1,0:T(8,128)(2,1)}, bf16[8,128,512]{2,1,0:T(8,128)(2,1)}, u32[]{:S(2)}, u32[]{:S(2)}) collective-permute-start(bf16[8,128,512]{2,1,0:T(8,128)(2,1)} %get-tuple-element.346), channel_id=1, source_target_pairs={{0,2},{1,3},{2,0},{3,1},{4,6},{5,7},{6,4},{7,5},{8,10},{9,11},{10,... | collective-permute-start | bytes 3145736 | tf_op jit(solution)/shard_map/ppermute | solution.py:250
  277.6 53.1 %all-to-all-start.4 = ((bf16[32,128,256]{2,1,0:T(8,128)(2,1)}), bf16[32,128,256]{2,1,0:T(8,128)(2,1)S(1)}, u32[]{:S(2)}, u32[]{:S(2)}) async-start(bf16[32,128,256]{2,1,0:T(8,128)(2,1)} %bitcast.256), calls=%async_computation.4 | async-start | bytes 4194304 | tf_op jit(solution)/shard_map/all_to_all | solution.py:242
  281.9 47.8 %collective-permute-start.22 = (bf16[8,128,512]{2,1,0:T(8,128)(2,1)}, bf16[8,128,512]{2,1,0:T(8,128)(2,1)S(1)}, u32[]{:S(2)}, u32[]{:S(2)}) collective-permute-start(bf16[8,128,512]{2,1,0:T(8,128)(2,1)} %get-tuple-element.345), channel_id=1, source_target_pairs={{0,2},{1,3},{2,0},{3,1},{4,6},{5,7},{6,4},{7,5},{8,10},{9,11},{10,... | collective-permute-start | bytes 3145736 | tf_op jit(solution)/shard_map/ppermute | solution.py:250
  330.7 144.7 %all-to-all-start.5 = ((bf16[32,384,256]{2,1,0:T(8,128)(2,1)}), bf16[32,384,256]{2,1,0:T(8,128)(2,1)}, u32[]{:S(2)}, u32[]{:S(2)}) async-start(bf16[32,384,256]{2,1,0:T(8,128)(2,1)} %bitcast.239), calls=%async_computation.5 | async-start | bytes 12582912 | tf_op jit(solution)/shard_map/all_to_all | solution.py:242
  335.4 82.2 %collective-permute-start.23 = (bf16[8,128,512]{2,1,0:T(8,128)(2,1)}, bf16[8,128,512]{2,1,0:T(8,128)(2,1)S(1)}, u32[]{:S(2)}, u32[]{:S(2)}) collective-permute-start(bf16[8,128,512]{2,1,0:T(8,128)(2,1)} %get-tuple-element.344), channel_id=1, source_target_pairs={{0,2},{1,3},{2,0},{3,1},{4,6},{5,7},{6,4},{7,5},{8,10},{9,11},{10,... | collective-permute-start | bytes 3145736 | tf_op jit(solution)/shard_map/ppermute | solution.py:250
  337.3 80.3 %collective-permute-start.28 = (bf16[8,128,512]{2,1,0:T(8,128)(2,1)}, bf16[8,128,512]{2,1,0:T(8,128)(2,1)S(1)}, u32[]{:S(2)}, u32[]{:S(2)}) collective-permute-start(bf16[8,128,512]{2,1,0:T(8,128)(2,1)} %get-tuple-element.346), channel_id=1, source_target_pairs={{0,1},{1,0},{2,3},{3,2},{4,5},{5,4},{6,7},{7,6},{8,9},{9,8},{10,11... | collective-permute-start | bytes 3145736 | tf_op jit(solution)/shard_map/ppermute | solution.py:250
  337.3 80.8 %collective-permute-start.29 = (bf16[8,128,512]{2,1,0:T(8,128)(2,1)}, bf16[8,128,512]{2,1,0:T(8,128)(2,1)}, u32[]{:S(2)}, u32[]{:S(2)}) collective-permute-start(bf16[8,128,512]{2,1,0:T(8,128)(2,1)} %collective-permute-done.21.refs_1_), channel_id=1, source_target_pairs={{0,1},{1,0},{2,3},{3,2},{4,5},{5,4},{6,7},{7,6},{8,9},{9,8},{10,11... | collective-permute-start | bytes 3145736 | tf_op jit(solution)/shard_map/ppermute | solution.py:250
  337.8 91.8 %collective-permute-start.26 = (bf16[8,128,512]{2,1,0:T(8,128)(2,1)}, bf16[8,128,512]{2,1,0:T(8,128)(2,1)S(1)}, u32[]{:S(2)}, u32[]{:S(2)}) collective-permute-start(bf16[8,128,512]{2,1,0:T(8,128)(2,1)} %get-tuple-element.345), channel_id=1, source_target_pairs={{0,1},{1,0},{2,3},{3,2},{4,5},{5,4},{6,7},{7,6},{8,9},{9,8},{10,11... | collective-permute-start | bytes 3145736 | tf_op jit(solution)/shard_map/ppermute | solution.py:250
  337.8 91.8 %collective-permute-start.27 = (bf16[8,128,512]{2,1,0:T(8,128)(2,1)S(1)}, bf16[8,128,512]{2,1,0:T(8,128)(2,1)}, u32[]{:S(2)}, u32[]{:S(2)}) collective-permute-start(bf16[8,128,512]{2,1,0:T(8,128)(2,1)S(1)} %collective-permute-done.22.refs_1_), channel_id=1, source_target_pairs={{0,1},{1,0},{2,3},{3,2},{4,5},{5,4},{6,7},{7,6},{8,9},{9,8},{10,11... | collective-permute-start | bytes 3145736 | tf_op jit(solution)/shard_map/ppermute | solution.py:250
  417.6 18.8 %collective-permute-start.24 = (bf16[8,128,512]{2,1,0:T(8,128)(2,1)}, bf16[8,128,512]{2,1,0:T(8,128)(2,1)S(1)}, u32[]{:S(2)}, u32[]{:S(2)}) collective-permute-start(bf16[8,128,512]{2,1,0:T(8,128)(2,1)} %get-tuple-element.344), channel_id=1, source_target_pairs={{0,1},{1,0},{2,3},{3,2},{4,5},{5,4},{6,7},{7,6},{8,9},{9,8},{10,11... | collective-permute-start | bytes 3145736 | tf_op jit(solution)/shard_map/ppermute | solution.py:250
  417.6 18.8 %collective-permute-start.25 = (bf16[8,128,512]{2,1,0:T(8,128)(2,1)S(1)}, bf16[8,128,512]{2,1,0:T(8,128)(2,1)}, u32[]{:S(2)}, u32[]{:S(2)}) collective-permute-start(bf16[8,128,512]{2,1,0:T(8,128)(2,1)S(1)} %collective-permute-done.23.refs_1_), channel_id=1, source_target_pairs={{0,1},{1,0},{2,3},{3,2},{4,5},{5,4},{6,7},{7,6},{8,9},{9,8},{10,11... | collective-permute-start | bytes 3145736 | tf_op jit(solution)/shard_map/ppermute | solution.py:250
  475.4 145.8 %all-to-all-start.6 = ((bf16[32,384,256]{2,1,0:T(8,128)(2,1)}), bf16[32,384,256]{2,1,0:T(8,128)(2,1)}, u32[]{:S(2)}, u32[]{:S(2)}) async-start(bf16[32,384,256]{2,1,0:T(8,128)(2,1)} %bitcast.237), calls=%async_computation.6 | async-start | bytes 12582912 | tf_op jit(solution)/shard_map/all_to_all | solution.py:242
  496.3 8.6 collective-permute-start.32
  496.5 10.5 %collective-permute-start.31 = (bf16[2,8,128,512]{3,2,1,0:T(8,128)(2,1)}, bf16[2,8,128,512]{3,2,1,0:T(8,128)(2,1)S(1)}, u32[]{:S(2)}, u32[]{:S(2)}) collective-permute-start(bf16[2,8,128,512]{3,2,1,0:T(8,128)(2,1)} %get-tuple-element.221), channel_id=1, source_target_pairs={{0,1},{1,0},{2,3},{3,2},{4,5},{5,4},{6,7},{7,6},{8,9},{9,8},{10,11... | collective-permute-start | bytes 6291464 | tf_op jit(solution)/shard_map/ppermute | solution.py:250
  504.7 4.7 collective-permute-start.30
  505.3 58.3 %collective-permute-start.34 = (bf16[8,128,512]{2,1,0:T(8,128)(2,1)S(1)}, bf16[8,128,512]{2,1,0:T(8,128)(2,1)S(1)}, u32[]{:S(2)}, u32[]{:S(2)}) collective-permute-start(bf16[8,128,512]{2,1,0:T(8,128)(2,1)S(1)} %fusion.9), channel_id=1, source_target_pairs={{0,2},{1,3},{2,0},{3,1},{4,6},{5,7},{6,4},{7,5},{8,10},{9,11},{10,... | collective-permute-start | bytes 3145736 | tf_op jit(solution)/shard_map/ppermute | solution.py:250
  507.3 79.2 %collective-permute-start.33 = (bf16[8,128,512]{2,1,0:T(8,128)(2,1)S(1)}, bf16[8,128,512]{2,1,0:T(8,128)(2,1)}, u32[]{:S(2)}, u32[]{:S(2)}) collective-permute-start(bf16[8,128,512]{2,1,0:T(8,128)(2,1)S(1)} %fusion.8), channel_id=1, source_target_pairs={{0,2},{1,3},{2,0},{3,1},{4,6},{5,7},{6,4},{7,5},{8,10},{9,11},{10,... | collective-permute-start | bytes 3145736 | tf_op jit(solution)/shard_map/ppermute | solution.py:250
  621.2 54.4 %all-to-all-start.7 = ((bf16[32,128,256]{2,1,0:T(8,128)(2,1)}), bf16[32,128,256]{2,1,0:T(8,128)(2,1)S(1)}, u32[]{:S(2)}, u32[]{:S(2)}) async-start(bf16[32,128,256]{2,1,0:T(8,128)(2,1)} %bitcast.257), calls=%async_computation.7 | async-start | bytes 4194304 | tf_op jit(solution)/shard_map/all_to_all | solution.py:242
  626.9 47.9 %collective-permute-start.35 = (bf16[8,128,512]{2,1,0:T(8,128)(2,1)S(1)}, bf16[8,128,512]{2,1,0:T(8,128)(2,1)}, u32[]{:S(2)}, u32[]{:S(2)}) collective-permute-start(bf16[8,128,512]{2,1,0:T(8,128)(2,1)S(1)} %fusion.7), channel_id=1, source_target_pairs={{0,2},{1,3},{2,0},{3,1},{4,6},{5,7},{6,4},{7,5},{8,10},{9,11},{10,... | collective-permute-start | bytes 3145736 | tf_op jit(solution)/shard_map/ppermute | solution.py:250
  676.9 54.2 %all-to-all-start.8 = ((bf16[32,128,256]{2,1,0:T(8,128)(2,1)}), bf16[32,128,256]{2,1,0:T(8,128)(2,1)S(1)}, u32[]{:S(2)}, u32[]{:S(2)}) async-start(bf16[32,128,256]{2,1,0:T(8,128)(2,1)} %bitcast.265), calls=%async_computation.8 | async-start | bytes 4194304 | tf_op jit(solution)/shard_map/all_to_all | solution.py:242
  695.5 35.7 %collective-permute-start.37 = (bf16[8,128,512]{2,1,0:T(8,128)(2,1)S(1)}, bf16[8,128,512]{2,1,0:T(8,128)(2,1)}, u32[]{:S(2)}, u32[]{:S(2)}) collective-permute-start(bf16[8,128,512]{2,1,0:T(8,128)(2,1)S(1)} %fusion.10), channel_id=1, source_target_pairs={{0,2},{1,3},{2,0},{3,1},{4,6},{5,7},{6,4},{7,5},{8,10},{9,11},{10,... | collective-permute-start | bytes 3145736 | tf_op jit(solution)/shard_map/ppermute | solution.py:250
  732.5 54.9 %all-to-all-start.9 = ((bf16[32,128,256]{2,1,0:T(8,128)(2,1)}), bf16[32,128,256]{2,1,0:T(8,128)(2,1)}, u32[]{:S(2)}, u32[]{:S(2)}) async-start(bf16[32,128,256]{2,1,0:T(8,128)(2,1)} %bitcast.260), calls=%async_computation.9 | async-start | bytes 4194304 | tf_op jit(solution)/shard_map/all_to_all | solution.py:242
  747.9 6.0 collective-permute-start.38
  751.9 21.0 %collective-permute-start.41 = (bf16[4,128,512]{2,1,0:T(8,128)(2,1)S(1)}, bf16[4,128,512]{2,1,0:T(8,128)(2,1)S(1)}, u32[]{:S(2)}, u32[]{:S(2)}) collective-permute-start(bf16[4,128,512]{2,1,0:T(8,128)(2,1)S(1)} %fusion.17), channel_id=1, source_target_pairs={{0,2},{1,3},{2,0},{3,1},{4,6},{5,7},{6,4},{7,5},{8,10},{9,11},{10,... | collective-permute-start | bytes 1572872 | tf_op jit(solution)/shard_map/ppermute | solution.py:250
  754.0 33.3 %collective-permute-start.40 = (bf16[4,128,512]{2,1,0:T(8,128)(2,1)S(1)}, bf16[4,128,512]{2,1,0:T(8,128)(2,1)}, u32[]{:S(2)}, u32[]{:S(2)}) collective-permute-start(bf16[4,128,512]{2,1,0:T(8,128)(2,1)S(1)} %fusion.16), channel_id=1, source_target_pairs={{0,2},{1,3},{2,0},{3,1},{4,6},{5,7},{6,4},{7,5},{8,10},{9,11},{10,... | collective-permute-start | bytes 1572872 | tf_op jit(solution)/shard_map/ppermute | solution.py:250
  787.4 56.1 %all-to-all-start.10 = ((bf16[32,128,256]{2,1,0:T(8,128)(2,1)}), bf16[32,128,256]{2,1,0:T(8,128)(2,1)S(1)}, u32[]{:S(2)}, u32[]{:S(2)}) async-start(bf16[32,128,256]{2,1,0:T(8,128)(2,1)} %bitcast.259), calls=%async_computation.10 | async-start | bytes 4194304 | tf_op jit(solution)/shard_map/all_to_all | solution.py:242
  800.2 8.1 collective-permute-start.42
  808.5 34.9 %collective-permute-start.44 = (bf16[6,128,512]{2,1,0:T(8,128)(2,1)S(1)}, bf16[6,128,512]{2,1,0:T(8,128)(2,1)}, u32[]{:S(2)}, u32[]{:S(2)}) collective-permute-start(bf16[6,128,512]{2,1,0:T(8,128)(2,1)S(1)} %fusion.15), channel_id=1, source_target_pairs={{0,2},{1,3},{2,0},{3,1},{4,6},{5,7},{6,4},{7,5},{8,10},{9,11},{10,... | collective-permute-start | bytes 2359304 | tf_op jit(solution)/shard_map/ppermute | solution.py:250
  812.5 30.9 %collective-permute-start.45 = (bf16[2,128,512]{2,1,0:T(8,128)(2,1)S(1)}, bf16[2,128,512]{2,1,0:T(8,128)(2,1)S(1)}, u32[]{:S(2)}, u32[]{:S(2)}) collective-permute-start(bf16[2,128,512]{2,1,0:T(8,128)(2,1)S(1)} %fusion.19), channel_id=1, source_target_pairs={{0,2},{1,3},{2,0},{3,1},{4,6},{5,7},{6,4},{7,5},{8,10},{9,11},{10,... | collective-permute-start | bytes 786440 | tf_op jit(solution)/shard_map/ppermute | solution.py:250
  844.8 53.5 %all-to-all-start.11 = ((bf16[32,128,256]{2,1,0:T(8,128)(2,1)}), bf16[32,128,256]{2,1,0:T(8,128)(2,1)}, u32[]{:S(2)}, u32[]{:S(2)}) async-start(bf16[32,128,256]{2,1,0:T(8,128)(2,1)} %bitcast.258), calls=%async_computation.11 | async-start | bytes 4194304 | tf_op jit(solution)/shard_map/all_to_all | solution.py:242
  862.4 35.9 %collective-permute-start.47 = (bf16[8,128,512]{2,1,0:T(8,128)(2,1)S(1)}, bf16[8,128,512]{2,1,0:T(8,128)(2,1)}, u32[]{:S(2)}, u32[]{:S(2)}) collective-permute-start(bf16[8,128,512]{2,1,0:T(8,128)(2,1)S(1)} %fusion.11), channel_id=1, source_target_pairs={{0,2},{1,3},{2,0},{3,1},{4,6},{5,7},{6,4},{7,5},{8,10},{9,11},{10,... | collective-permute-start | bytes 3145736 | tf_op jit(solution)/shard_map/ppermute | solution.py:250
  913.5 25.4 %collective-permute-start.49 = (bf16[8,128,512]{2,1,0:T(8,128)(2,1)S(1)}, bf16[8,128,512]{2,1,0:T(8,128)(2,1)}, u32[]{:S(2)}, u32[]{:S(2)}) collective-permute-start(bf16[8,128,512]{2,1,0:T(8,128)(2,1)S(1)} %fusion.12), channel_id=1, source_target_pairs={{0,2},{1,3},{2,0},{3,1},{4,6},{5,7},{6,4},{7,5},{8,10},{9,11},{10,... | collective-permute-start | bytes 3145736 | tf_op jit(solution)/shard_map/ppermute | solution.py:250
  (98 other events, 475.8 us)

commit v2 on v1

--- a/solution.py
+++ b/solution.py
@@ -9,7 +9,7 @@
 BOTH = ("seq", "chan")
 BF = jnp.bfloat16
 F32 = jnp.float32
-VMEM_BYTES = 56 * 1024 * 1024
+VMEM_BYTES = 60 * 1024 * 1024
 
 
 def dot(left, right, left_dim, right_dim):
@@ -58,8 +58,8 @@
     out_specs, out_shape, aliases = [], [], {}
     for k, out in enumerate(outs):
         if out == "pairs":
-            out_specs.append(pl.BlockSpec((2, step, rows, BS), lambda a, o: (0, a, 0, 0)))
-            out_shape.append(jax.ShapeDtypeStruct((2, count, rows, BS), BF))
+            out_specs.append(blocks(0, rows, BS))
+            out_shape.append(jax.ShapeDtypeStruct((count, rows, BS), BF))
             continue
         shape, first, earlier = out
         out_specs.append(
@@ -127,7 +127,7 @@
 
 
 def query_body(order, b, w0, w1, w2, w3, arrived, cot, query, *rest):
-    grad_query, keep, send = rest[-3:]
+    grad_query, *sums = rest[-5:]
     rows = w0.shape[1]
     weight = jnp.concatenate([w[b] for w in (w0, w1, w2, w3)], axis=0)
     three = rows_in(arrived, order, b)
@@ -138,17 +138,17 @@
         here = slice(k * rows, (k + 1) * rows)
         gate = rows_in(cot, order, b, k).astype(F32)
         grad_query[b, rows_of(order, k, rows), :] = (gate * mixed[here]).astype(BF)
-        (send if k >= 2 else keep)[k % 2, b] = pairs[here]
+        sums[k][b] = pairs[here]
 
 
 def key_body(order, b, w0, w1, w2, w3, arrived, key, value, *rest):
-    grad_key, grad_value, keep, send = rest[-4:]
+    grad_key, grad_value, *sums = rest[-6:]
     rows = w0.shape[1]
     weight = jnp.concatenate([w[b] for w in (w0, w1, w2, w3)], axis=0)
     grad_one = stacked(lambda k: rows_in(arrived, order, b, k))
     pairs = dot(grad_one, times(key[b], value[b]), 1, 1).astype(BF)
     for k in range(4):
-        (send if k >= 2 else keep)[k % 2, b] = pairs[k * rows : (k + 1) * rows]
+        sums[k][b] = pairs[k * rows : (k + 1) * rows]
     grad_kv = dot(weight, grad_one, 0, 0)
     grad_key[b] = (grad_kv * value[b].astype(F32)).astype(BF)
     grad_value[b] = (grad_kv * key[b].astype(F32)).astype(BF)
@@ -313,14 +313,13 @@
             return shaped
         return jnp.transpose(shaped, (1, 0, 2, 3)).reshape(-1, BS, width)
 
-    def near_sum(keep, send):
-        got = near(send)
-        passed = (keep[1].astype(F32) + got[1].astype(F32)).astype(BF)
-        return (keep, got), passed
+    def near_sum(keep, keep_far, send, send_far):
+        passed = (keep_far.astype(F32) + near(send_far).astype(F32)).astype(BF)
+        return (keep, near(send)), passed
 
     def far_sum(mine, got):
         keep, near_got = mine
-        return (keep[0].astype(F32) + near_got[0].astype(F32) + got.astype(F32)).astype(BF)
+        return (keep.astype(F32) + near_got.astype(F32) + got.astype(F32)).astype(BF)
 
     def far_sums(mine, got):
         return [far_sum((mine[2 * k], mine[2 * k + 1]), g) for k, g in enumerate(got)]
@@ -340,20 +339,20 @@
     def make_query(start, shift, count, shard, arrived, first, earlier):
         return token_call(
             query_body, order, shard, start, shift, count, (arrived, first), [cot, query],
-            [((local, BS, width), start, e) for e in earlier] + ["pairs", "pairs"], 4,
+            [((local, BS, width), start, e) for e in earlier] + ["pairs"] * 4, 4,
         )
 
     def make_key(start, shift, count, shard, arrived, first, earlier):
         return token_call(
             key_body, order, shard, start, shift, count, (arrived, first), [key, value],
-            [((local, BS, width), start, e) for e in earlier] + ["pairs", "pairs"], 4,
+            [((local, BS, width), start, e) for e in earlier] + ["pairs"] * 4, 4,
         )
 
     def steps(make, start, pieces, arrived, earlier):
         mine, got = [], []
         for at, count, shard, shift in pieces:
-            *earlier, keep, give = make(start + at, shift, count, shard, arrived, at, earlier)
-            near_mine, passed = near_sum(keep, give)
+            *earlier, a, b, c, d = make(start + at, shift, count, shard, arrived, at, earlier)
+            near_mine, passed = near_sum(a, b, c, d)
             mine += near_mine
             got.append(far(passed))
         return earlier, mine, got
@@ -457,10 +456,10 @@
     arrived = receive_out(back_a)
     grad_query, c_mine, c_pass = None, [], []
     for k in (1, 2, 3):
-        grad_query, keep, give = make_query(
+        grad_query, *pairs = make_query(
             k * unit, 0, unit, c_shards[k], arrived, (k - 1) * unit, [grad_query]
         )
-        mine, passed = near_sum(keep, give)
+        mine, passed = near_sum(*pairs)
         c_mine += mine
         c_pass.append(passed)
     c_got = [far(p) for p in c_pass[:2]]
@@ -489,38 +488,48 @@
     pieces = [(0, unit, c_shards[0], 0)]
     grad_query, mine, got = steps(make_query, 0, pieces, receive_out(back_b), [grad_query])
     c_sums = far_sums(c_mine, c_got)
-    (recv, send), (grad_query,), mine, got, c_sums = joined(
-        [recv, send_out(outs[0])], grad_query, mine, got, c_sums
-    )
-    later = exchange(send)
+    merged = [jnp.concatenate(p, axis=0) for p in zip(*[s[2][1:] for s in b_pieces[1]])]
+    (recv, *sends), (grad_query,), mine, got, c_sums, merged = joined(
+        [recv, *[send_out(out) for out in outs]], grad_query, mine, got, c_sums, merged
+    )
+    b_pieces[1] = [(0, unit, [factor_b1, *merged], 0)]
+    later = exchange(sends[0])
 
     c_sums = far_sums(mine, got) + c_sums
     grads, sums = [None, None], []
     for k in range(3):
         grads, mine, got = steps(make_key, k * unit, b_pieces[k], receive_out(recv), grads)
-        if k < 2:
-            (recv, send), grads, mine, got, sums, c_sums = joined(
-                [later, send_out(outs[k + 1])], grads, mine, got, sums, c_sums
-            )
-            later = exchange(send)
-        else:
-            grad_c1 = jnp.concatenate(c_sums, axis=0)
+        if k == 0:
             grad_b2 = jnp.swapaxes(unspread(grad_b2, b_spans), 1, 2)
             grad_c2 = unspread(grad_c2, c_spans)
-            sums = [jnp.concatenate(sums, axis=0)]
-            (recv, grad_b2, grad_c2, grad_c1), grads, mine, got, sums = joined(
-                [later, grad_b2, grad_c2, grad_c1], grads, mine, got, sums
+            (later, send, grad_b2, grad_c2), grads, mine, got = joined(
+                [later, sends[1], grad_b2, grad_c2], grads, mine, got
             )
+        elif k == 1:
+            grad_c1 = jnp.concatenate(c_sums, axis=0)
+            (later, send, grad_c1), grads, mine, got, sums = joined(
+                [later, sends[2], grad_c1], grads, mine, got, sums
+            )
+        else:
+            rest = jnp.zeros((local - 2 * unit, *factor_b1.shape[1:]), BF)
+            grad_b1 = jnp.concatenate([*sums, rest], axis=0)
+            (later, grad_b1), grads, mine, got = joined([later, grad_b1], grads, mine, got)
+        recv = later
+        if k < 2:
+            later = exchange(send)
         sums += far_sums(mine, got)
+    grad_b1 = lax.dynamic_update_slice(
+        grad_b1, jnp.concatenate(sums[-len(got) :], axis=0), (2 * unit, 0, 0)
+    )
     grads, mine, got = steps(make_key, 3 * unit, b_pieces[3], receive_out(recv), grads)
-    sums += far_sums(mine, got)
+    grad_b1 = lax.dynamic_update_slice(grad_b1, far_sums(mine, got)[0], (3 * unit, 0, 0))
 
     return (
         grad_query.reshape(query_in.shape),
         grads[0].reshape(query_in.shape),
         grads[1].reshape(query_in.shape),
         grad_freq,
-        jnp.concatenate(sums, axis=0),
+        grad_b1,
         grad_b2,
         grad_c2,
         grad_c1,

time: 953 us -> 946 us (level)
    convert_element_type x20 -> x16, other arithmetic: 24.3 us -> 16.8 us  [the longest x7 10.7 us: far_sum(): (keep.astype(F32) + near_got.astype(F32) + got.astype(F32)).astype(BF)]
    unnamed x170 -> x136, local copies, waits for them, and re-layouts: 28.7 us -> 22 us
    pallas_call x20 -> x19, Pallas kernels: 123 us -> 118 us  [token_call(): pl.pallas_call(body, grid_spec=pltpu.PrefetchScalarGridSpec(num_scalar_pr...]
    ppermute x50 -> x57, waiting for transfers between devices: 472 us -> 469 us  [swap(): lax.ppermute(tensor, 'chan', [(m, m ^ distance) for m in range(chan_count)])]
    ppermute x50 -> x57, starting transfers between devices: 44.7 us -> 45 us  [swap(): lax.ppermute(tensor, 'chan', [(m, m ^ distance) for m in range(chan_count)])]
  transfers between devices with their start and end apart: 62 -> 69, of which waited for: 36 -> 41; matrix products, arithmetic and copies ran while one was open for 10% -> 11% of each run, Pallas kernels for 16% -> 16%
where the time goes in v2:
time: 946 us; the launch traced here: 936 us
  waiting for transfers between devices  543 us (57%)
  Pallas kernels  157 us (17%)
  starting transfers between devices  108 us (11%)
  local copies, waits for them, and re-layouts  85.7 us (9%)
  other arithmetic  39.3 us (4%)
    ppermute x57, waiting for transfers between devices, swap(): lax.ppermute(tensor, 'chan', [(m, m ^ distance) for m in range(chan_count)])  469 us
    pallas_call x19, Pallas kernels, token_call(): pl.pallas_call(body, grid_spec=pltpu.PrefetchScalarGridSpec(num_scalar_pr...  118 us
    all_to_all x12, waiting for transfers between devices, exchange(): return lax.all_to_all(tensor, BOTH, split_axis=0, concat_axis=0, tiled=True)  74.3 us
    all_to_all x12, starting transfers between devices, exchange(): return lax.all_to_all(tensor, BOTH, split_axis=0, concat_axis=0, tiled=True)  63.4 us
    ppermute x57, starting transfers between devices, swap(): lax.ppermute(tensor, 'chan', [(m, m ^ distance) for m in range(chan_count)])  45 us
    pallas_call x2, Pallas kernels, freq_call(): pl.pallas_call(body, grid=(count // step,), in_specs=[spec(x) for x in in...  39.7 us
    reshape x6, local copies, waits for them, and re-layouts, send_out(): shaped = tensor.reshape(rows, chan_count, seq_count, -1, width)  27.4 us
    unnamed x136, local copies, waits for them, and re-layouts  22 us
  transfers between devices with their start and end apart: 69, of which 41 were waited for; matrix products, arithmetic and copies ran while one was open for 11% of the time, Pallas kernels for 16%

profile of v2, /device:TPU:0, one launch (start us, length us, event | category | flops | bytes accessed | tf_op | source)
XLA Modules:
  0.0 935.8 jit_solution(17159682625279716608)
XLA Ops:
  12.4 5.2 collective-permute-done.refs_1_
  26.3 6.8 collective-permute-done.3.refs_1_
  44.9 8.6 collective-permute-done.6.refs_1_
  53.5 6.1 all-to-all-start
  63.2 5.9 shard_map.154.refs_6_
  69.1 13.3 %collective-permute-done.9.refs_1_ = bf16[2,128,512]{2,1,0:T(8,128)(2,1)S(1)} collective-permute-done((bf16[2,128,512]{2,1,0:T(8,128)(2,1)S(1)}, bf16[2,128,512]{2,1,0:T(8,128)(2,1)S(1)}, u32[]{:S(2)}, u32[]{:S(2)}) %collective-permute-start.9) | collective-permute-done | bytes 262176 | tf_op jit(solution)/shard_map/ppermute | solution.py:250
  94.7 18.7 %collective-permute-done.12.refs_1_ = bf16[8,128,512]{2,1,0:T(8,128)(2,1)} collective-permute-done((bf16[8,128,512]{2,1,0:T(8,128)(2,1)}, bf16[8,128,512]{2,1,0:T(8,128)(2,1)}, u32[]{:S(2)}, u32[]{:S(2)}) %collective-permute-start.12) | collective-permute-done | bytes 1048608 | tf_op jit(solution)/shard_map/ppermute | solution.py:250
  113.5 8.7 all-to-all-start.1
  128.8 5.9 shard_map.156
  134.7 35.2 %collective-permute-done.15.refs_1_ = bf16[8,128,512]{2,1,0:T(8,128)(2,1)S(1)} collective-permute-done((bf16[8,128,512]{2,1,0:T(8,128)(2,1)}, bf16[8,128,512]{2,1,0:T(8,128)(2,1)S(1)}, u32[]{:S(2)}, u32[]{:S(2)}) %collective-permute-start.15) | collective-permute-done | bytes 1048608 | tf_op jit(solution)/shard_map/ppermute | solution.py:250
  185.3 5.9 shard_map.157
  191.2 32.6 %collective-permute-done.18.refs_1_ = bf16[8,128,512]{2,1,0:T(8,128)(2,1)} collective-permute-done((bf16[8,128,512]{2,1,0:T(8,128)(2,1)}, bf16[8,128,512]{2,1,0:T(8,128)(2,1)}, u32[]{:S(2)}, u32[]{:S(2)}) %collective-permute-start.18) | collective-permute-done | bytes 1048608 | tf_op jit(solution)/shard_map/ppermute | solution.py:250
  233.4 5.9 shard_map.158
  239.4 36.6 %collective-permute-done.21.refs_1_ = bf16[8,128,512]{2,1,0:T(8,128)(2,1)} collective-permute-done((bf16[8,128,512]{2,1,0:T(8,128)(2,1)}, bf16[8,128,512]{2,1,0:T(8,128)(2,1)}, u32[]{:S(2)}, u32[]{:S(2)}) %collective-permute-start.21) | collective-permute-done | bytes 1048608 | tf_op jit(solution)/shard_map/ppermute | solution.py:250
  286.9 16.3 %shard_map.159 = (bf16[16,256,1024]{2,1,0:T(8,128)(2,1)}, bf16[16,4,64,256]{3,2,1,0:T(8,128)(2,1)}, bf16[16,4,192,256]{3,2,1,0:T(8,128)(2,1)}) custom-call(bf16[16,256,256]{2,1,0:T(8,128)(2,1)} %get-tuple-element.206.refs_0_, bf16[16,256,256]{2,1,0:T(8,128)(2,1)} %get-tuple-element.207.refs_1_, bf16[16,256,1024]{2,1,0:T(8,128)(2,1)} %refs_2_.3, ...), custom_call_target="tpu_custom_call" | custom-call | flops 4294967296 | bytes 37748736 | tf_op jit(solution)/shard_map/pallas_call | solution.py:170
  303.2 10.6 %copy.42 = bf16[16,4,8,24,256]{4,0,3,1,2:T(8,128)(2,1)} copy(bf16[16,4,8,24,256]{4,3,2,1,0:T(8,128)(2,1)} %bitcast.206) | data formatting | bytes 12582912 | tf_op jit(solution)/shard_map/reshape | solution.py:307
  313.8 15.2 %collective-permute-done.22.refs_1_ = bf16[8,128,512]{2,1,0:T(8,128)(2,1)S(1)} collective-permute-done((bf16[8,128,512]{2,1,0:T(8,128)(2,1)}, bf16[8,128,512]{2,1,0:T(8,128)(2,1)S(1)}, u32[]{:S(2)}, u32[]{:S(2)}) %collective-permute-start.22) | collective-permute-done | bytes 1048608 | tf_op jit(solution)/shard_map/ppermute | solution.py:250
  338.1 78.8 %collective-permute-done.23.refs_1_ = bf16[8,128,512]{2,1,0:T(8,128)(2,1)} collective-permute-done((bf16[8,128,512]{2,1,0:T(8,128)(2,1)}, bf16[8,128,512]{2,1,0:T(8,128)(2,1)}, u32[]{:S(2)}, u32[]{:S(2)}) %collective-permute-start.23) | collective-permute-done | bytes 1048608 | tf_op jit(solution)/shard_map/ppermute | solution.py:250
  416.9 5.8 shard_map.160.refs_6_
  427.9 5.8 shard_map.161.refs_6_
  433.8 5.9 shard_map.162
  439.6 35.1 %all-to-all-done.5 = bf16[32,384,256]{2,1,0:T(8,128)(2,1)} async-done(((bf16[32,384,256]{2,1,0:T(8,128)(2,1)}), bf16[32,384,256]{2,1,0:T(8,128)(2,1)}, u32[]{:S(2)}, u32[]{:S(2)}) %all-to-all-start.5) | async-done | bytes 6291488 | tf_op jit(solution)/shard_map/all_to_all | solution.py:242
  474.7 5.7 all-to-all-start.6
  480.4 7.6 shard_map.163
  488.0 7.6 shard_map.164
  496.1 7.7 shard_map.165
  511.2 51.6 %collective-permute-done.37 = bf16[8,128,512]{2,1,0:T(8,128)(2,1)S(1)} collective-permute-done((bf16[8,128,512]{2,1,0:T(8,128)(2,1)S(1)}, bf16[8,128,512]{2,1,0:T(8,128)(2,1)S(1)}, u32[]{:S(2)}, u32[]{:S(2)}) %collective-permute-start.37) | collective-permute-done | bytes 1048608 | tf_op jit(solution)/shard_map/ppermute | solution.py:250
  563.9 21.8 %collective-permute-done.35 = bf16[8,128,512]{2,1,0:T(8,128)(2,1)} collective-permute-done((bf16[8,128,512]{2,1,0:T(8,128)(2,1)S(1)}, bf16[8,128,512]{2,1,0:T(8,128)(2,1)}, u32[]{:S(2)}, u32[]{:S(2)}) %collective-permute-start.35) | collective-permute-done | bytes 1048608 | tf_op jit(solution)/shard_map/ppermute | solution.py:250
  585.7 34.8 %all-to-all-done.6 = bf16[32,384,256]{2,1,0:T(8,128)(2,1)} async-done(((bf16[32,384,256]{2,1,0:T(8,128)(2,1)}), bf16[32,384,256]{2,1,0:T(8,128)(2,1)}, u32[]{:S(2)}, u32[]{:S(2)}) %all-to-all-start.6) | async-done | bytes 6291488 | tf_op jit(solution)/shard_map/all_to_all | solution.py:242
  620.5 5.7 all-to-all-start.7
  628.1 7.7 copy.45
  635.9 23.4 %shard_map.166 = (bf16[16,256,1024]{2,1,0:T(8,128)(2,1)}, bf16[16,256,256]{2,1,0:T(8,128)(2,1)}, bf16[16,256,256]{2,1,0:T(8,128)(2,1)}, bf16[16,4,64,256]{3,2,1,...) custom-call(bf16[16,256,256]{2,1,0:T(8,128)(2,1)} %get-tuple-element, ...), custom_call_target="tpu_custom_call" | custom-call | flops 10737418240 | bytes 58720256 | tf_op jit(solution)/shard_map/pallas_call | solution.py:170
  663.9 10.2 %collective-permute-done.38 = bf16[8,128,512]{2,1,0:T(8,128)(2,1)} collective-permute-done((bf16[8,128,512]{2,1,0:T(8,128)(2,1)S(1)}, bf16[8,128,512]{2,1,0:T(8,128)(2,1)}, u32[]{:S(2)}, u32[]{:S(2)}) %collective-permute-start.38) | collective-permute-done | bytes 1048608 | tf_op jit(solution)/shard_map/ppermute | solution.py:250
  680.4 7.7 shard_map.167
  713.6 15.5 %collective-permute-done.41 = bf16[8,128,512]{2,1,0:T(8,128)(2,1)} collective-permute-done((bf16[8,128,512]{2,1,0:T(8,128)(2,1)S(1)}, bf16[8,128,512]{2,1,0:T(8,128)(2,1)}, u32[]{:S(2)}, u32[]{:S(2)}) %collective-permute-start.41) | collective-permute-done | bytes 1048608 | tf_op jit(solution)/shard_map/ppermute | solution.py:250
  730.5 5.4 all-to-all-start.9
  735.9 5.2 shard_map.168
  741.1 5.3 shard_map.169
  755.6 14.7 %collective-permute-done.47 = bf16[4,128,512]{2,1,0:T(8,128)(2,1)S(1)} collective-permute-done((bf16[4,128,512]{2,1,0:T(8,128)(2,1)S(1)}, bf16[4,128,512]{2,1,0:T(8,128)(2,1)S(1)}, u32[]{:S(2)}, u32[]{:S(2)}) %collective-permute-start.47) | collective-permute-done | bytes 524320 | tf_op jit(solution)/shard_map/ppermute | solution.py:250
  771.1 13.7 %collective-permute-done.45 = bf16[4,128,512]{2,1,0:T(8,128)(2,1)} collective-permute-done((bf16[4,128,512]{2,1,0:T(8,128)(2,1)S(1)}, bf16[4,128,512]{2,1,0:T(8,128)(2,1)}, u32[]{:S(2)}, u32[]{:S(2)}) %collective-permute-start.45) | collective-permute-done | bytes 524320 | tf_op jit(solution)/shard_map/ppermute | solution.py:250
  784.8 4.9 all-to-all-start.10
  789.7 7.9 shard_map.170
  811.4 26.9 %collective-permute-done.50 = bf16[8,128,512]{2,1,0:T(8,128)(2,1)} collective-permute-done((bf16[8,128,512]{2,1,0:T(8,128)(2,1)S(1)}, bf16[8,128,512]{2,1,0:T(8,128)(2,1)}, u32[]{:S(2)}, u32[]{:S(2)}) %collective-permute-start.50) | collective-permute-done | bytes 1048608 | tf_op jit(solution)/shard_map/ppermute | solution.py:250
  839.7 5.5 all-to-all-start.11
  845.2 7.9 shard_map.171
  863.5 30.4 %collective-permute-done.53 = bf16[8,128,512]{2,1,0:T(8,128)(2,1)} collective-permute-done((bf16[8,128,512]{2,1,0:T(8,128)(2,1)S(1)}, bf16[8,128,512]{2,1,0:T(8,128)(2,1)}, u32[]{:S(2)}, u32[]{:S(2)}) %collective-permute-start.53) | collective-permute-done | bytes 1048608 | tf_op jit(solution)/shard_map/ppermute | solution.py:250
  893.9 7.9 shard_map.172
  914.3 18.1 %collective-permute-done.56 = bf16[8,128,512]{2,1,0:T(8,128)(2,1)} collective-permute-done((bf16[8,128,512]{2,1,0:T(8,128)(2,1)S(1)}, bf16[8,128,512]{2,1,0:T(8,128)(2,1)}, u32[]{:S(2)}, u32[]{:S(2)}) %collective-permute-start.56) | collective-permute-done | bytes 1048608 | tf_op jit(solution)/shard_map/ppermute | solution.py:250
  (301 shorter events, 204.3 us)
Async XLA Ops:
  2.5 15.1 %collective-permute-start = (bf16[4,128,512]{2,1,0:T(8,128)(2,1)}, bf16[4,128,512]{2,1,0:T(8,128)(2,1)S(1)}, u32[]{:S(2)}, u32[]{:S(2)}) collective-permute-start(bf16[4,128,512]{2,1,0:T(8,128)(2,1)} %slice.66), channel_id=1, source_target_pairs={{0,2},{1,3},{2,0},{3,1},{4,6},{5,7},{6,4},{7,5},{8,10},{9,11},{10,... | collective-permute-start | bytes 1572872 | tf_op jit(solution)/shard_map/ppermute | solution.py:250
  5.5 15.8 %collective-permute-start.1 = (bf16[4,128,512]{2,1,0:T(8,128)(2,1)}, bf16[4,128,512]{2,1,0:T(8,128)(2,1)S(1)}, u32[]{:S(2)}, u32[]{:S(2)}) collective-permute-start(bf16[4,128,512]{2,1,0:T(8,128)(2,1)} %slice.66), channel_id=1, source_target_pairs={{0,1},{1,0},{2,3},{3,2},{4,5},{5,4},{6,7},{7,6},{8,9},{9,8},{10,11... | collective-permute-start | bytes 1572872 | tf_op jit(solution)/shard_map/ppermute | solution.py:250
  18.9 14.2 %collective-permute-start.3 = (bf16[4,128,512]{2,1,0:T(8,128)(2,1)S(1)}, bf16[4,128,512]{2,1,0:T(8,128)(2,1)S(1)}, u32[]{:S(2)}, u32[]{:S(2)}) collective-permute-start(bf16[4,128,512]{2,1,0:T(8,128)(2,1)S(1)} %slice.73), channel_id=1, source_target_pairs={{0,2},{1,3},{2,0},{3,1},{4,6},{5,7},{6,4},{7,5},{8,10},{9,11},{10,... | collective-permute-start | bytes 1572872 | tf_op jit(solution)/shard_map/ppermute | solution.py:250
  34.5 19.0 %collective-permute-start.6 = (bf16[6,128,512]{2,1,0:T(8,128)(2,1)S(1)}, bf16[6,128,512]{2,1,0:T(8,128)(2,1)S(1)}, u32[]{:S(2)}, u32[]{:S(2)}) collective-permute-start(bf16[6,128,512]{2,1,0:T(8,128)(2,1)S(1)} %slice.74), channel_id=1, source_target_pairs={{0,2},{1,3},{2,0},{3,1},{4,6},{5,7},{6,4},{7,5},{8,10},{9,11},{10,... | collective-permute-start | bytes 2359304 | tf_op jit(solution)/shard_map/ppermute | solution.py:250
  53.5 60.0 %all-to-all-start = ((bf16[32,128,256]{2,1,0:T(8,128)(2,1)}), bf16[32,128,256]{2,1,0:T(8,128)(2,1)S(1)}, u32[]{:S(2)}, u32[]{:S(2)}) async-start(bf16[32,128,256]{2,1,0:T(8,128)(2,1)} %bitcast.180), calls=%async_computation | async-start | bytes 4194304 | tf_op jit(solution)/shard_map/all_to_all | solution.py:242
  61.1 21.2 %collective-permute-start.9 = (bf16[2,128,512]{2,1,0:T(8,128)(2,1)S(1)}, bf16[2,128,512]{2,1,0:T(8,128)(2,1)S(1)}, u32[]{:S(2)}, u32[]{:S(2)}) collective-permute-start(bf16[2,128,512]{2,1,0:T(8,128)(2,1)S(1)} %slice.75), channel_id=1, source_target_pairs={{0,2},{1,3},{2,0},{3,1},{4,6},{5,7},{6,4},{7,5},{8,10},{9,11},{10,... | collective-permute-start | bytes 786440 | tf_op jit(solution)/shard_map/ppermute | solution.py:250
  84.7 28.8 %collective-permute-start.12 = (bf16[8,128,512]{2,1,0:T(8,128)(2,1)}, bf16[8,128,512]{2,1,0:T(8,128)(2,1)}, u32[]{:S(2)}, u32[]{:S(2)}) collective-permute-start(bf16[8,128,512]{2,1,0:T(8,128)(2,1)} %slice.76), channel_id=1, source_target_pairs={{0,2},{1,3},{2,0},{3,1},{4,6},{5,7},{6,4},{7,5},{8,10},{9,11},{10,... | collective-permute-start | bytes 3145736 | tf_op jit(solution)/shard_map/ppermute | solution.py:250
  113.5 57.5 %all-to-all-start.1 = ((bf16[32,128,256]{2,1,0:T(8,128)(2,1)}), bf16[32,128,256]{2,1,0:T(8,128)(2,1)}, u32[]{:S(2)}, u32[]{:S(2)}) async-start(bf16[32,128,256]{2,1,0:T(8,128)(2,1)} %bitcast.181), calls=%async_computation.1 | async-start | bytes 4194304 | tf_op jit(solution)/shard_map/all_to_all | solution.py:242
  122.2 6.6 collective-permute-start.13
  122.5 6.3 collective-permute-start.14
  125.1 44.8 %collective-permute-start.15 = (bf16[8,128,512]{2,1,0:T(8,128)(2,1)}, bf16[8,128,512]{2,1,0:T(8,128)(2,1)S(1)}, u32[]{:S(2)}, u32[]{:S(2)}) collective-permute-start(bf16[8,128,512]{2,1,0:T(8,128)(2,1)} %slice.77), channel_id=1, source_target_pairs={{0,2},{1,3},{2,0},{3,1},{4,6},{5,7},{6,4},{7,5},{8,10},{9,11},{10,... | collective-permute-start | bytes 3145736 | tf_op jit(solution)/shard_map/ppermute | solution.py:250
  171.0 52.9 %all-to-all-start.2 = ((bf16[32,128,256]{2,1,0:T(8,128)(2,1)}), bf16[32,128,256]{2,1,0:T(8,128)(2,1)S(1)}, u32[]{:S(2)}, u32[]{:S(2)}) async-start(bf16[32,128,256]{2,1,0:T(8,128)(2,1)} %bitcast.192), calls=%async_computation.2 | async-start | bytes 4194304 | tf_op jit(solution)/shard_map/all_to_all | solution.py:242
  179.9 43.8 %collective-permute-start.18 = (bf16[8,128,512]{2,1,0:T(8,128)(2,1)}, bf16[8,128,512]{2,1,0:T(8,128)(2,1)}, u32[]{:S(2)}, u32[]{:S(2)}) collective-permute-start(bf16[8,128,512]{2,1,0:T(8,128)(2,1)} %get-tuple-element.363), channel_id=1, source_target_pairs={{0,2},{1,3},{2,0},{3,1},{4,6},{5,7},{6,4},{7,5},{8,10},{9,11},{10,... | collective-permute-start | bytes 3145736 | tf_op jit(solution)/shard_map/ppermute | solution.py:250
  223.9 53.0 %all-to-all-start.3 = ((bf16[32,128,256]{2,1,0:T(8,128)(2,1)}), bf16[32,128,256]{2,1,0:T(8,128)(2,1)}, u32[]{:S(2)}, u32[]{:S(2)}) async-start(bf16[32,128,256]{2,1,0:T(8,128)(2,1)} %bitcast.193), calls=%async_computation.3 | async-start | bytes 4194304 | tf_op jit(solution)/shard_map/all_to_all | solution.py:242
  228.7 47.2 %collective-permute-start.21 = (bf16[8,128,512]{2,1,0:T(8,128)(2,1)}, bf16[8,128,512]{2,1,0:T(8,128)(2,1)}, u32[]{:S(2)}, u32[]{:S(2)}) collective-permute-start(bf16[8,128,512]{2,1,0:T(8,128)(2,1)} %get-tuple-element.362), channel_id=1, source_target_pairs={{0,2},{1,3},{2,0},{3,1},{4,6},{5,7},{6,4},{7,5},{8,10},{9,11},{10,... | collective-permute-start | bytes 3145736 | tf_op jit(solution)/shard_map/ppermute | solution.py:250
  276.9 53.1 %all-to-all-start.4 = ((bf16[32,128,256]{2,1,0:T(8,128)(2,1)}), bf16[32,128,256]{2,1,0:T(8,128)(2,1)S(1)}, u32[]{:S(2)}, u32[]{:S(2)}) async-start(bf16[32,128,256]{2,1,0:T(8,128)(2,1)} %bitcast.194), calls=%async_computation.4 | async-start | bytes 4194304 | tf_op jit(solution)/shard_map/all_to_all | solution.py:242
  281.3 47.8 %collective-permute-start.22 = (bf16[8,128,512]{2,1,0:T(8,128)(2,1)}, bf16[8,128,512]{2,1,0:T(8,128)(2,1)S(1)}, u32[]{:S(2)}, u32[]{:S(2)}) collective-permute-start(bf16[8,128,512]{2,1,0:T(8,128)(2,1)} %get-tuple-element.361), channel_id=1, source_target_pairs={{0,2},{1,3},{2,0},{3,1},{4,6},{5,7},{6,4},{7,5},{8,10},{9,11},{10,... | collective-permute-start | bytes 3145736 | tf_op jit(solution)/shard_map/ppermute | solution.py:250
  330.0 144.7 %all-to-all-start.5 = ((bf16[32,384,256]{2,1,0:T(8,128)(2,1)}), bf16[32,384,256]{2,1,0:T(8,128)(2,1)}, u32[]{:S(2)}, u32[]{:S(2)}) async-start(bf16[32,384,256]{2,1,0:T(8,128)(2,1)} %bitcast.177), calls=%async_computation.5 | async-start | bytes 12582912 | tf_op jit(solution)/shard_map/all_to_all | solution.py:242
  335.1 81.8 %collective-permute-start.23 = (bf16[8,128,512]{2,1,0:T(8,128)(2,1)}, bf16[8,128,512]{2,1,0:T(8,128)(2,1)}, u32[]{:S(2)}, u32[]{:S(2)}) collective-permute-start(bf16[8,128,512]{2,1,0:T(8,128)(2,1)} %get-tuple-element.360), channel_id=1, source_target_pairs={{0,2},{1,3},{2,0},{3,1},{4,6},{5,7},{6,4},{7,5},{8,10},{9,11},{10,... | collective-permute-start | bytes 3145736 | tf_op jit(solution)/shard_map/ppermute | solution.py:250
  336.8 80.1 %collective-permute-start.29 = (bf16[8,128,512]{2,1,0:T(8,128)(2,1)}, bf16[8,128,512]{2,1,0:T(8,128)(2,1)}, u32[]{:S(2)}, u32[]{:S(2)}) collective-permute-start(bf16[8,128,512]{2,1,0:T(8,128)(2,1)} %collective-permute-done.21.refs_1_), channel_id=1, source_target_pairs={{0,1},{1,0},{2,3},{3,2},{4,5},{5,4},{6,7},{7,6},{8,9},{9,8},{10,11... | collective-permute-start | bytes 3145736 | tf_op jit(solution)/shard_map/ppermute | solution.py:250
  336.9 91.0 %collective-permute-start.26 = (bf16[8,128,512]{2,1,0:T(8,128)(2,1)}, bf16[8,128,512]{2,1,0:T(8,128)(2,1)}, u32[]{:S(2)}, u32[]{:S(2)}) collective-permute-start(bf16[8,128,512]{2,1,0:T(8,128)(2,1)} %get-tuple-element.361), channel_id=1, source_target_pairs={{0,1},{1,0},{2,3},{3,2},{4,5},{5,4},{6,7},{7,6},{8,9},{9,8},{10,11... | collective-permute-start | bytes 3145736 | tf_op jit(solution)/shard_map/ppermute | solution.py:250
  337.3 90.6 %collective-permute-start.27 = (bf16[8,128,512]{2,1,0:T(8,128)(2,1)S(1)}, bf16[8,128,512]{2,1,0:T(8,128)(2,1)}, u32[]{:S(2)}, u32[]{:S(2)}) collective-permute-start(bf16[8,128,512]{2,1,0:T(8,128)(2,1)S(1)} %collective-permute-done.22.refs_1_), channel_id=1, source_target_pairs={{0,1},{1,0},{2,3},{3,2},{4,5},{5,4},{6,7},{7,6},{8,9},{9,8},{10,11... | collective-permute-start | bytes 3145736 | tf_op jit(solution)/shard_map/ppermute | solution.py:250
  337.7 96.0 %collective-permute-start.24 = (bf16[8,128,512]{2,1,0:T(8,128)(2,1)}, bf16[8,128,512]{2,1,0:T(8,128)(2,1)}, u32[]{:S(2)}, u32[]{:S(2)}) collective-permute-start(bf16[8,128,512]{2,1,0:T(8,128)(2,1)} %get-tuple-element.360), channel_id=1, source_target_pairs={{0,1},{1,0},{2,3},{3,2},{4,5},{5,4},{6,7},{7,6},{8,9},{9,8},{10,11... | collective-permute-start | bytes 3145736 | tf_op jit(solution)/shard_map/ppermute | solution.py:250
  416.9 16.8 %collective-permute-start.25 = (bf16[8,128,512]{2,1,0:T(8,128)(2,1)}, bf16[8,128,512]{2,1,0:T(8,128)(2,1)}, u32[]{:S(2)}, u32[]{:S(2)}) collective-permute-start(bf16[8,128,512]{2,1,0:T(8,128)(2,1)} %collective-permute-done.23.refs_1_), channel_id=1, source_target_pairs={{0,1},{1,0},{2,3},{3,2},{4,5},{5,4},{6,7},{7,6},{8,9},{9,8},{10,11... | collective-permute-start | bytes 3145736 | tf_op jit(solution)/shard_map/ppermute | solution.py:250
  474.7 145.8 %all-to-all-start.6 = ((bf16[32,384,256]{2,1,0:T(8,128)(2,1)}), bf16[32,384,256]{2,1,0:T(8,128)(2,1)}, u32[]{:S(2)}, u32[]{:S(2)}) async-start(bf16[32,384,256]{2,1,0:T(8,128)(2,1)} %bitcast.175), calls=%async_computation.6 | async-start | bytes 12582912 | tf_op jit(solution)/shard_map/all_to_all | solution.py:242
  495.6 9.0 collective-permute-start.36
  495.8 9.5 %collective-permute-start.34 = (bf16[8,128,512]{2,1,0:T(8,128)(2,1)}, bf16[8,128,512]{2,1,0:T(8,128)(2,1)S(1)}, u32[]{:S(2)}, u32[]{:S(2)}) collective-permute-start(bf16[8,128,512]{2,1,0:T(8,128)(2,1)} %get-tuple-element.235), channel_id=1, source_target_pairs={{0,1},{1,0},{2,3},{3,2},{4,5},{5,4},{6,7},{7,6},{8,9},{9,8},{10,11... | collective-permute-start | bytes 3145736 | tf_op jit(solution)/shard_map/ppermute | solution.py:250
  504.6 6.7 collective-permute-start.31
  505.2 57.7 %collective-permute-start.37 = (bf16[8,128,512]{2,1,0:T(8,128)(2,1)S(1)}, bf16[8,128,512]{2,1,0:T(8,128)(2,1)S(1)}, u32[]{:S(2)}, u32[]{:S(2)}) collective-permute-start(bf16[8,128,512]{2,1,0:T(8,128)(2,1)S(1)} %add_convert_fusion.11), channel_id=1, source_target_pairs={{0,2},{1,3},{2,0},{3,1},{4,6},{5,7},{6,4},{7,5},{8,10},{9,11},{10,... | collective-permute-start | bytes 3145736 | tf_op jit(solution)/shard_map/ppermute | solution.py:250
  507.3 78.4 %collective-permute-start.35 = (bf16[8,128,512]{2,1,0:T(8,128)(2,1)S(1)}, bf16[8,128,512]{2,1,0:T(8,128)(2,1)}, u32[]{:S(2)}, u32[]{:S(2)}) collective-permute-start(bf16[8,128,512]{2,1,0:T(8,128)(2,1)S(1)} %add_convert_fusion.12), channel_id=1, source_target_pairs={{0,2},{1,3},{2,0},{3,1},{4,6},{5,7},{6,4},{7,5},{8,10},{9,11},{10,... | collective-permute-start | bytes 3145736 | tf_op jit(solution)/shard_map/ppermute | solution.py:250
  620.5 54.4 %all-to-all-start.7 = ((bf16[32,128,256]{2,1,0:T(8,128)(2,1)}), bf16[32,128,256]{2,1,0:T(8,128)(2,1)S(1)}, u32[]{:S(2)}, u32[]{:S(2)}) async-start(bf16[32,128,256]{2,1,0:T(8,128)(2,1)} %bitcast.198), calls=%async_computation.7 | async-start | bytes 4194304 | tf_op jit(solution)/shard_map/all_to_all | solution.py:242
  626.2 47.9 %collective-permute-start.38 = (bf16[8,128,512]{2,1,0:T(8,128)(2,1)S(1)}, bf16[8,128,512]{2,1,0:T(8,128)(2,1)}, u32[]{:S(2)}, u32[]{:S(2)}) collective-permute-start(bf16[8,128,512]{2,1,0:T(8,128)(2,1)S(1)} %add_convert_fusion.13), channel_id=1, source_target_pairs={{0,2},{1,3},{2,0},{3,1},{4,6},{5,7},{6,4},{7,5},{8,10},{9,11},{10,... | collective-permute-start | bytes 3145736 | tf_op jit(solution)/shard_map/ppermute | solution.py:250
  676.3 52.9 %all-to-all-start.8 = ((bf16[32,128,256]{2,1,0:T(8,128)(2,1)}), bf16[32,128,256]{2,1,0:T(8,128)(2,1)S(1)}, u32[]{:S(2)}, u32[]{:S(2)}) async-start(bf16[32,128,256]{2,1,0:T(8,128)(2,1)} %bitcast.200), calls=%async_computation.8 | async-start | bytes 4194304 | tf_op jit(solution)/shard_map/all_to_all | solution.py:242
  692.0 20.6 %collective-permute-start.39 = (bf16[8,128,512]{2,1,0:T(8,128)(2,1)S(1)}, bf16[8,128,512]{2,1,0:T(8,128)(2,1)S(1)}, u32[]{:S(2)}, u32[]{:S(2)}) collective-permute-start(bf16[8,128,512]{2,1,0:T(8,128)(2,1)S(1)} %copy-done.64), channel_id=1, source_target_pairs={{0,1},{1,0},{2,3},{3,2},{4,5},{5,4},{6,7},{7,6},{8,9},{9,8},{10,11... | collective-permute-start | bytes 3145736 | tf_op jit(solution)/shard_map/ppermute | solution.py:250
  692.6 36.5 %collective-permute-start.41 = (bf16[8,128,512]{2,1,0:T(8,128)(2,1)S(1)}, bf16[8,128,512]{2,1,0:T(8,128)(2,1)}, u32[]{:S(2)}, u32[]{:S(2)}) collective-permute-start(bf16[8,128,512]{2,1,0:T(8,128)(2,1)S(1)} %add_convert_fusion.10), channel_id=1, source_target_pairs={{0,2},{1,3},{2,0},{3,1},{4,6},{5,7},{6,4},{7,5},{8,10},{9,11},{10,... | collective-permute-start | bytes 3145736 | tf_op jit(solution)/shard_map/ppermute | solution.py:250
  730.5 54.3 %all-to-all-start.9 = ((bf16[32,128,256]{2,1,0:T(8,128)(2,1)}), bf16[32,128,256]{2,1,0:T(8,128)(2,1)}, u32[]{:S(2)}, u32[]{:S(2)}) async-start(bf16[32,128,256]{2,1,0:T(8,128)(2,1)} %bitcast.199), calls=%async_computation.9 | async-start | bytes 4194304 | tf_op jit(solution)/shard_map/all_to_all | solution.py:242
  747.9 7.7 collective-permute-start.43
  748.0 7.5 collective-permute-start.42
  748.8 21.5 %collective-permute-start.47 = (bf16[4,128,512]{2,1,0:T(8,128)(2,1)S(1)}, bf16[4,128,512]{2,1,0:T(8,128)(2,1)S(1)}, u32[]{:S(2)}, u32[]{:S(2)}) collective-permute-start(bf16[4,128,512]{2,1,0:T(8,128)(2,1)S(1)} %add_convert_fusion.16), channel_id=1, source_target_pairs={{0,2},{1,3},{2,0},{3,1},{4,6},{5,7},{6,4},{7,5},{8,10},{9,11},{10,... | collective-permute-start | bytes 1572872 | tf_op jit(solution)/shard_map/ppermute | solution.py:250
  750.9 33.9 %collective-permute-start.45 = (bf16[4,128,512]{2,1,0:T(8,128)(2,1)S(1)}, bf16[4,128,512]{2,1,0:T(8,128)(2,1)}, u32[]{:S(2)}, u32[]{:S(2)}) collective-permute-start(bf16[4,128,512]{2,1,0:T(8,128)(2,1)S(1)} %add_convert_fusion.17), channel_id=1, source_target_pairs={{0,2},{1,3},{2,0},{3,1},{4,6},{5,7},{6,4},{7,5},{8,10},{9,11},{10,... | collective-permute-start | bytes 1572872 | tf_op jit(solution)/shard_map/ppermute | solution.py:250
  784.8 53.7 %all-to-all-start.10 = ((bf16[32,128,256]{2,1,0:T(8,128)(2,1)}), bf16[32,128,256]{2,1,0:T(8,128)(2,1)S(1)}, u32[]{:S(2)}, u32[]{:S(2)}) async-start(bf16[32,128,256]{2,1,0:T(8,128)(2,1)} %bitcast.196), calls=%async_computation.10 | async-start | bytes 4194304 | tf_op jit(solution)/shard_map/all_to_all | solution.py:242
  797.9 12.5 %collective-permute-start.48 = (bf16[8,128,512]{2,1,0:T(8,128)(2,1)}, bf16[8,128,512]{2,1,0:T(8,128)(2,1)S(1)}, u32[]{:S(2)}, u32[]{:S(2)}) collective-permute-start(bf16[8,128,512]{2,1,0:T(8,128)(2,1)} %get-tuple-element.311), channel_id=1, source_target_pairs={{0,1},{1,0},{2,3},{3,2},{4,5},{5,4},{6,7},{7,6},{8,9},{9,8},{10,11... | collective-permute-start | bytes 3145736 | tf_op jit(solution)/shard_map/ppermute | solution.py:250
  802.0 36.3 %collective-permute-start.50 = (bf16[8,128,512]{2,1,0:T(8,128)(2,1)S(1)}, bf16[8,128,512]{2,1,0:T(8,128)(2,1)}, u32[]{:S(2)}, u32[]{:S(2)}) collective-permute-start(bf16[8,128,512]{2,1,0:T(8,128)(2,1)S(1)} %add_convert_fusion.5), channel_id=1, source_target_pairs={{0,2},{1,3},{2,0},{3,1},{4,6},{5,7},{6,4},{7,5},{8,10},{9,11},{10,... | collective-permute-start | bytes 3145736 | tf_op jit(solution)/shard_map/ppermute | solution.py:250
  839.7 54.2 %all-to-all-start.11 = ((bf16[32,128,256]{2,1,0:T(8,128)(2,1)}), bf16[32,128,256]{2,1,0:T(8,128)(2,1)}, u32[]{:S(2)}, u32[]{:S(2)}) async-start(bf16[32,128,256]{2,1,0:T(8,128)(2,1)} %bitcast.195), calls=%async_computation.11 | async-start | bytes 4194304 | tf_op jit(solution)/shard_map/all_to_all | solution.py:242
  853.6 10.0 %collective-permute-start.51 = (bf16[8,128,512]{2,1,0:T(8,128)(2,1)}, bf16[8,128,512]{2,1,0:T(8,128)(2,1)}, u32[]{:S(2)}, u32[]{:S(2)}) collective-permute-start(bf16[8,128,512]{2,1,0:T(8,128)(2,1)} %get-tuple-element.332), channel_id=1, source_target_pairs={{0,1},{1,0},{2,3},{3,2},{4,5},{5,4},{6,7},{7,6},{8,9},{9,8},{10,11... | collective-permute-start | bytes 3145736 | tf_op jit(solution)/shard_map/ppermute | solution.py:250
  857.6 36.3 %collective-permute-start.53 = (bf16[8,128,512]{2,1,0:T(8,128)(2,1)S(1)}, bf16[8,128,512]{2,1,0:T(8,128)(2,1)}, u32[]{:S(2)}, u32[]{:S(2)}) collective-permute-start(bf16[8,128,512]{2,1,0:T(8,128)(2,1)S(1)} %add_convert_fusion.3), channel_id=1, source_target_pairs={{0,2},{1,3},{2,0},{3,1},{4,6},{5,7},{6,4},{7,5},{8,10},{9,11},{10,... | collective-permute-start | bytes 3145736 | tf_op jit(solution)/shard_map/ppermute | solution.py:250
  901.9 12.4 %collective-permute-start.54 = (bf16[8,128,512]{2,1,0:T(8,128)(2,1)}, bf16[8,128,512]{2,1,0:T(8,128)(2,1)}, u32[]{:S(2)}, u32[]{:S(2)}) collective-permute-start(bf16[8,128,512]{2,1,0:T(8,128)(2,1)} %get-tuple-element.346), channel_id=1, source_target_pairs={{0,1},{1,0},{2,3},{3,2},{4,5},{5,4},{6,7},{7,6},{8,9},{9,8},{10,11... | collective-permute-start | bytes 3145736 | tf_op jit(solution)/shard_map/ppermute | solution.py:250
  907.0 25.4 %collective-permute-start.56 = (bf16[8,128,512]{2,1,0:T(8,128)(2,1)S(1)}, bf16[8,128,512]{2,1,0:T(8,128)(2,1)}, u32[]{:S(2)}, u32[]{:S(2)}) collective-permute-start(bf16[8,128,512]{2,1,0:T(8,128)(2,1)S(1)} %add_convert_fusion.1), channel_id=1, source_target_pairs={{0,2},{1,3},{2,0},{3,1},{4,6},{5,7},{6,4},{7,5},{8,10},{9,11},{10,... | collective-permute-start | bytes 3145736 | tf_op jit(solution)/shard_map/ppermute | solution.py:250
  (88 other events, 492.3 us)

commit v3 on v2

--- a/solution.py
+++ b/solution.py
@@ -9,7 +9,7 @@
 BOTH = ("seq", "chan")
 BF = jnp.bfloat16
 F32 = jnp.float32
-VMEM_BYTES = 60 * 1024 * 1024
+VMEM_BYTES = 44 * 1024 * 1024
 
 
 def dot(left, right, left_dim, right_dim):
@@ -259,7 +259,6 @@
     tok_rows, width = query_in.shape
     local = tok_rows // BS
     unit = local // 4
-    half = unit // 2
     rows, blocks, _ = freq_kernel.shape
     query, key, value, cot = [
         x.reshape(local, BS, width) for x in (query_in, key_in, value_in, cotangent)
@@ -361,23 +360,16 @@
     c_spans = [(0, unit), (unit, 3 * unit)]
     b_pieces, c_shards, ones = [], [], []
 
-    part0a = factor_b1[:half]
-    moved0a = far(part0a)
+    part = factor_b1[:unit]
+    moved = far(part)
     b2 = spread(jnp.swapaxes(factor_b2, 1, 2), b_spans)
     c2 = spread(factor_c2, c_spans)
-    moved0a, factor_b1, factor_c1, b2, c2 = tie(moved0a, factor_b1, factor_c1, b2, c2)
-    part0b = factor_b1[half:unit]
-    moved0b = far(part0b)
-    shard = gathered(factor_b1, part0a, moved0a)
-    out = make_one(0, 0, half, shard, 0, None)
-    out, moved0b, factor_b1 = tie(out, moved0b, factor_b1)
-    b_pieces.append([(0, half, shard, 0)])
+    moved, factor_b1, factor_c1, b2, c2 = tie(moved, factor_b1, factor_c1, b2, c2)
+    b_pieces.append([(0, unit, gathered(factor_b1, part, moved), 0)])
     most = unit - max(1, unit // 4)
     part1a = factor_b1[unit : unit + most]
     moved1a = far(part1a)
-    shard = gathered(factor_b1, part0b, moved0b)
-    send = send_in(make_one(half, 0, unit - half, shard, half, out))
-    b_pieces[0].append((half, unit - half, shard, 0))
+    send = send_in(make_one(0, 0, unit, b_pieces[0][0][2], 0, None))
     send, moved1a, factor_b1 = tie(send, moved1a, factor_b1)
     recv = exchange(send)
 
@@ -454,22 +446,19 @@
     three1 = exchange(send)
 
     arrived = receive_out(back_a)
-    grad_query, c_mine, c_pass = None, [], []
+    grad_query, c_mine, c_got = None, [], []
     for k in (1, 2, 3):
         grad_query, *pairs = make_query(
             k * unit, 0, unit, c_shards[k], arrived, (k - 1) * unit, [grad_query]
         )
         mine, passed = near_sum(*pairs)
+        arrived, passed = tie(arrived, passed)
         c_mine += mine
-        c_pass.append(passed)
-    c_got = [far(p) for p in c_pass[:2]]
-    three1, send_b, grad_query, passed, *rest = tie(
-        three1, send_b, grad_query, c_pass[2], *c_mine, *c_got
-    )
+        c_got.append(far(passed))
+    three1, send_b, grad_query, *rest = tie(three1, send_b, grad_query, *c_mine, *c_got)
     c_mine, c_got = rest[:6], rest[6:]
     back_b = exchange(send_b)
 
-    c_got.append(far(passed))
     three1 = receive_in(three1)
     grad_freq, grad_b2, grad_c2, *outs = backward_freq(
         b2, c2, freq_kernel, spectrum, ones, [three0, three1]

time: 946 us -> 941 us (level)
  Pallas kernels: 157 us -> 126 us
  local copies, waits for them, and re-layouts: 85.7 us -> 116 us
    unnamed x136 -> x218, local copies, waits for them, and re-layouts: 22 us -> 50.6 us
    pallas_call x19 -> x17, Pallas kernels: 118 us -> 90 us  [token_call(): pl.pallas_call(body, grid_spec=pltpu.PrefetchScalarGridSpec(num_scalar_pr...]
    ppermute x57 -> x51, waiting for transfers between devices: 469 us -> 496 us  [swap(): lax.ppermute(tensor, 'chan', [(m, m ^ distance) for m in range(chan_count)])]
    all_to_all x12, waiting for transfers between devices: 74.3 us -> 52.5 us  [exchange(): return lax.all_to_all(tensor, BOTH, split_axis=0, concat_axis=0, tiled=True)]
    ppermute x57 -> x51, starting transfers between devices: 45 us -> 40.8 us  [swap(): lax.ppermute(tensor, 'chan', [(m, m ^ distance) for m in range(chan_count)])]
  transfers between devices with their start and end apart: 69 -> 63, of which waited for: 41 -> 35; matrix products, arithmetic and copies ran while one was open for 11% -> 11% of each run, Pallas kernels for 16% -> 13%
where the time goes in v3:
time: 941 us; the launch traced here: 931 us
  waiting for transfers between devices  549 us (58%)
  Pallas kernels  126 us (13%)
  local copies, waits for them, and re-layouts  116 us (12%)
  starting transfers between devices  103 us (11%)
  other arithmetic  35.7 us (4%)
    ppermute x51, waiting for transfers between devices, swap(): lax.ppermute(tensor, 'chan', [(m, m ^ distance) for m in range(chan_count)])  496 us
    pallas_call x17, Pallas kernels, token_call(): pl.pallas_call(body, grid_spec=pltpu.PrefetchScalarGridSpec(num_scalar_pr...  90 us
    all_to_all x12, starting transfers between devices, exchange(): return lax.all_to_all(tensor, BOTH, split_axis=0, concat_axis=0, tiled=True)  62 us
    all_to_all x12, waiting for transfers between devices, exchange(): return lax.all_to_all(tensor, BOTH, split_axis=0, concat_axis=0, tiled=True)  52.5 us
    unnamed x218, local copies, waits for them, and re-layouts  50.6 us
    ppermute x51, starting transfers between devices, swap(): lax.ppermute(tensor, 'chan', [(m, m ^ distance) for m in range(chan_count)])  40.8 us
    pallas_call x2, Pallas kernels, freq_call(): pl.pallas_call(body, grid=(count // step,), in_specs=[spec(x) for x in in...  35.7 us
    reshape x6, local copies, waits for them, and re-layouts, send_out(): shaped = tensor.reshape(rows, chan_count, seq_count, -1, width)  26.5 us
  transfers between devices with their start and end apart: 63, of which 35 were waited for; matrix products, arithmetic and copies ran while one was open for 11% of the time, Pallas kernels for 13%

profile of v3, /device:TPU:0, one launch (start us, length us, event | category | flops | bytes accessed | tf_op | source)
XLA Modules:
  0.0 931.0 jit_solution(13896521989559151392)
XLA Ops:
  15.1 14.1 %collective-permute-done.refs_1_ = bf16[8,128,512]{2,1,0:T(8,128)(2,1)S(1)} collective-permute-done((bf16[8,128,512]{2,1,0:T(8,128)(2,1)}, bf16[8,128,512]{2,1,0:T(8,128)(2,1)S(1)}, u32[]{:S(2)}, u32[]{:S(2)}) %collective-permute-start) | collective-permute-done | bytes 1048608 | tf_op jit(solution)/shard_map/ppermute | solution.py:250
  36.5 4.7 shard_map.152
  41.2 10.4 %collective-permute-done.3.refs_1_ = bf16[6,128,512]{2,1,0:T(8,128)(2,1)} collective-permute-done((bf16[6,128,512]{2,1,0:T(8,128)(2,1)}, bf16[6,128,512]{2,1,0:T(8,128)(2,1)}, u32[]{:S(2)}, u32[]{:S(2)}) %collective-permute-start.3) | collective-permute-done | bytes 786464 | tf_op jit(solution)/shard_map/ppermute | solution.py:250
  51.6 6.1 all-to-all-start
  63.6 5.2 shard_map.153.refs_6_
  68.8 11.6 %collective-permute-done.6.refs_1_ = bf16[2,128,512]{2,1,0:T(8,128)(2,1)S(1)} collective-permute-done((bf16[2,128,512]{2,1,0:T(8,128)(2,1)S(1)}, bf16[2,128,512]{2,1,0:T(8,128)(2,1)S(1)}, u32[]{:S(2)}, u32[]{:S(2)}) %collective-permute-start.6) | collective-permute-done | bytes 262176 | tf_op jit(solution)/shard_map/ppermute | solution.py:250
  90.0 21.2 %collective-permute-done.9.refs_1_ = bf16[8,128,512]{2,1,0:T(8,128)(2,1)} collective-permute-done((bf16[8,128,512]{2,1,0:T(8,128)(2,1)}, bf16[8,128,512]{2,1,0:T(8,128)(2,1)}, u32[]{:S(2)}, u32[]{:S(2)}) %collective-permute-start.9) | collective-permute-done | bytes 1048608 | tf_op jit(solution)/shard_map/ppermute | solution.py:250
  112.6 7.7 all-to-all-start.1
  132.8 35.2 %collective-permute-done.12.refs_1_ = bf16[8,128,512]{2,1,0:T(8,128)(2,1)S(1)} collective-permute-done((bf16[8,128,512]{2,1,0:T(8,128)(2,1)S(1)}, bf16[8,128,512]{2,1,0:T(8,128)(2,1)S(1)}, u32[]{:S(2)}, u32[]{:S(2)}) %collective-permute-start.12) | collective-permute-done | bytes 1048608 | tf_op jit(solution)/shard_map/ppermute | solution.py:250
  169.1 4.3 all-to-all-start.2
  188.7 33.0 %collective-permute-done.15.refs_1_ = bf16[8,128,512]{2,1,0:T(8,128)(2,1)} collective-permute-done((bf16[8,128,512]{2,1,0:T(8,128)(2,1)S(1)}, bf16[8,128,512]{2,1,0:T(8,128)(2,1)}, u32[]{:S(2)}, u32[]{:S(2)}) %collective-permute-start.15) | collective-permute-done | bytes 1048608 | tf_op jit(solution)/shard_map/ppermute | solution.py:250
  222.1 4.3 all-to-all-start.3
  237.9 36.3 %collective-permute-done.18.refs_1_ = bf16[8,128,512]{2,1,0:T(8,128)(2,1)} collective-permute-done((bf16[8,128,512]{2,1,0:T(8,128)(2,1)}, bf16[8,128,512]{2,1,0:T(8,128)(2,1)}, u32[]{:S(2)}, u32[]{:S(2)}) %collective-permute-start.18) | collective-permute-done | bytes 1048608 | tf_op jit(solution)/shard_map/ppermute | solution.py:250
  275.1 4.5 all-to-all-start.4
  285.3 14.7 %shard_map.158 = (bf16[16,256,1024]{2,1,0:T(8,128)(2,1)}, bf16[16,4,64,256]{3,2,1,0:T(8,128)(2,1)S(1)}, bf16[16,4,192,256]{3,2,1,0:T(8,128)(2,1)}) custom-call(bf16[16,256,256]{2,1,0:T(8,128)(2,1)S(1)} %copy-done.12, bf16[16,256,256]{2,1,0:T(8,128)(2,1)S(1)} %copy-done.13, bf16[16,256,1024]{2,1,0:T(8,128)(2,1)} %refs_2_.3, ...), custom_call_target="tpu_custom_call" | custom-call | flops 4294967296 | bytes 37748736 | tf_op jit(solution)/shard_map/pallas_call | solution.py:170
  300.0 11.4 %copy.39 = bf16[16,4,8,24,256]{4,0,3,1,2:T(8,128)(2,1)} copy(bf16[16,4,8,24,256]{4,3,2,1,0:T(8,128)(2,1)} %bitcast.200) | data formatting | bytes 12582912 | tf_op jit(solution)/shard_map/reshape | solution.py:306
  311.4 16.0 %collective-permute-done.19.refs_1_ = bf16[8,128,512]{2,1,0:T(8,128)(2,1)} collective-permute-done((bf16[8,128,512]{2,1,0:T(8,128)(2,1)}, bf16[8,128,512]{2,1,0:T(8,128)(2,1)}, u32[]{:S(2)}, u32[]{:S(2)}) %collective-permute-start.19) | collective-permute-done | bytes 1048608 | tf_op jit(solution)/shard_map/ppermute | solution.py:250
  328.3 4.7 all-to-all-start.5
  336.1 79.1 %collective-permute-done.20.refs_1_ = bf16[8,128,512]{2,1,0:T(8,128)(2,1)S(1)} collective-permute-done((bf16[8,128,512]{2,1,0:T(8,128)(2,1)}, bf16[8,128,512]{2,1,0:T(8,128)(2,1)S(1)}, u32[]{:S(2)}, u32[]{:S(2)}) %collective-permute-start.20) | collective-permute-done | bytes 1048608 | tf_op jit(solution)/shard_map/ppermute | solution.py:250
  417.4 4.8 shard_map.159.refs_6_
  429.0 5.0 shard_map.160.refs_6_
  434.0 4.6 shard_map.161
  439.6 33.4 %all-to-all-done.5 = bf16[32,384,256]{2,1,0:T(8,128)(2,1)} async-done(((bf16[32,384,256]{2,1,0:T(8,128)(2,1)}), bf16[32,384,256]{2,1,0:T(8,128)(2,1)}, u32[]{:S(2)}, u32[]{:S(2)}) %all-to-all-start.5) | async-done | bytes 6291488 | tf_op jit(solution)/shard_map/all_to_all | solution.py:242
  473.0 5.7 all-to-all-start.6
  481.1 6.3 shard_map.162
  490.5 6.3 shard_map.163
  499.9 6.1 shard_map.164
  511.9 49.3 %collective-permute-done.32 = bf16[8,128,512]{2,1,0:T(8,128)(2,1)S(1)} collective-permute-done((bf16[8,128,512]{2,1,0:T(8,128)(2,1)S(1)}, bf16[8,128,512]{2,1,0:T(8,128)(2,1)S(1)}, u32[]{:S(2)}, u32[]{:S(2)}) %collective-permute-start.32) | collective-permute-done | bytes 1048608 | tf_op jit(solution)/shard_map/ppermute | solution.py:250
  561.2 23.4 %collective-permute-done.33 = bf16[8,128,512]{2,1,0:T(8,128)(2,1)S(1)} collective-permute-done((bf16[8,128,512]{2,1,0:T(8,128)(2,1)S(1)}, bf16[8,128,512]{2,1,0:T(8,128)(2,1)S(1)}, u32[]{:S(2)}, u32[]{:S(2)}) %collective-permute-start.33) | collective-permute-done | bytes 1048608 | tf_op jit(solution)/shard_map/ppermute | solution.py:250
  585.6 30.7 %collective-permute-done.35 = bf16[8,128,512]{2,1,0:T(8,128)(2,1)} collective-permute-done((bf16[8,128,512]{2,1,0:T(8,128)(2,1)S(1)}, bf16[8,128,512]{2,1,0:T(8,128)(2,1)}, u32[]{:S(2)}, u32[]{:S(2)}) %collective-permute-start.35) | collective-permute-done | bytes 1048608 | tf_op jit(solution)/shard_map/ppermute | solution.py:250
  618.9 6.5 all-to-all-start.7
  625.4 7.7 copy.42
  633.1 21.0 %shard_map.165 = (bf16[16,256,1024]{2,1,0:T(8,128)(2,1)}, bf16[16,256,256]{2,1,0:T(8,128)(2,1)S(1)}, bf16[16,256,256]{2,1,0:T(8,128)(2,1)S(1)}, bf16[16,4,64,256...) custom-call(bf16[16,256,256]{2,1,0:T(8,128)(2,1)} %get-tuple-element, ...), custom_call_target="tpu_custom_call" | custom-call | flops 10737418240 | bytes 58720256 | tf_op jit(solution)/shard_map/pallas_call | solution.py:170
  661.1 13.1 %all-to-all-done.7 = bf16[32,128,256]{2,1,0:T(8,128)(2,1)S(1)} async-done(((bf16[32,128,256]{2,1,0:T(8,128)(2,1)}), bf16[32,128,256]{2,1,0:T(8,128)(2,1)S(1)}, u32[]{:S(2)}, u32[]{:S(2)}) %all-to-all-start.7) | async-done | bytes 2097184 | tf_op jit(solution)/shard_map/all_to_all | solution.py:242
  675.5 4.1 all-to-all-start.8
  683.6 6.0 shard_map.166
  713.2 16.3 %collective-permute-done.38 = bf16[8,128,512]{2,1,0:T(8,128)(2,1)} collective-permute-done((bf16[8,128,512]{2,1,0:T(8,128)(2,1)S(1)}, bf16[8,128,512]{2,1,0:T(8,128)(2,1)}, u32[]{:S(2)}, u32[]{:S(2)}) %collective-permute-start.38) | collective-permute-done | bytes 1048608 | tf_op jit(solution)/shard_map/ppermute | solution.py:250
  729.5 4.3 all-to-all-start.9
  737.5 6.2 shard_map.167
  754.0 28.7 %collective-permute-done.41 = bf16[8,128,512]{2,1,0:T(8,128)(2,1)} collective-permute-done((bf16[8,128,512]{2,1,0:T(8,128)(2,1)S(1)}, bf16[8,128,512]{2,1,0:T(8,128)(2,1)}, u32[]{:S(2)}, u32[]{:S(2)}) %collective-permute-start.41) | collective-permute-done | bytes 1048608 | tf_op jit(solution)/shard_map/ppermute | solution.py:250
  782.8 4.8 all-to-all-start.10
  791.3 6.5 shard_map.168
  810.4 26.3 %collective-permute-done.44 = bf16[8,128,512]{2,1,0:T(8,128)(2,1)} collective-permute-done((bf16[8,128,512]{2,1,0:T(8,128)(2,1)S(1)}, bf16[8,128,512]{2,1,0:T(8,128)(2,1)}, u32[]{:S(2)}, u32[]{:S(2)}) %collective-permute-start.44) | collective-permute-done | bytes 1048608 | tf_op jit(solution)/shard_map/ppermute | solution.py:250
  836.7 5.1 all-to-all-start.11
  844.3 6.4 shard_map.169
  860.9 29.5 %collective-permute-done.47 = bf16[8,128,512]{2,1,0:T(8,128)(2,1)} collective-permute-done((bf16[8,128,512]{2,1,0:T(8,128)(2,1)S(1)}, bf16[8,128,512]{2,1,0:T(8,128)(2,1)}, u32[]{:S(2)}, u32[]{:S(2)}) %collective-permute-start.47) | collective-permute-done | bytes 1048608 | tf_op jit(solution)/shard_map/ppermute | solution.py:250
  890.6 6.7 shard_map.170
  908.9 18.6 %collective-permute-done.50 = bf16[8,128,512]{2,1,0:T(8,128)(2,1)} collective-permute-done((bf16[8,128,512]{2,1,0:T(8,128)(2,1)}, bf16[8,128,512]{2,1,0:T(8,128)(2,1)}, u32[]{:S(2)}, u32[]{:S(2)}) %collective-permute-start.50) | collective-permute-done | bytes 1048608 | tf_op jit(solution)/shard_map/ppermute | solution.py:250
  (366 shorter events, 210.9 us)
Async XLA Ops:
  2.9 26.3 %collective-permute-start = (bf16[8,128,512]{2,1,0:T(8,128)(2,1)}, bf16[8,128,512]{2,1,0:T(8,128)(2,1)S(1)}, u32[]{:S(2)}, u32[]{:S(2)}) collective-permute-start(bf16[8,128,512]{2,1,0:T(8,128)(2,1)} %slice.63), channel_id=1, source_target_pairs={{0,2},{1,3},{2,0},{3,1},{4,6},{5,7},{6,4},{7,5},{8,10},{9,11},{10,... | collective-permute-start | bytes 3145736 | tf_op jit(solution)/shard_map/ppermute | solution.py:250
  5.9 27.7 %collective-permute-start.1 = (bf16[8,128,512]{2,1,0:T(8,128)(2,1)}, bf16[8,128,512]{2,1,0:T(8,128)(2,1)S(1)}, u32[]{:S(2)}, u32[]{:S(2)}) collective-permute-start(bf16[8,128,512]{2,1,0:T(8,128)(2,1)} %slice.63), channel_id=1, source_target_pairs={{0,1},{1,0},{2,3},{3,2},{4,5},{5,4},{6,7},{7,6},{8,9},{9,8},{10,11... | collective-permute-start | bytes 3145736 | tf_op jit(solution)/shard_map/ppermute | solution.py:250
  31.7 19.9 %collective-permute-start.3 = (bf16[6,128,512]{2,1,0:T(8,128)(2,1)}, bf16[6,128,512]{2,1,0:T(8,128)(2,1)}, u32[]{:S(2)}, u32[]{:S(2)}) collective-permute-start(bf16[6,128,512]{2,1,0:T(8,128)(2,1)} %slice.70), channel_id=1, source_target_pairs={{0,2},{1,3},{2,0},{3,1},{4,6},{5,7},{6,4},{7,5},{8,10},{9,11},{10,... | collective-permute-start | bytes 2359304 | tf_op jit(solution)/shard_map/ppermute | solution.py:250
  51.6 59.7 %all-to-all-start = ((bf16[32,128,256]{2,1,0:T(8,128)(2,1)}), bf16[32,128,256]{2,1,0:T(8,128)(2,1)S(1)}, u32[]{:S(2)}, u32[]{:S(2)}) async-start(bf16[32,128,256]{2,1,0:T(8,128)(2,1)} %bitcast.17), calls=%async_computation | async-start | bytes 4194304 | tf_op jit(solution)/shard_map/all_to_all | solution.py:242
  59.2 21.2 %collective-permute-start.6 = (bf16[2,128,512]{2,1,0:T(8,128)(2,1)S(1)}, bf16[2,128,512]{2,1,0:T(8,128)(2,1)S(1)}, u32[]{:S(2)}, u32[]{:S(2)}) collective-permute-start(bf16[2,128,512]{2,1,0:T(8,128)(2,1)S(1)} %slice.71), channel_id=1, source_target_pairs={{0,2},{1,3},{2,0},{3,1},{4,6},{5,7},{6,4},{7,5},{8,10},{9,11},{10,... | collective-permute-start | bytes 786440 | tf_op jit(solution)/shard_map/ppermute | solution.py:250
  81.5 29.8 %collective-permute-start.9 = (bf16[8,128,512]{2,1,0:T(8,128)(2,1)}, bf16[8,128,512]{2,1,0:T(8,128)(2,1)}, u32[]{:S(2)}, u32[]{:S(2)}) collective-permute-start(bf16[8,128,512]{2,1,0:T(8,128)(2,1)} %slice.72), channel_id=1, source_target_pairs={{0,2},{1,3},{2,0},{3,1},{4,6},{5,7},{6,4},{7,5},{8,10},{9,11},{10,... | collective-permute-start | bytes 3145736 | tf_op jit(solution)/shard_map/ppermute | solution.py:250
  112.6 56.5 %all-to-all-start.1 = ((bf16[32,128,256]{2,1,0:T(8,128)(2,1)}), bf16[32,128,256]{2,1,0:T(8,128)(2,1)}, u32[]{:S(2)}, u32[]{:S(2)}) async-start(bf16[32,128,256]{2,1,0:T(8,128)(2,1)} %bitcast.20), calls=%async_computation.1 | async-start | bytes 4194304 | tf_op jit(solution)/shard_map/all_to_all | solution.py:242
  120.3 4.4 collective-permute-start.10
  122.3 45.7 %collective-permute-start.12 = (bf16[8,128,512]{2,1,0:T(8,128)(2,1)S(1)}, bf16[8,128,512]{2,1,0:T(8,128)(2,1)S(1)}, u32[]{:S(2)}, u32[]{:S(2)}) collective-permute-start(bf16[8,128,512]{2,1,0:T(8,128)(2,1)S(1)} %slice.73), channel_id=1, source_target_pairs={{0,2},{1,3},{2,0},{3,1},{4,6},{5,7},{6,4},{7,5},{8,10},{9,11},{10,... | collective-permute-start | bytes 3145736 | tf_op jit(solution)/shard_map/ppermute | solution.py:250
  169.1 53.0 %all-to-all-start.2 = ((bf16[32,128,256]{2,1,0:T(8,128)(2,1)}), bf16[32,128,256]{2,1,0:T(8,128)(2,1)}, u32[]{:S(2)}, u32[]{:S(2)}) async-start(bf16[32,128,256]{2,1,0:T(8,128)(2,1)} %bitcast.140), calls=%async_computation.2 | async-start | bytes 4194304 | tf_op jit(solution)/shard_map/all_to_all | solution.py:242
  177.3 6.0 collective-permute-start.13
  177.5 5.8 collective-permute-start.14
  177.8 43.9 %collective-permute-start.15 = (bf16[8,128,512]{2,1,0:T(8,128)(2,1)S(1)}, bf16[8,128,512]{2,1,0:T(8,128)(2,1)}, u32[]{:S(2)}, u32[]{:S(2)}) collective-permute-start(bf16[8,128,512]{2,1,0:T(8,128)(2,1)S(1)} %get-tuple-element.347), channel_id=1, source_target_pairs={{0,2},{1,3},{2,0},{3,1},{4,6},{5,7},{6,4},{7,5},{8,10},{9,11},{10,... | collective-permute-start | bytes 3145736 | tf_op jit(solution)/shard_map/ppermute | solution.py:250
  222.1 53.0 %all-to-all-start.3 = ((bf16[32,128,256]{2,1,0:T(8,128)(2,1)}), bf16[32,128,256]{2,1,0:T(8,128)(2,1)}, u32[]{:S(2)}, u32[]{:S(2)}) async-start(bf16[32,128,256]{2,1,0:T(8,128)(2,1)} %bitcast.141), calls=%async_computation.3 | async-start | bytes 4194304 | tf_op jit(solution)/shard_map/all_to_all | solution.py:242
  226.3 6.0 collective-permute-start.16
  226.6 5.8 collective-permute-start.17
  226.9 47.2 %collective-permute-start.18 = (bf16[8,128,512]{2,1,0:T(8,128)(2,1)}, bf16[8,128,512]{2,1,0:T(8,128)(2,1)}, u32[]{:S(2)}, u32[]{:S(2)}) collective-permute-start(bf16[8,128,512]{2,1,0:T(8,128)(2,1)} %get-tuple-element.346), channel_id=1, source_target_pairs={{0,2},{1,3},{2,0},{3,1},{4,6},{5,7},{6,4},{7,5},{8,10},{9,11},{10,... | collective-permute-start | bytes 3145736 | tf_op jit(solution)/shard_map/ppermute | solution.py:250
  275.1 53.2 %all-to-all-start.4 = ((bf16[32,128,256]{2,1,0:T(8,128)(2,1)}), bf16[32,128,256]{2,1,0:T(8,128)(2,1)}, u32[]{:S(2)}, u32[]{:S(2)}) async-start(bf16[32,128,256]{2,1,0:T(8,128)(2,1)} %bitcast.142), calls=%async_computation.4 | async-start | bytes 4194304 | tf_op jit(solution)/shard_map/all_to_all | solution.py:242
  279.6 47.8 %collective-permute-start.19 = (bf16[8,128,512]{2,1,0:T(8,128)(2,1)}, bf16[8,128,512]{2,1,0:T(8,128)(2,1)}, u32[]{:S(2)}, u32[]{:S(2)}) collective-permute-start(bf16[8,128,512]{2,1,0:T(8,128)(2,1)} %get-tuple-element.345), channel_id=1, source_target_pairs={{0,2},{1,3},{2,0},{3,1},{4,6},{5,7},{6,4},{7,5},{8,10},{9,11},{10,... | collective-permute-start | bytes 3145736 | tf_op jit(solution)/shard_map/ppermute | solution.py:250
  328.3 144.7 %all-to-all-start.5 = ((bf16[32,384,256]{2,1,0:T(8,128)(2,1)}), bf16[32,384,256]{2,1,0:T(8,128)(2,1)}, u32[]{:S(2)}, u32[]{:S(2)}) async-start(bf16[32,384,256]{2,1,0:T(8,128)(2,1)} %bitcast.184), calls=%async_computation.5 | async-start | bytes 12582912 | tf_op jit(solution)/shard_map/all_to_all | solution.py:242
  333.4 81.8 %collective-permute-start.20 = (bf16[8,128,512]{2,1,0:T(8,128)(2,1)}, bf16[8,128,512]{2,1,0:T(8,128)(2,1)S(1)}, u32[]{:S(2)}, u32[]{:S(2)}) collective-permute-start(bf16[8,128,512]{2,1,0:T(8,128)(2,1)} %get-tuple-element.344), channel_id=1, source_target_pairs={{0,2},{1,3},{2,0},{3,1},{4,6},{5,7},{6,4},{7,5},{8,10},{9,11},{10,... | collective-permute-start | bytes 3145736 | tf_op jit(solution)/shard_map/ppermute | solution.py:250
  335.1 80.1 %collective-permute-start.26 = (bf16[8,128,512]{2,1,0:T(8,128)(2,1)}, bf16[8,128,512]{2,1,0:T(8,128)(2,1)S(1)}, u32[]{:S(2)}, u32[]{:S(2)}) collective-permute-start(bf16[8,128,512]{2,1,0:T(8,128)(2,1)} %collective-permute-done.18.refs_1_), channel_id=1, source_target_pairs={{0,1},{1,0},{2,3},{3,2},{4,5},{5,4},{6,7},{7,6},{8,9},{9,8},{10,11... | collective-permute-start | bytes 3145736 | tf_op jit(solution)/shard_map/ppermute | solution.py:250
  335.2 93.8 %collective-permute-start.23 = (bf16[8,128,512]{2,1,0:T(8,128)(2,1)}, bf16[8,128,512]{2,1,0:T(8,128)(2,1)S(1)}, u32[]{:S(2)}, u32[]{:S(2)}) collective-permute-start(bf16[8,128,512]{2,1,0:T(8,128)(2,1)} %get-tuple-element.345), channel_id=1, source_target_pairs={{0,1},{1,0},{2,3},{3,2},{4,5},{5,4},{6,7},{7,6},{8,9},{9,8},{10,11... | collective-permute-start | bytes 3145736 | tf_op jit(solution)/shard_map/ppermute | solution.py:250
  335.6 93.4 %collective-permute-start.24 = (bf16[8,128,512]{2,1,0:T(8,128)(2,1)}, bf16[8,128,512]{2,1,0:T(8,128)(2,1)S(1)}, u32[]{:S(2)}, u32[]{:S(2)}) collective-permute-start(bf16[8,128,512]{2,1,0:T(8,128)(2,1)} %collective-permute-done.19.refs_1_), channel_id=1, source_target_pairs={{0,1},{1,0},{2,3},{3,2},{4,5},{5,4},{6,7},{7,6},{8,9},{9,8},{10,11... | collective-permute-start | bytes 3145736 | tf_op jit(solution)/shard_map/ppermute | solution.py:250
  335.7 98.3 %collective-permute-start.21 = (bf16[8,128,512]{2,1,0:T(8,128)(2,1)}, bf16[8,128,512]{2,1,0:T(8,128)(2,1)S(1)}, u32[]{:S(2)}, u32[]{:S(2)}) collective-permute-start(bf16[8,128,512]{2,1,0:T(8,128)(2,1)} %get-tuple-element.344), channel_id=1, source_target_pairs={{0,1},{1,0},{2,3},{3,2},{4,5},{5,4},{6,7},{7,6},{8,9},{9,8},{10,11... | collective-permute-start | bytes 3145736 | tf_op jit(solution)/shard_map/ppermute | solution.py:250
  415.2 18.8 %collective-permute-start.22 = (bf16[8,128,512]{2,1,0:T(8,128)(2,1)S(1)}, bf16[8,128,512]{2,1,0:T(8,128)(2,1)S(1)}, u32[]{:S(2)}, u32[]{:S(2)}) collective-permute-start(bf16[8,128,512]{2,1,0:T(8,128)(2,1)S(1)} %collective-permute-done.20.refs_1_), channel_id=1, source_target_pairs={{0,1},{1,0},{2,3},{3,2},{4,5},{5,4},{6,7},{7,6},{8,9},{9,8},{10,11... | collective-permute-start | bytes 3145736 | tf_op jit(solution)/shard_map/ppermute | solution.py:250
  473.0 145.9 %all-to-all-start.6 = ((bf16[32,384,256]{2,1,0:T(8,128)(2,1)}), bf16[32,384,256]{2,1,0:T(8,128)(2,1)}, u32[]{:S(2)}, u32[]{:S(2)}) async-start(bf16[32,384,256]{2,1,0:T(8,128)(2,1)} %bitcast.180), calls=%async_computation.6 | async-start | bytes 12582912 | tf_op jit(solution)/shard_map/all_to_all | solution.py:242
  506.2 4.5 collective-permute-start.29
  506.5 5.4 collective-permute-start.30
  506.7 54.5 %collective-permute-start.32 = (bf16[8,128,512]{2,1,0:T(8,128)(2,1)S(1)}, bf16[8,128,512]{2,1,0:T(8,128)(2,1)S(1)}, u32[]{:S(2)}, u32[]{:S(2)}) collective-permute-start(bf16[8,128,512]{2,1,0:T(8,128)(2,1)S(1)} %add_convert_fusion.15), channel_id=1, source_target_pairs={{0,2},{1,3},{2,0},{3,1},{4,6},{5,7},{6,4},{7,5},{8,10},{9,11},{10,... | collective-permute-start | bytes 3145736 | tf_op jit(solution)/shard_map/ppermute | solution.py:250
  508.4 52.8 %collective-permute-start.31 = (bf16[8,128,512]{2,1,0:T(8,128)(2,1)S(1)}, bf16[8,128,512]{2,1,0:T(8,128)(2,1)S(1)}, u32[]{:S(2)}, u32[]{:S(2)}) collective-permute-start(bf16[8,128,512]{2,1,0:T(8,128)(2,1)S(1)} %get-tuple-element.226), channel_id=1, source_target_pairs={{0,1},{1,0},{2,3},{3,2},{4,5},{5,4},{6,7},{7,6},{8,9},{9,8},{10,11... | collective-permute-start | bytes 3145736 | tf_op jit(solution)/shard_map/ppermute | solution.py:250
  508.7 75.9 %collective-permute-start.33 = (bf16[8,128,512]{2,1,0:T(8,128)(2,1)S(1)}, bf16[8,128,512]{2,1,0:T(8,128)(2,1)S(1)}, u32[]{:S(2)}, u32[]{:S(2)}) collective-permute-start(bf16[8,128,512]{2,1,0:T(8,128)(2,1)S(1)} %add_convert_fusion.14), channel_id=1, source_target_pairs={{0,2},{1,3},{2,0},{3,1},{4,6},{5,7},{6,4},{7,5},{8,10},{9,11},{10,... | collective-permute-start | bytes 3145736 | tf_op jit(solution)/shard_map/ppermute | solution.py:250
  510.7 105.6 %collective-permute-start.35 = (bf16[8,128,512]{2,1,0:T(8,128)(2,1)S(1)}, bf16[8,128,512]{2,1,0:T(8,128)(2,1)}, u32[]{:S(2)}, u32[]{:S(2)}) collective-permute-start(bf16[8,128,512]{2,1,0:T(8,128)(2,1)S(1)} %add_convert_fusion.13), channel_id=1, source_target_pairs={{0,2},{1,3},{2,0},{3,1},{4,6},{5,7},{6,4},{7,5},{8,10},{9,11},{10,... | collective-permute-start | bytes 3145736 | tf_op jit(solution)/shard_map/ppermute | solution.py:250
  618.9 55.3 %all-to-all-start.7 = ((bf16[32,128,256]{2,1,0:T(8,128)(2,1)}), bf16[32,128,256]{2,1,0:T(8,128)(2,1)S(1)}, u32[]{:S(2)}, u32[]{:S(2)}) async-start(bf16[32,128,256]{2,1,0:T(8,128)(2,1)} %bitcast.193), calls=%async_computation.7 | async-start | bytes 4194304 | tf_op jit(solution)/shard_map/all_to_all | solution.py:242
  675.5 54.0 %all-to-all-start.8 = ((bf16[32,128,256]{2,1,0:T(8,128)(2,1)}), bf16[32,128,256]{2,1,0:T(8,128)(2,1)S(1)}, u32[]{:S(2)}, u32[]{:S(2)}) async-start(bf16[32,128,256]{2,1,0:T(8,128)(2,1)} %bitcast.197), calls=%async_computation.8 | async-start | bytes 4194304 | tf_op jit(solution)/shard_map/all_to_all | solution.py:242
  693.2 19.1 %collective-permute-start.36 = (bf16[8,128,512]{2,1,0:T(8,128)(2,1)S(1)}, bf16[8,128,512]{2,1,0:T(8,128)(2,1)S(1)}, u32[]{:S(2)}, u32[]{:S(2)}) collective-permute-start(bf16[8,128,512]{2,1,0:T(8,128)(2,1)S(1)} %get-tuple-element.258), channel_id=1, source_target_pairs={{0,1},{1,0},{2,3},{3,2},{4,5},{5,4},{6,7},{7,6},{8,9},{9,8},{10,11... | collective-permute-start | bytes 3145736 | tf_op jit(solution)/shard_map/ppermute | solution.py:250
  693.7 35.7 %collective-permute-start.38 = (bf16[8,128,512]{2,1,0:T(8,128)(2,1)S(1)}, bf16[8,128,512]{2,1,0:T(8,128)(2,1)}, u32[]{:S(2)}, u32[]{:S(2)}) collective-permute-start(bf16[8,128,512]{2,1,0:T(8,128)(2,1)S(1)} %add_convert_fusion.12), channel_id=1, source_target_pairs={{0,2},{1,3},{2,0},{3,1},{4,6},{5,7},{6,4},{7,5},{8,10},{9,11},{10,... | collective-permute-start | bytes 3145736 | tf_op jit(solution)/shard_map/ppermute | solution.py:250
  729.5 53.3 %all-to-all-start.9 = ((bf16[32,128,256]{2,1,0:T(8,128)(2,1)}), bf16[32,128,256]{2,1,0:T(8,128)(2,1)}, u32[]{:S(2)}, u32[]{:S(2)}) async-start(bf16[32,128,256]{2,1,0:T(8,128)(2,1)} %bitcast.195), calls=%async_computation.9 | async-start | bytes 4194304 | tf_op jit(solution)/shard_map/all_to_all | solution.py:242
  744.2 8.8 collective-permute-start.39
  746.8 36.0 %collective-permute-start.41 = (bf16[8,128,512]{2,1,0:T(8,128)(2,1)S(1)}, bf16[8,128,512]{2,1,0:T(8,128)(2,1)}, u32[]{:S(2)}, u32[]{:S(2)}) collective-permute-start(bf16[8,128,512]{2,1,0:T(8,128)(2,1)S(1)} %add_convert_fusion.8), channel_id=1, source_target_pairs={{0,2},{1,3},{2,0},{3,1},{4,6},{5,7},{6,4},{7,5},{8,10},{9,11},{10,... | collective-permute-start | bytes 3145736 | tf_op jit(solution)/shard_map/ppermute | solution.py:250
  782.8 53.9 %all-to-all-start.10 = ((bf16[32,128,256]{2,1,0:T(8,128)(2,1)}), bf16[32,128,256]{2,1,0:T(8,128)(2,1)S(1)}, u32[]{:S(2)}, u32[]{:S(2)}) async-start(bf16[32,128,256]{2,1,0:T(8,128)(2,1)} %bitcast.194), calls=%async_computation.10 | async-start | bytes 4194304 | tf_op jit(solution)/shard_map/all_to_all | solution.py:242
  798.1 11.3 %collective-permute-start.42 = (bf16[8,128,512]{2,1,0:T(8,128)(2,1)S(1)}, bf16[8,128,512]{2,1,0:T(8,128)(2,1)S(1)}, u32[]{:S(2)}, u32[]{:S(2)}) collective-permute-start(bf16[8,128,512]{2,1,0:T(8,128)(2,1)S(1)} %get-tuple-element.299), channel_id=1, source_target_pairs={{0,1},{1,0},{2,3},{3,2},{4,5},{5,4},{6,7},{7,6},{8,9},{9,8},{10,11... | collective-permute-start | bytes 3145736 | tf_op jit(solution)/shard_map/ppermute | solution.py:250
  800.9 35.8 %collective-permute-start.44 = (bf16[8,128,512]{2,1,0:T(8,128)(2,1)S(1)}, bf16[8,128,512]{2,1,0:T(8,128)(2,1)}, u32[]{:S(2)}, u32[]{:S(2)}) collective-permute-start(bf16[8,128,512]{2,1,0:T(8,128)(2,1)S(1)} %add_convert_fusion.6), channel_id=1, source_target_pairs={{0,2},{1,3},{2,0},{3,1},{4,6},{5,7},{6,4},{7,5},{8,10},{9,11},{10,... | collective-permute-start | bytes 3145736 | tf_op jit(solution)/shard_map/ppermute | solution.py:250
  836.7 53.9 %all-to-all-start.11 = ((bf16[32,128,256]{2,1,0:T(8,128)(2,1)}), bf16[32,128,256]{2,1,0:T(8,128)(2,1)}, u32[]{:S(2)}, u32[]{:S(2)}) async-start(bf16[32,128,256]{2,1,0:T(8,128)(2,1)} %bitcast.191), calls=%async_computation.11 | async-start | bytes 4194304 | tf_op jit(solution)/shard_map/all_to_all | solution.py:242
  851.1 8.8 collective-permute-start.45
  853.7 36.7 %collective-permute-start.47 = (bf16[8,128,512]{2,1,0:T(8,128)(2,1)S(1)}, bf16[8,128,512]{2,1,0:T(8,128)(2,1)}, u32[]{:S(2)}, u32[]{:S(2)}) collective-permute-start(bf16[8,128,512]{2,1,0:T(8,128)(2,1)S(1)} %add_convert_fusion.3), channel_id=1, source_target_pairs={{0,2},{1,3},{2,0},{3,1},{4,6},{5,7},{6,4},{7,5},{8,10},{9,11},{10,... | collective-permute-start | bytes 3145736 | tf_op jit(solution)/shard_map/ppermute | solution.py:250
  897.4 11.6 %collective-permute-start.48 = (bf16[8,128,512]{2,1,0:T(8,128)(2,1)}, bf16[8,128,512]{2,1,0:T(8,128)(2,1)}, u32[]{:S(2)}, u32[]{:S(2)}) collective-permute-start(bf16[8,128,512]{2,1,0:T(8,128)(2,1)} %get-tuple-element.330), channel_id=1, source_target_pairs={{0,1},{1,0},{2,3},{3,2},{4,5},{5,4},{6,7},{7,6},{8,9},{9,8},{10,11... | collective-permute-start | bytes 3145736 | tf_op jit(solution)/shard_map/ppermute | solution.py:250
  902.1 25.5 %collective-permute-start.50 = (bf16[8,128,512]{2,1,0:T(8,128)(2,1)}, bf16[8,128,512]{2,1,0:T(8,128)(2,1)}, u32[]{:S(2)}, u32[]{:S(2)}) collective-permute-start(bf16[8,128,512]{2,1,0:T(8,128)(2,1)} %add_convert_fusion.1), channel_id=1, source_target_pairs={{0,2},{1,3},{2,0},{3,1},{4,6},{5,7},{6,4},{7,5},{8,10},{9,11},{10,... | collective-permute-start | bytes 3145736 | tf_op jit(solution)/shard_map/ppermute | solution.py:250
  (123 other events, 907.0 us)

commit v4 on v3

--- a/solution.py
+++ b/solution.py
@@ -9,7 +9,7 @@
 BOTH = ("seq", "chan")
 BF = jnp.bfloat16
 F32 = jnp.float32
-VMEM_BYTES = 44 * 1024 * 1024
+VMEM_BYTES = 48 * 1024 * 1024
 
 
 def dot(left, right, left_dim, right_dim):

time: 941 us -> 937 us (level)
  local copies, waits for them, and re-layouts: 116 us -> 87.8 us
  waiting for transfers between devices: 549 us -> 563 us
  Pallas kernels: 126 us -> 138 us
    unnamed x218 -> x136, local copies, waits for them, and re-layouts: 50.6 us -> 17 us
    ppermute x51, waiting for transfers between devices: 496 us -> 510 us  [swap(): lax.ppermute(tensor, 'chan', [(m, m ^ distance) for m in range(chan_count)])]
    pallas_call x17, Pallas kernels: 90 us -> 100 us  [token_call(): pl.pallas_call(body, grid_spec=pltpu.PrefetchScalarGridSpec(num_scalar_pr...]
  transfers between devices with their start and end apart: 63 -> 63, of which waited for: 35 -> 38; matrix products, arithmetic and copies ran while one was open for 11% -> 11% of each run, Pallas kernels for 13% -> 14%
where the time goes in v4:
time: 937 us; the launch traced here: 928 us
  waiting for transfers between devices  563 us (60%)
  Pallas kernels  138 us (15%)
  starting transfers between devices  104 us (11%)
  local copies, waits for them, and re-layouts  87.8 us (9%)
  other arithmetic  33.7 us (4%)
    ppermute x51, waiting for transfers between devices, swap(): lax.ppermute(tensor, 'chan', [(m, m ^ distance) for m in range(chan_count)])  510 us
    pallas_call x17, Pallas kernels, token_call(): pl.pallas_call(body, grid_spec=pltpu.PrefetchScalarGridSpec(num_scalar_pr...  100 us
    all_to_all x12, starting transfers between devices, exchange(): return lax.all_to_all(tensor, BOTH, split_axis=0, concat_axis=0, tiled=True)  63.8 us
    all_to_all x12, waiting for transfers between devices, exchange(): return lax.all_to_all(tensor, BOTH, split_axis=0, concat_axis=0, tiled=True)  53.2 us
    ppermute x51, starting transfers between devices, swap(): lax.ppermute(tensor, 'chan', [(m, m ^ distance) for m in range(chan_count)])  40 us
    pallas_call x2, Pallas kernels, freq_call(): pl.pallas_call(body, grid=(count // step,), in_specs=[spec(x) for x in in...  37.5 us
    reshape x6, local copies, waits for them, and re-layouts, send_out(): shaped = tensor.reshape(rows, chan_count, seq_count, -1, width)  28.1 us
    transpose x6, local copies, waits for them, and re-layouts, receive_in(): jnp.transpose(shaped, (3, 1, 0, 2, 4)).reshape(rows, chan_count, -1, width)  26 us
  transfers between devices with their start and end apart: 63, of which 38 were waited for; matrix products, arithmetic and copies ran while one was open for 11% of the time, Pallas kernels for 14%

profile of v4, /device:TPU:0, one launch (start us, length us, event | category | flops | bytes accessed | tf_op | source)
XLA Modules:
  0.0 927.8 jit_solution(1193134305976676914)
XLA Ops:
  13.2 16.0 %collective-permute-done.refs_1_ = bf16[8,128,512]{2,1,0:T(8,128)(2,1)S(1)} collective-permute-done((bf16[8,128,512]{2,1,0:T(8,128)(2,1)}, bf16[8,128,512]{2,1,0:T(8,128)(2,1)S(1)}, u32[]{:S(2)}, u32[]{:S(2)}) %collective-permute-start) | collective-permute-done | bytes 1048608 | tf_op jit(solution)/shard_map/ppermute | solution.py:250
  33.5 5.5 shard_map.152
  39.0 12.6 %collective-permute-done.3.refs_1_ = bf16[6,128,512]{2,1,0:T(8,128)(2,1)} collective-permute-done((bf16[6,128,512]{2,1,0:T(8,128)(2,1)}, bf16[6,128,512]{2,1,0:T(8,128)(2,1)}, u32[]{:S(2)}, u32[]{:S(2)}) %collective-permute-start.3) | collective-permute-done | bytes 786464 | tf_op jit(solution)/shard_map/ppermute | solution.py:250
  51.6 6.2 all-to-all-start
  61.5 5.4 shard_map.153.refs_6_
  67.0 13.5 %collective-permute-done.6.refs_1_ = bf16[2,128,512]{2,1,0:T(8,128)(2,1)S(1)} collective-permute-done((bf16[2,128,512]{2,1,0:T(8,128)(2,1)S(1)}, bf16[2,128,512]{2,1,0:T(8,128)(2,1)S(1)}, u32[]{:S(2)}, u32[]{:S(2)}) %collective-permute-start.6) | collective-permute-done | bytes 262176 | tf_op jit(solution)/shard_map/ppermute | solution.py:250
  91.4 20.1 %collective-permute-done.9.refs_1_ = bf16[8,128,512]{2,1,0:T(8,128)(2,1)} collective-permute-done((bf16[8,128,512]{2,1,0:T(8,128)(2,1)}, bf16[8,128,512]{2,1,0:T(8,128)(2,1)}, u32[]{:S(2)}, u32[]{:S(2)}) %collective-permute-start.9) | collective-permute-done | bytes 1048608 | tf_op jit(solution)/shard_map/ppermute | solution.py:250
  111.5 8.8 all-to-all-start.1
  127.6 5.3 shard_map.155
  132.9 35.1 %collective-permute-done.12.refs_1_ = bf16[8,128,512]{2,1,0:T(8,128)(2,1)S(1)} collective-permute-done((bf16[8,128,512]{2,1,0:T(8,128)(2,1)S(1)}, bf16[8,128,512]{2,1,0:T(8,128)(2,1)S(1)}, u32[]{:S(2)}, u32[]{:S(2)}) %collective-permute-start.12) | collective-permute-done | bytes 1048608 | tf_op jit(solution)/shard_map/ppermute | solution.py:250
  183.2 5.0 shard_map.156
  188.3 33.4 %collective-permute-done.15.refs_1_ = bf16[8,128,512]{2,1,0:T(8,128)(2,1)} collective-permute-done((bf16[8,128,512]{2,1,0:T(8,128)(2,1)S(1)}, bf16[8,128,512]{2,1,0:T(8,128)(2,1)}, u32[]{:S(2)}, u32[]{:S(2)}) %collective-permute-start.15) | collective-permute-done | bytes 1048608 | tf_op jit(solution)/shard_map/ppermute | solution.py:250
  232.3 5.3 shard_map.157
  237.5 36.6 %collective-permute-done.18.refs_1_ = bf16[8,128,512]{2,1,0:T(8,128)(2,1)} collective-permute-done((bf16[8,128,512]{2,1,0:T(8,128)(2,1)}, bf16[8,128,512]{2,1,0:T(8,128)(2,1)}, u32[]{:S(2)}, u32[]{:S(2)}) %collective-permute-start.18) | collective-permute-done | bytes 1048608 | tf_op jit(solution)/shard_map/ppermute | solution.py:250
  285.2 15.4 %shard_map.158 = (bf16[16,256,1024]{2,1,0:T(8,128)(2,1)}, bf16[16,4,64,256]{3,2,1,0:T(8,128)(2,1)S(1)}, bf16[16,4,192,256]{3,2,1,0:T(8,128)(2,1)}) custom-call(bf16[16,256,256]{2,1,0:T(8,128)(2,1)S(1)} %get-tuple-element.195.refs_0_, bf16[16,256,256]{2,1,0:T(8,128)(2,1)} %get-tuple-element.196.refs_1_, bf16[16,256,1024]{2,1,0:T(8,128)(2,1)} %refs_2_.3, ...), custom_call_target="tpu_custom_call" | custom-call | flops 4294967296 | bytes 37748736 | tf_op jit(solution)/shard_map/pallas_call | solution.py:170
  300.6 11.4 %copy.39 = bf16[16,4,8,24,256]{4,0,3,1,2:T(8,128)(2,1)} copy(bf16[16,4,8,24,256]{4,3,2,1,0:T(8,128)(2,1)} %bitcast.190) | data formatting | bytes 12582912 | tf_op jit(solution)/shard_map/reshape | solution.py:306
  312.0 15.4 %collective-permute-done.19.refs_1_ = bf16[8,128,512]{2,1,0:T(8,128)(2,1)} collective-permute-done((bf16[8,128,512]{2,1,0:T(8,128)(2,1)}, bf16[8,128,512]{2,1,0:T(8,128)(2,1)}, u32[]{:S(2)}, u32[]{:S(2)}) %collective-permute-start.19) | collective-permute-done | bytes 1048608 | tf_op jit(solution)/shard_map/ppermute | solution.py:250
  328.3 4.7 all-to-all-start.5
  336.2 79.1 %collective-permute-done.20.refs_1_ = bf16[8,128,512]{2,1,0:T(8,128)(2,1)S(1)} collective-permute-done((bf16[8,128,512]{2,1,0:T(8,128)(2,1)}, bf16[8,128,512]{2,1,0:T(8,128)(2,1)S(1)}, u32[]{:S(2)}, u32[]{:S(2)}) %collective-permute-start.20) | collective-permute-done | bytes 1048608 | tf_op jit(solution)/shard_map/ppermute | solution.py:250
  415.3 5.1 shard_map.159.refs_6_
  427.3 5.3 shard_map.160.refs_6_
  432.6 4.9 shard_map.161
  438.4 34.6 %all-to-all-done.5 = bf16[32,384,256]{2,1,0:T(8,128)(2,1)} async-done(((bf16[32,384,256]{2,1,0:T(8,128)(2,1)}), bf16[32,384,256]{2,1,0:T(8,128)(2,1)}, u32[]{:S(2)}, u32[]{:S(2)}) %all-to-all-start.5) | async-done | bytes 6291488 | tf_op jit(solution)/shard_map/all_to_all | solution.py:242
  473.1 5.7 all-to-all-start.6
  478.8 6.9 shard_map.162
  488.6 6.9 shard_map.163
  498.5 6.6 shard_map.164
  511.0 50.3 %collective-permute-done.32 = bf16[8,128,512]{2,1,0:T(8,128)(2,1)S(1)} collective-permute-done((bf16[8,128,512]{2,1,0:T(8,128)(2,1)S(1)}, bf16[8,128,512]{2,1,0:T(8,128)(2,1)S(1)}, u32[]{:S(2)}, u32[]{:S(2)}) %collective-permute-start.32) | collective-permute-done | bytes 1048608 | tf_op jit(solution)/shard_map/ppermute | solution.py:250
  561.3 23.5 %collective-permute-done.33 = bf16[8,128,512]{2,1,0:T(8,128)(2,1)S(1)} collective-permute-done((bf16[8,128,512]{2,1,0:T(8,128)(2,1)S(1)}, bf16[8,128,512]{2,1,0:T(8,128)(2,1)S(1)}, u32[]{:S(2)}, u32[]{:S(2)}) %collective-permute-start.33) | collective-permute-done | bytes 1048608 | tf_op jit(solution)/shard_map/ppermute | solution.py:250
  585.8 30.7 %collective-permute-done.35 = bf16[8,128,512]{2,1,0:T(8,128)(2,1)} collective-permute-done((bf16[8,128,512]{2,1,0:T(8,128)(2,1)S(1)}, bf16[8,128,512]{2,1,0:T(8,128)(2,1)}, u32[]{:S(2)}, u32[]{:S(2)}) %collective-permute-start.35) | collective-permute-done | bytes 1048608 | tf_op jit(solution)/shard_map/ppermute | solution.py:250
  618.9 5.8 all-to-all-start.7
  624.7 7.7 copy.42
  632.5 22.1 %shard_map.165 = (bf16[16,256,1024]{2,1,0:T(8,128)(2,1)}, bf16[16,256,256]{2,1,0:T(8,128)(2,1)S(1)}, bf16[16,256,256]{2,1,0:T(8,128)(2,1)S(1)}, bf16[16,4,64,256...) custom-call(bf16[16,256,256]{2,1,0:T(8,128)(2,1)} %copy-done, ...), custom_call_target="tpu_custom_call" | custom-call | flops 10737418240 | bytes 58720256 | tf_op jit(solution)/shard_map/pallas_call | solution.py:170
  657.2 4.6 copy.43
  661.8 11.7 %all-to-all-done.7 = bf16[32,128,256]{2,1,0:T(8,128)(2,1)} async-done(((bf16[32,128,256]{2,1,0:T(8,128)(2,1)}), bf16[32,128,256]{2,1,0:T(8,128)(2,1)}, u32[]{:S(2)}, u32[]{:S(2)}) %all-to-all-start.7) | async-done | bytes 2097184 | tf_op jit(solution)/shard_map/all_to_all | solution.py:242
  677.8 6.9 shard_map.166
  707.6 18.7 %collective-permute-done.38 = bf16[8,128,512]{2,1,0:T(8,128)(2,1)} collective-permute-done((bf16[8,128,512]{2,1,0:T(8,128)(2,1)S(1)}, bf16[8,128,512]{2,1,0:T(8,128)(2,1)}, u32[]{:S(2)}, u32[]{:S(2)}) %collective-permute-start.38) | collective-permute-done | bytes 1048608 | tf_op jit(solution)/shard_map/ppermute | solution.py:250
  726.5 5.1 all-to-all-start.9
  731.6 7.0 shard_map.167
  748.8 31.4 %collective-permute-done.41 = bf16[8,128,512]{2,1,0:T(8,128)(2,1)} collective-permute-done((bf16[8,128,512]{2,1,0:T(8,128)(2,1)S(1)}, bf16[8,128,512]{2,1,0:T(8,128)(2,1)}, u32[]{:S(2)}, u32[]{:S(2)}) %collective-permute-start.41) | collective-permute-done | bytes 1048608 | tf_op jit(solution)/shard_map/ppermute | solution.py:250
  780.4 5.1 all-to-all-start.10
  785.5 7.0 shard_map.168
  805.1 28.9 %collective-permute-done.44 = bf16[8,128,512]{2,1,0:T(8,128)(2,1)} collective-permute-done((bf16[8,128,512]{2,1,0:T(8,128)(2,1)S(1)}, bf16[8,128,512]{2,1,0:T(8,128)(2,1)}, u32[]{:S(2)}, u32[]{:S(2)}) %collective-permute-start.44) | collective-permute-done | bytes 1048608 | tf_op jit(solution)/shard_map/ppermute | solution.py:250
  834.2 5.1 all-to-all-start.11
  839.3 7.2 shard_map.169
  856.7 31.1 %collective-permute-done.47 = bf16[8,128,512]{2,1,0:T(8,128)(2,1)} collective-permute-done((bf16[8,128,512]{2,1,0:T(8,128)(2,1)S(1)}, bf16[8,128,512]{2,1,0:T(8,128)(2,1)}, u32[]{:S(2)}, u32[]{:S(2)}) %collective-permute-start.47) | collective-permute-done | bytes 1048608 | tf_op jit(solution)/shard_map/ppermute | solution.py:250
  888.1 7.2 shard_map.170
  907.4 17.0 %collective-permute-done.50 = bf16[8,128,512]{2,1,0:T(8,128)(2,1)} collective-permute-done((bf16[8,128,512]{2,1,0:T(8,128)(2,1)S(1)}, bf16[8,128,512]{2,1,0:T(8,128)(2,1)}, u32[]{:S(2)}, u32[]{:S(2)}) %collective-permute-start.50) | collective-permute-done | bytes 1048608 | tf_op jit(solution)/shard_map/ppermute | solution.py:250
  (284 shorter events, 181.4 us)
Async XLA Ops:
  2.9 26.3 %collective-permute-start = (bf16[8,128,512]{2,1,0:T(8,128)(2,1)}, bf16[8,128,512]{2,1,0:T(8,128)(2,1)S(1)}, u32[]{:S(2)}, u32[]{:S(2)}) collective-permute-start(bf16[8,128,512]{2,1,0:T(8,128)(2,1)} %slice.63), channel_id=1, source_target_pairs={{0,2},{1,3},{2,0},{3,1},{4,6},{5,7},{6,4},{7,5},{8,10},{9,11},{10,... | collective-permute-start | bytes 3145736 | tf_op jit(solution)/shard_map/ppermute | solution.py:250
  5.9 27.7 %collective-permute-start.1 = (bf16[8,128,512]{2,1,0:T(8,128)(2,1)}, bf16[8,128,512]{2,1,0:T(8,128)(2,1)}, u32[]{:S(2)}, u32[]{:S(2)}) collective-permute-start(bf16[8,128,512]{2,1,0:T(8,128)(2,1)} %slice.63), channel_id=1, source_target_pairs={{0,1},{1,0},{2,3},{3,2},{4,5},{5,4},{6,7},{7,6},{8,9},{9,8},{10,11... | collective-permute-start | bytes 3145736 | tf_op jit(solution)/shard_map/ppermute | solution.py:250
  31.7 19.9 %collective-permute-start.3 = (bf16[6,128,512]{2,1,0:T(8,128)(2,1)}, bf16[6,128,512]{2,1,0:T(8,128)(2,1)}, u32[]{:S(2)}, u32[]{:S(2)}) collective-permute-start(bf16[6,128,512]{2,1,0:T(8,128)(2,1)} %slice.70), channel_id=1, source_target_pairs={{0,2},{1,3},{2,0},{3,1},{4,6},{5,7},{6,4},{7,5},{8,10},{9,11},{10,... | collective-permute-start | bytes 2359304 | tf_op jit(solution)/shard_map/ppermute | solution.py:250
  51.6 59.9 %all-to-all-start = ((bf16[32,128,256]{2,1,0:T(8,128)(2,1)}), bf16[32,128,256]{2,1,0:T(8,128)(2,1)}, u32[]{:S(2)}, u32[]{:S(2)}) async-start(bf16[32,128,256]{2,1,0:T(8,128)(2,1)} %bitcast.17), calls=%async_computation | async-start | bytes 4194304 | tf_op jit(solution)/shard_map/all_to_all | solution.py:242
  59.4 21.1 %collective-permute-start.6 = (bf16[2,128,512]{2,1,0:T(8,128)(2,1)S(1)}, bf16[2,128,512]{2,1,0:T(8,128)(2,1)S(1)}, u32[]{:S(2)}, u32[]{:S(2)}) collective-permute-start(bf16[2,128,512]{2,1,0:T(8,128)(2,1)S(1)} %slice.71), channel_id=1, source_target_pairs={{0,2},{1,3},{2,0},{3,1},{4,6},{5,7},{6,4},{7,5},{8,10},{9,11},{10,... | collective-permute-start | bytes 786440 | tf_op jit(solution)/shard_map/ppermute | solution.py:250
  82.7 28.8 %collective-permute-start.9 = (bf16[8,128,512]{2,1,0:T(8,128)(2,1)}, bf16[8,128,512]{2,1,0:T(8,128)(2,1)}, u32[]{:S(2)}, u32[]{:S(2)}) collective-permute-start(bf16[8,128,512]{2,1,0:T(8,128)(2,1)} %slice.72), channel_id=1, source_target_pairs={{0,2},{1,3},{2,0},{3,1},{4,6},{5,7},{6,4},{7,5},{8,10},{9,11},{10,... | collective-permute-start | bytes 3145736 | tf_op jit(solution)/shard_map/ppermute | solution.py:250
  111.5 57.6 %all-to-all-start.1 = ((bf16[32,128,256]{2,1,0:T(8,128)(2,1)}), bf16[32,128,256]{2,1,0:T(8,128)(2,1)}, u32[]{:S(2)}, u32[]{:S(2)}) async-start(bf16[32,128,256]{2,1,0:T(8,128)(2,1)} %bitcast.20), calls=%async_computation.1 | async-start | bytes 4194304 | tf_op jit(solution)/shard_map/all_to_all | solution.py:242
  120.3 7.3 collective-permute-start.10
  120.6 7.0 collective-permute-start.11
  122.2 45.8 %collective-permute-start.12 = (bf16[8,128,512]{2,1,0:T(8,128)(2,1)S(1)}, bf16[8,128,512]{2,1,0:T(8,128)(2,1)S(1)}, u32[]{:S(2)}, u32[]{:S(2)}) collective-permute-start(bf16[8,128,512]{2,1,0:T(8,128)(2,1)S(1)} %slice.73), channel_id=1, source_target_pairs={{0,2},{1,3},{2,0},{3,1},{4,6},{5,7},{6,4},{7,5},{8,10},{9,11},{10,... | collective-permute-start | bytes 3145736 | tf_op jit(solution)/shard_map/ppermute | solution.py:250
  169.1 53.0 %all-to-all-start.2 = ((bf16[32,128,256]{2,1,0:T(8,128)(2,1)}), bf16[32,128,256]{2,1,0:T(8,128)(2,1)}, u32[]{:S(2)}, u32[]{:S(2)}) async-start(bf16[32,128,256]{2,1,0:T(8,128)(2,1)} %bitcast.26), calls=%async_computation.2 | async-start | bytes 4194304 | tf_op jit(solution)/shard_map/all_to_all | solution.py:242
  177.4 5.8 collective-permute-start.13
  177.6 5.7 collective-permute-start.14
  177.9 43.8 %collective-permute-start.15 = (bf16[8,128,512]{2,1,0:T(8,128)(2,1)S(1)}, bf16[8,128,512]{2,1,0:T(8,128)(2,1)}, u32[]{:S(2)}, u32[]{:S(2)}) collective-permute-start(bf16[8,128,512]{2,1,0:T(8,128)(2,1)S(1)} %get-tuple-element.347), channel_id=1, source_target_pairs={{0,2},{1,3},{2,0},{3,1},{4,6},{5,7},{6,4},{7,5},{8,10},{9,11},{10,... | collective-permute-start | bytes 3145736 | tf_op jit(solution)/shard_map/ppermute | solution.py:250
  222.1 53.0 %all-to-all-start.3 = ((bf16[32,128,256]{2,1,0:T(8,128)(2,1)}), bf16[32,128,256]{2,1,0:T(8,128)(2,1)}, u32[]{:S(2)}, u32[]{:S(2)}) async-start(bf16[32,128,256]{2,1,0:T(8,128)(2,1)} %bitcast.32), calls=%async_computation.3 | async-start | bytes 4194304 | tf_op jit(solution)/shard_map/all_to_all | solution.py:242
  226.4 5.9 collective-permute-start.16
  226.6 5.7 collective-permute-start.17
  226.9 47.2 %collective-permute-start.18 = (bf16[8,128,512]{2,1,0:T(8,128)(2,1)}, bf16[8,128,512]{2,1,0:T(8,128)(2,1)}, u32[]{:S(2)}, u32[]{:S(2)}) collective-permute-start(bf16[8,128,512]{2,1,0:T(8,128)(2,1)} %get-tuple-element.346), channel_id=1, source_target_pairs={{0,2},{1,3},{2,0},{3,1},{4,6},{5,7},{6,4},{7,5},{8,10},{9,11},{10,... | collective-permute-start | bytes 3145736 | tf_op jit(solution)/shard_map/ppermute | solution.py:250
  275.1 53.2 %all-to-all-start.4 = ((bf16[32,128,256]{2,1,0:T(8,128)(2,1)}), bf16[32,128,256]{2,1,0:T(8,128)(2,1)}, u32[]{:S(2)}, u32[]{:S(2)}) async-start(bf16[32,128,256]{2,1,0:T(8,128)(2,1)} %bitcast.40), calls=%async_computation.4 | async-start | bytes 4194304 | tf_op jit(solution)/shard_map/all_to_all | solution.py:242
  279.6 47.8 %collective-permute-start.19 = (bf16[8,128,512]{2,1,0:T(8,128)(2,1)}, bf16[8,128,512]{2,1,0:T(8,128)(2,1)}, u32[]{:S(2)}, u32[]{:S(2)}) collective-permute-start(bf16[8,128,512]{2,1,0:T(8,128)(2,1)} %get-tuple-element.345), channel_id=1, source_target_pairs={{0,2},{1,3},{2,0},{3,1},{4,6},{5,7},{6,4},{7,5},{8,10},{9,11},{10,... | collective-permute-start | bytes 3145736 | tf_op jit(solution)/shard_map/ppermute | solution.py:250
  328.3 144.7 %all-to-all-start.5 = ((bf16[32,384,256]{2,1,0:T(8,128)(2,1)}), bf16[32,384,256]{2,1,0:T(8,128)(2,1)}, u32[]{:S(2)}, u32[]{:S(2)}) async-start(bf16[32,384,256]{2,1,0:T(8,128)(2,1)} %bitcast.174), calls=%async_computation.5 | async-start | bytes 12582912 | tf_op jit(solution)/shard_map/all_to_all | solution.py:242
  333.5 81.8 %collective-permute-start.20 = (bf16[8,128,512]{2,1,0:T(8,128)(2,1)}, bf16[8,128,512]{2,1,0:T(8,128)(2,1)S(1)}, u32[]{:S(2)}, u32[]{:S(2)}) collective-permute-start(bf16[8,128,512]{2,1,0:T(8,128)(2,1)} %get-tuple-element.344), channel_id=1, source_target_pairs={{0,2},{1,3},{2,0},{3,1},{4,6},{5,7},{6,4},{7,5},{8,10},{9,11},{10,... | collective-permute-start | bytes 3145736 | tf_op jit(solution)/shard_map/ppermute | solution.py:250
  335.2 80.1 %collective-permute-start.26 = (bf16[8,128,512]{2,1,0:T(8,128)(2,1)}, bf16[8,128,512]{2,1,0:T(8,128)(2,1)S(1)}, u32[]{:S(2)}, u32[]{:S(2)}) collective-permute-start(bf16[8,128,512]{2,1,0:T(8,128)(2,1)} %collective-permute-done.18.refs_1_), channel_id=1, source_target_pairs={{0,1},{1,0},{2,3},{3,2},{4,5},{5,4},{6,7},{7,6},{8,9},{9,8},{10,11... | collective-permute-start | bytes 3145736 | tf_op jit(solution)/shard_map/ppermute | solution.py:250
  335.3 92.0 %collective-permute-start.23 = (bf16[8,128,512]{2,1,0:T(8,128)(2,1)}, bf16[8,128,512]{2,1,0:T(8,128)(2,1)S(1)}, u32[]{:S(2)}, u32[]{:S(2)}) collective-permute-start(bf16[8,128,512]{2,1,0:T(8,128)(2,1)} %get-tuple-element.345), channel_id=1, source_target_pairs={{0,1},{1,0},{2,3},{3,2},{4,5},{5,4},{6,7},{7,6},{8,9},{9,8},{10,11... | collective-permute-start | bytes 3145736 | tf_op jit(solution)/shard_map/ppermute | solution.py:250
  335.7 91.5 %collective-permute-start.24 = (bf16[8,128,512]{2,1,0:T(8,128)(2,1)}, bf16[8,128,512]{2,1,0:T(8,128)(2,1)S(1)}, u32[]{:S(2)}, u32[]{:S(2)}) collective-permute-start(bf16[8,128,512]{2,1,0:T(8,128)(2,1)} %collective-permute-done.19.refs_1_), channel_id=1, source_target_pairs={{0,1},{1,0},{2,3},{3,2},{4,5},{5,4},{6,7},{7,6},{8,9},{9,8},{10,11... | collective-permute-start | bytes 3145736 | tf_op jit(solution)/shard_map/ppermute | solution.py:250
  335.8 96.7 %collective-permute-start.21 = (bf16[8,128,512]{2,1,0:T(8,128)(2,1)}, bf16[8,128,512]{2,1,0:T(8,128)(2,1)S(1)}, u32[]{:S(2)}, u32[]{:S(2)}) collective-permute-start(bf16[8,128,512]{2,1,0:T(8,128)(2,1)} %get-tuple-element.344), channel_id=1, source_target_pairs={{0,1},{1,0},{2,3},{3,2},{4,5},{5,4},{6,7},{7,6},{8,9},{9,8},{10,11... | collective-permute-start | bytes 3145736 | tf_op jit(solution)/shard_map/ppermute | solution.py:250
  415.3 17.3 %collective-permute-start.22 = (bf16[8,128,512]{2,1,0:T(8,128)(2,1)S(1)}, bf16[8,128,512]{2,1,0:T(8,128)(2,1)S(1)}, u32[]{:S(2)}, u32[]{:S(2)}) collective-permute-start(bf16[8,128,512]{2,1,0:T(8,128)(2,1)S(1)} %collective-permute-done.20.refs_1_), channel_id=1, source_target_pairs={{0,1},{1,0},{2,3},{3,2},{4,5},{5,4},{6,7},{7,6},{8,9},{9,8},{10,11... | collective-permute-start | bytes 3145736 | tf_op jit(solution)/shard_map/ppermute | solution.py:250
  473.1 145.9 %all-to-all-start.6 = ((bf16[32,384,256]{2,1,0:T(8,128)(2,1)}), bf16[32,384,256]{2,1,0:T(8,128)(2,1)}, u32[]{:S(2)}, u32[]{:S(2)}) async-start(bf16[32,384,256]{2,1,0:T(8,128)(2,1)} %bitcast.170), calls=%async_computation.6 | async-start | bytes 12582912 | tf_op jit(solution)/shard_map/all_to_all | solution.py:242
  505.6 5.4 collective-permute-start.30
  505.8 55.5 %collective-permute-start.32 = (bf16[8,128,512]{2,1,0:T(8,128)(2,1)S(1)}, bf16[8,128,512]{2,1,0:T(8,128)(2,1)S(1)}, u32[]{:S(2)}, u32[]{:S(2)}) collective-permute-start(bf16[8,128,512]{2,1,0:T(8,128)(2,1)S(1)} %add_convert_fusion.15), channel_id=1, source_target_pairs={{0,2},{1,3},{2,0},{3,1},{4,6},{5,7},{6,4},{7,5},{8,10},{9,11},{10,... | collective-permute-start | bytes 3145736 | tf_op jit(solution)/shard_map/ppermute | solution.py:250
  507.5 53.8 %collective-permute-start.31 = (bf16[8,128,512]{2,1,0:T(8,128)(2,1)S(1)}, bf16[8,128,512]{2,1,0:T(8,128)(2,1)S(1)}, u32[]{:S(2)}, u32[]{:S(2)}) collective-permute-start(bf16[8,128,512]{2,1,0:T(8,128)(2,1)S(1)} %get-tuple-element.226), channel_id=1, source_target_pairs={{0,1},{1,0},{2,3},{3,2},{4,5},{5,4},{6,7},{7,6},{8,9},{9,8},{10,11... | collective-permute-start | bytes 3145736 | tf_op jit(solution)/shard_map/ppermute | solution.py:250
  507.8 77.0 %collective-permute-start.33 = (bf16[8,128,512]{2,1,0:T(8,128)(2,1)S(1)}, bf16[8,128,512]{2,1,0:T(8,128)(2,1)S(1)}, u32[]{:S(2)}, u32[]{:S(2)}) collective-permute-start(bf16[8,128,512]{2,1,0:T(8,128)(2,1)S(1)} %add_convert_fusion.14), channel_id=1, source_target_pairs={{0,2},{1,3},{2,0},{3,1},{4,6},{5,7},{6,4},{7,5},{8,10},{9,11},{10,... | collective-permute-start | bytes 3145736 | tf_op jit(solution)/shard_map/ppermute | solution.py:250
  509.8 106.6 %collective-permute-start.35 = (bf16[8,128,512]{2,1,0:T(8,128)(2,1)S(1)}, bf16[8,128,512]{2,1,0:T(8,128)(2,1)}, u32[]{:S(2)}, u32[]{:S(2)}) collective-permute-start(bf16[8,128,512]{2,1,0:T(8,128)(2,1)S(1)} %add_convert_fusion.13), channel_id=1, source_target_pairs={{0,2},{1,3},{2,0},{3,1},{4,6},{5,7},{6,4},{7,5},{8,10},{9,11},{10,... | collective-permute-start | bytes 3145736 | tf_op jit(solution)/shard_map/ppermute | solution.py:250
  618.9 54.5 %all-to-all-start.7 = ((bf16[32,128,256]{2,1,0:T(8,128)(2,1)}), bf16[32,128,256]{2,1,0:T(8,128)(2,1)}, u32[]{:S(2)}, u32[]{:S(2)}) async-start(bf16[32,128,256]{2,1,0:T(8,128)(2,1)} %bitcast.185), calls=%async_computation.7 | async-start | bytes 4194304 | tf_op jit(solution)/shard_map/all_to_all | solution.py:242
  673.5 53.0 %all-to-all-start.8 = ((bf16[32,128,256]{2,1,0:T(8,128)(2,1)}), bf16[32,128,256]{2,1,0:T(8,128)(2,1)}, u32[]{:S(2)}, u32[]{:S(2)}) async-start(bf16[32,128,256]{2,1,0:T(8,128)(2,1)} %bitcast.68), calls=%async_computation.8 | async-start | bytes 4194304 | tf_op jit(solution)/shard_map/all_to_all | solution.py:242
  687.2 19.4 %collective-permute-start.36 = (bf16[8,128,512]{2,1,0:T(8,128)(2,1)S(1)}, bf16[8,128,512]{2,1,0:T(8,128)(2,1)S(1)}, u32[]{:S(2)}, u32[]{:S(2)}) collective-permute-start(bf16[8,128,512]{2,1,0:T(8,128)(2,1)S(1)} %get-tuple-element.258), channel_id=1, source_target_pairs={{0,1},{1,0},{2,3},{3,2},{4,5},{5,4},{6,7},{7,6},{8,9},{9,8},{10,11... | collective-permute-start | bytes 3145736 | tf_op jit(solution)/shard_map/ppermute | solution.py:250
  687.9 38.4 %collective-permute-start.38 = (bf16[8,128,512]{2,1,0:T(8,128)(2,1)S(1)}, bf16[8,128,512]{2,1,0:T(8,128)(2,1)}, u32[]{:S(2)}, u32[]{:S(2)}) collective-permute-start(bf16[8,128,512]{2,1,0:T(8,128)(2,1)S(1)} %add_convert_fusion.12), channel_id=1, source_target_pairs={{0,2},{1,3},{2,0},{3,1},{4,6},{5,7},{6,4},{7,5},{8,10},{9,11},{10,... | collective-permute-start | bytes 3145736 | tf_op jit(solution)/shard_map/ppermute | solution.py:250
  726.5 53.9 %all-to-all-start.9 = ((bf16[32,128,256]{2,1,0:T(8,128)(2,1)}), bf16[32,128,256]{2,1,0:T(8,128)(2,1)}, u32[]{:S(2)}, u32[]{:S(2)}) async-start(bf16[32,128,256]{2,1,0:T(8,128)(2,1)} %bitcast.187), calls=%async_computation.9 | async-start | bytes 4194304 | tf_op jit(solution)/shard_map/all_to_all | solution.py:242
  738.8 9.0 collective-permute-start.39
  741.6 38.5 %collective-permute-start.41 = (bf16[8,128,512]{2,1,0:T(8,128)(2,1)S(1)}, bf16[8,128,512]{2,1,0:T(8,128)(2,1)}, u32[]{:S(2)}, u32[]{:S(2)}) collective-permute-start(bf16[8,128,512]{2,1,0:T(8,128)(2,1)S(1)} %add_convert_fusion.8), channel_id=1, source_target_pairs={{0,2},{1,3},{2,0},{3,1},{4,6},{5,7},{6,4},{7,5},{8,10},{9,11},{10,... | collective-permute-start | bytes 3145736 | tf_op jit(solution)/shard_map/ppermute | solution.py:250
  780.4 53.9 %all-to-all-start.10 = ((bf16[32,128,256]{2,1,0:T(8,128)(2,1)}), bf16[32,128,256]{2,1,0:T(8,128)(2,1)}, u32[]{:S(2)}, u32[]{:S(2)}) async-start(bf16[32,128,256]{2,1,0:T(8,128)(2,1)} %bitcast.186), calls=%async_computation.10 | async-start | bytes 4194304 | tf_op jit(solution)/shard_map/all_to_all | solution.py:242
  792.7 11.4 %collective-permute-start.42 = (bf16[8,128,512]{2,1,0:T(8,128)(2,1)S(1)}, bf16[8,128,512]{2,1,0:T(8,128)(2,1)S(1)}, u32[]{:S(2)}, u32[]{:S(2)}) collective-permute-start(bf16[8,128,512]{2,1,0:T(8,128)(2,1)S(1)} %get-tuple-element.299), channel_id=1, source_target_pairs={{0,1},{1,0},{2,3},{3,2},{4,5},{5,4},{6,7},{7,6},{8,9},{9,8},{10,11... | collective-permute-start | bytes 3145736 | tf_op jit(solution)/shard_map/ppermute | solution.py:250
  795.5 38.4 %collective-permute-start.44 = (bf16[8,128,512]{2,1,0:T(8,128)(2,1)S(1)}, bf16[8,128,512]{2,1,0:T(8,128)(2,1)}, u32[]{:S(2)}, u32[]{:S(2)}) collective-permute-start(bf16[8,128,512]{2,1,0:T(8,128)(2,1)S(1)} %add_convert_fusion.6), channel_id=1, source_target_pairs={{0,2},{1,3},{2,0},{3,1},{4,6},{5,7},{6,4},{7,5},{8,10},{9,11},{10,... | collective-permute-start | bytes 3145736 | tf_op jit(solution)/shard_map/ppermute | solution.py:250
  834.2 53.9 %all-to-all-start.11 = ((bf16[32,128,256]{2,1,0:T(8,128)(2,1)}), bf16[32,128,256]{2,1,0:T(8,128)(2,1)}, u32[]{:S(2)}, u32[]{:S(2)}) async-start(bf16[32,128,256]{2,1,0:T(8,128)(2,1)} %bitcast.183), calls=%async_computation.11 | async-start | bytes 4194304 | tf_op jit(solution)/shard_map/all_to_all | solution.py:242
  846.8 8.9 collective-permute-start.45
  849.6 38.2 %collective-permute-start.47 = (bf16[8,128,512]{2,1,0:T(8,128)(2,1)S(1)}, bf16[8,128,512]{2,1,0:T(8,128)(2,1)}, u32[]{:S(2)}, u32[]{:S(2)}) collective-permute-start(bf16[8,128,512]{2,1,0:T(8,128)(2,1)S(1)} %add_convert_fusion.3), channel_id=1, source_target_pairs={{0,2},{1,3},{2,0},{3,1},{4,6},{5,7},{6,4},{7,5},{8,10},{9,11},{10,... | collective-permute-start | bytes 3145736 | tf_op jit(solution)/shard_map/ppermute | solution.py:250
  895.2 12.2 %collective-permute-start.48 = (bf16[8,128,512]{2,1,0:T(8,128)(2,1)}, bf16[8,128,512]{2,1,0:T(8,128)(2,1)}, u32[]{:S(2)}, u32[]{:S(2)}) collective-permute-start(bf16[8,128,512]{2,1,0:T(8,128)(2,1)} %get-tuple-element.330), channel_id=1, source_target_pairs={{0,1},{1,0},{2,3},{3,2},{4,5},{5,4},{6,7},{7,6},{8,9},{9,8},{10,11... | collective-permute-start | bytes 3145736 | tf_op jit(solution)/shard_map/ppermute | solution.py:250
  899.0 25.4 %collective-permute-start.50 = (bf16[8,128,512]{2,1,0:T(8,128)(2,1)S(1)}, bf16[8,128,512]{2,1,0:T(8,128)(2,1)}, u32[]{:S(2)}, u32[]{:S(2)}) collective-permute-start(bf16[8,128,512]{2,1,0:T(8,128)(2,1)S(1)} %add_convert_fusion.1), channel_id=1, source_target_pairs={{0,2},{1,3},{2,0},{3,1},{4,6},{5,7},{6,4},{7,5},{8,10},{9,11},{10,... | collective-permute-start | bytes 3145736 | tf_op jit(solution)/shard_map/ppermute | solution.py:250
  (82 other events, 940.1 us)
